TPU v7x, 32 devices: a whole 2x2x4 slice. The times are simulated.
32 devices in a mesh: dp: 16 (over z, x, core), seq: 2 (over y).
Axes of the slice: x: 2, y: 2, z: 4, core: 2. Of those that a mesh axis runs over, the one named last changes fastest.
Arguments:
- inputs: bfloat16 [1024, 16, 768], P('seq', 'dp'), may hold values from -6 to 6
- cotangent: bfloat16 [1024, 16, 768], P('seq', 'dp'), may hold values from -6 to 6
- tie_slots: int32 [12], replicated, may hold values from 0 to 1
- gain_first: float32 [2, 768], P(None, 'dp'), may hold values from 0.1 to 1.9
- shift_first: float32 [2, 768], P(None, 'dp'), may hold values from -3 to 3
- weight_triple: float32 [2, 768, 2304], P(None, 'dp'), may hold values from -0.3125 to 0.3125
- bias_pair: float32 [2, 1536], P(None, 'dp'), may hold values from -3 to 3
- weight_merge: float32 [2, 768, 768], P(None, 'dp'), may hold values from -1.25 to 1.25
- bias_merge: float32 [2, 768], P(None, 'dp'), may hold values from -4 to 4
- gain_second: float32 [2, 768], P(None, 'dp'), may hold values from 0.1 to 1.9
- shift_second: float32 [2, 768], P(None, 'dp'), may hold values from -3 to 3
- weight_expand: float32 [2, 768, 3072], P(None, 'dp'), may hold values from -0.21875 to 0.21875
- bias_expand: float32 [2, 3072], P(None, 'dp'), may hold values from -3 to 3
- weight_shrink: float32 [2, 3072, 768], P(None, 'dp'), may hold values from -0.109375 to 0.109375
- bias_shrink: float32 [2, 768], P(None, 'dp'), may hold values from -4 to 4
Outputs:
- layer_output: bfloat16 [1024, 16, 768], P('seq', 'dp')
- input_grad: float32 [1024, 16, 768], P('seq', 'dp')
- grad_gain_first: float32 [2, 768], P(None, 'dp')
- grad_shift_first: float32 [2, 768], P(None, 'dp')
- grad_weight_triple: float32 [2, 768, 2304], P(None, 'dp')
- grad_bias_pair: float32 [2, 1536], P(None, 'dp')
- grad_weight_merge: float32 [2, 768, 768], P(None, 'dp')
- grad_bias_merge: float32 [2, 768], P(None, 'dp')
- grad_gain_second: float32 [2, 768], P(None, 'dp')
- grad_shift_second: float32 [2, 768], P(None, 'dp')
- grad_weight_expand: float32 [2, 768, 3072], P(None, 'dp')
- grad_bias_expand: float32 [2, 3072], P(None, 'dp')
- grad_weight_shrink: float32 [2, 3072, 768], P(None, 'dp')
- grad_bias_shrink: float32 [2, 768], P(None, 'dp')
Inputs may be any that keep to these rules, and one draw needn't show every extreme that they name: `tie_slots`: entry i picks the slot of parameter tensor i, in the order of the masters among the arguments.
All inputs are finite; a program needn't handle non-finite values.
Results may differ from a plain program's by a relative error of at most 0.034.
Values may be sent and summed in bfloat16 or wider, within the bound.
No kernel may reach another device: no remote copies, remote signals or barrier semaphores. Data moves between devices by JAX's collectives and lax.ppermute only.
A program may use at most 128 MiB of HBM per device.

v0:
```python
import math

import jax
import jax.numpy as jnp
from jax import lax
from jax.sharding import PartitionSpec as P

H = 12


EPSILON = 1e-05
NEGATIVE = -1e30


def layer_norm(values, gain, shift):
    average = jnp.mean(values, axis=-1, keepdims=True)
    centered = values - average
    variance = jnp.mean(centered * centered, axis=-1, keepdims=True)
    return centered * lax.rsqrt(variance + EPSILON) * gain + shift


def collect(masters, slots):
    chosen = [
        lax.dynamic_index_in_dim(masters[number], slots[number], 0, keepdims=False).astype(
            jnp.bfloat16
        )
        for number in range(6)
    ]
    return (
        lax.all_gather(chosen[0], "dp", axis=0, tiled=True),
        lax.all_gather(chosen[1], "dp", axis=0, tiled=True),
        lax.all_gather(chosen[2], "dp", axis=0, tiled=True),
        lax.all_gather(chosen[3], "dp", axis=0, tiled=True),
        lax.all_gather(chosen[4], "dp", axis=0, tiled=True),
        lax.all_gather(chosen[5], "dp", axis=0, tiled=True),
    )


def reduce_grads(grads):
    parts = (
        lax.psum_scatter(
            grads[0].astype(jnp.bfloat16), "dp", scatter_dimension=0, tiled=True
        ).astype(jnp.float32),
        lax.psum_scatter(
            grads[1].astype(jnp.bfloat16), "dp", scatter_dimension=0, tiled=True
        ).astype(jnp.float32),
        lax.psum_scatter(
            grads[2].astype(jnp.bfloat16), "dp", scatter_dimension=0, tiled=True
        ).astype(jnp.float32),
        lax.psum_scatter(
            grads[3].astype(jnp.bfloat16), "dp", scatter_dimension=0, tiled=True
        ).astype(jnp.float32),
        lax.psum_scatter(
            grads[4].astype(jnp.bfloat16), "dp", scatter_dimension=0, tiled=True
        ).astype(jnp.float32),
        lax.psum_scatter(
            grads[5].astype(jnp.bfloat16), "dp", scatter_dimension=0, tiled=True
        ).astype(jnp.float32),
    )
    return (
        lax.psum(parts[0].astype(jnp.bfloat16), "seq").astype(jnp.float32),
        lax.psum(parts[1].astype(jnp.bfloat16), "seq").astype(jnp.float32),
        lax.psum(parts[2].astype(jnp.bfloat16), "seq").astype(jnp.float32),
        lax.psum(parts[3].astype(jnp.bfloat16), "seq").astype(jnp.float32),
        lax.psum(parts[4].astype(jnp.bfloat16), "seq").astype(jnp.float32),
        lax.psum(parts[5].astype(jnp.bfloat16), "seq").astype(jnp.float32),
    )


def into_slots(grads, masters, slots):
    placed = []
    for number in range(6):
        slot_count = masters[number].shape[0]
        marker = (jnp.arange(slot_count) == slots[number]).astype(jnp.float32)
        shaped = marker.reshape((slot_count,) + (1,) * grads[number].ndim)
        placed.append(shaped * grads[number][None])
    return placed


def per_device(
    inputs,
    cotangent,
    tie_slots,
    gain_first,
    shift_first,
    weight_triple,
    bias_pair,
    weight_merge,
    bias_merge,
    gain_second,
    shift_second,
    weight_expand,
    bias_expand,
    weight_shrink,
    bias_shrink,
):
    local_len, seq_count, width = inputs.shape
    row_count = local_len * seq_count
    head_count = H
    head_size = width // head_count
    scaling = 1.0 / math.sqrt(head_size)
    first_masters = (gain_first, shift_first, weight_triple, bias_pair, weight_merge, bias_merge)
    second_masters = (
        gain_second,
        shift_second,
        weight_expand,
        bias_expand,
        weight_shrink,
        bias_shrink,
    )
    first_set = collect(first_masters, tie_slots[0:6])
    gain_one = first_set[0].astype(jnp.float32)
    shift_one = first_set[1].astype(jnp.float32)
    triple_weight = first_set[2]
    pair_bias = first_set[3]
    merge_weight = first_set[4]
    merge_bias = first_set[5].astype(jnp.float32)
    flat_in = inputs.reshape(row_count, width).astype(jnp.float32)
    normed, norm_one_pull = jax.vjp(layer_norm, flat_in, gain_one, shift_one)
    normed_low = normed.astype(jnp.bfloat16)
    bias_full = jnp.concatenate(
        [pair_bias[:width], jnp.zeros((width,), jnp.bfloat16), pair_bias[width:]]
    ).astype(jnp.float32)
    triple = jnp.dot(normed_low, triple_weight, preferred_element_type=jnp.float32) + bias_full
    triple = triple.astype(jnp.bfloat16).reshape(local_len, seq_count, 3 * width)
    queries = triple[:, :, :width].reshape(local_len, seq_count, head_count, head_size)
    gathered = lax.all_gather(triple[:, :, width:], "seq", axis=0, tiled=True)
    query_pos = lax.axis_index("seq") * local_len + jnp.arange(local_len)
    total_len = gathered.shape[0]
    block = math.gcd(total_len, 256)
    starts = jnp.arange(total_len // block) * block

    def piece_at(start, size):
        piece = lax.dynamic_slice_in_dim(gathered, start, size, 0)
        key_rows = piece[:, :, :width].reshape(size, seq_count, head_count, head_size)
        value_rows = piece[:, :, width:].reshape(size, seq_count, head_count, head_size)
        scores = (
            jnp.einsum("qbhd,kbhd->bhqk", queries, key_rows, preferred_element_type=jnp.float32)
            * scaling
        )
        key_pos = start + jnp.arange(size)
        allowed = query_pos[:, None] >= key_pos[None, :]
        return (jnp.where(allowed, scores, NEGATIVE), allowed, key_rows, value_rows)

    def stats_step(carry, start):
        top, total = carry
        scores, allowed, key_rows, value_rows = piece_at(start, block)
        new_top = jnp.maximum(top, jnp.max(scores, axis=-1))
        lifted = jnp.where(allowed, jnp.exp(scores - new_top[..., None]), 0.0)
        total = total * jnp.exp(top - new_top) + jnp.sum(lifted, axis=-1)
        return ((new_top, total), None)

    stat_shape = (seq_count, head_count, local_len)
    stats, unused = lax.scan(
        stats_step,
        (jnp.full(stat_shape, NEGATIVE, jnp.float32), jnp.zeros(stat_shape, jnp.float32)),
        starts,
    )
    top, total = stats

    def probabilities(scores, allowed):
        return jnp.where(allowed, jnp.exp(scores - top[..., None]) / total[..., None], 0.0)

    def output_step(carry, start):
        scores, allowed, key_rows, value_rows = piece_at(start, block)
        probs = probabilities(scores, allowed).astype(jnp.bfloat16)
        return (
            carry
            + jnp.einsum("bhqk,kbhd->qbhd", probs, value_rows, preferred_element_type=jnp.float32),
            None,
        )

    attended, unused = lax.scan(
        output_step, jnp.zeros((local_len, seq_count, head_count, head_size), jnp.float32), starts
    )
    attended_low = attended.reshape(row_count, width).astype(jnp.bfloat16)
    middle = (
        flat_in
        + jnp.dot(attended_low, merge_weight, preferred_element_type=jnp.float32)
        + merge_bias
    )
    second_set = collect(second_masters, tie_slots[6:12])
    gain_two = second_set[0].astype(jnp.float32)
    shift_two = second_set[1].astype(jnp.float32)
    expand_weight = second_set[2]
    expand_bias = second_set[3].astype(jnp.float32)
    shrink_weight = second_set[4]
    shrink_bias = second_set[5].astype(jnp.float32)
    second, norm_two_pull = jax.vjp(layer_norm, middle, gain_two, shift_two)
    second_low = second.astype(jnp.bfloat16)
    hidden = jnp.dot(second_low, expand_weight, preferred_element_type=jnp.float32) + expand_bias
    active, gelu_pull = jax.vjp(lambda values: jax.nn.gelu(values, approximate=True), hidden)
    active_low = active.astype(jnp.bfloat16)
    result = (
        middle
        + jnp.dot(active_low, shrink_weight, preferred_element_type=jnp.float32)
        + shrink_bias
    )
    output = result.reshape(local_len, seq_count, width).astype(jnp.bfloat16)
    out_grad = cotangent.reshape(row_count, width)
    grad_shrink_weight = jnp.einsum(
        "rf,rd->fd", active_low, out_grad, preferred_element_type=jnp.float32
    )
    grad_shrink_bias = jnp.sum(out_grad.astype(jnp.float32), axis=0)
    active_grad = jnp.einsum(
        "rd,fd->rf", out_grad, shrink_weight, preferred_element_type=jnp.float32
    )
    hidden_grad = gelu_pull(active_grad)[0].astype(jnp.bfloat16)
    grad_expand_weight = jnp.einsum(
        "rd,rf->df", second_low, hidden_grad, preferred_element_type=jnp.float32
    )
    grad_expand_bias = jnp.sum(hidden_grad.astype(jnp.float32), axis=0)
    second_grad = jnp.einsum(
        "rf,df->rd", hidden_grad, expand_weight, preferred_element_type=jnp.float32
    )
    middle_part, grad_gain_two, grad_shift_two = norm_two_pull(second_grad)
    middle_grad = out_grad.astype(jnp.float32) + middle_part
    second_grads = reduce_grads(
        (
            grad_gain_two,
            grad_shift_two,
            grad_expand_weight,
            grad_expand_bias,
            grad_shrink_weight,
            grad_shrink_bias,
        )
    )
    branch_grad = middle_grad.astype(jnp.bfloat16)
    grad_merge_weight = jnp.einsum(
        "rd,re->de", attended_low, branch_grad, preferred_element_type=jnp.float32
    )
    grad_merge_bias = jnp.sum(branch_grad.astype(jnp.float32), axis=0)
    attended_grad = jnp.einsum(
        "re,de->rd", branch_grad, merge_weight, preferred_element_type=jnp.float32
    )
    attended_grad = attended_grad.astype(jnp.bfloat16).reshape(
        local_len, seq_count, head_count, head_size
    )

    def delta_step(carry, start):
        scores, allowed, key_rows, value_rows = piece_at(start, block)
        probs = probabilities(scores, allowed)
        prob_grad = jnp.einsum(
            "qbhd,kbhd->bhqk", attended_grad, value_rows, preferred_element_type=jnp.float32
        )
        return (carry + jnp.sum(probs * prob_grad, axis=-1), None)

    delta, unused = lax.scan(delta_step, jnp.zeros(stat_shape, jnp.float32), starts)

    def score_grad(start, size):
        scores, allowed, key_rows, value_rows = piece_at(start, size)
        probs = probabilities(scores, allowed)
        prob_grad = jnp.einsum(
            "qbhd,kbhd->bhqk", attended_grad, value_rows, preferred_element_type=jnp.float32
        )
        grad_low = (probs * (prob_grad - delta[..., None])).astype(jnp.bfloat16)
        return (probs, grad_low, key_rows)

    def query_step(carry, start):
        probs, grad_low, key_rows = score_grad(start, block)
        return (
            carry
            + jnp.einsum("bhqk,kbhd->qbhd", grad_low, key_rows, preferred_element_type=jnp.float32),
            None,
        )

    query_grad, unused = lax.scan(
        query_step, jnp.zeros((local_len, seq_count, head_count, head_size), jnp.float32), starts
    )
    query_grad = query_grad * scaling
    count = lax.axis_size("seq") * local_len
    size = math.gcd(count, block)

    def one_block(offset):
        probs, grad_low, key_rows = score_grad(offset, size)
        key_grad = (
            jnp.einsum("bhqk,qbhd->kbhd", grad_low, queries, preferred_element_type=jnp.float32)
            * scaling
        )
        value_grad = jnp.einsum(
            "bhqk,qbhd->kbhd",
            probs.astype(jnp.bfloat16),
            attended_grad,
            preferred_element_type=jnp.float32,
        )
        return jnp.concatenate(
            [key_grad.reshape(size, seq_count, width), value_grad.reshape(size, seq_count, width)],
            axis=2,
        )

    terms = lax.map(one_block, jnp.arange(count // size) * size)
    pair_grad = lax.psum_scatter(
        terms.reshape(count, seq_count, 2 * width).astype(jnp.bfloat16),
        "seq",
        scatter_dimension=0,
        tiled=True,
    ).astype(jnp.float32)
    triple_grad = jnp.concatenate(
        [query_grad.reshape(row_count, width), pair_grad.reshape(row_count, 2 * width)], axis=1
    ).astype(jnp.bfloat16)
    grad_triple_weight = jnp.einsum(
        "rd,re->de", normed_low, triple_grad, preferred_element_type=jnp.float32
    )
    column_sums = jnp.sum(triple_grad.astype(jnp.float32), axis=0)
    grad_pair_bias = jnp.concatenate([column_sums[:width], column_sums[2 * width :]])
    normed_grad = jnp.einsum(
        "re,de->rd", triple_grad, triple_weight, preferred_element_type=jnp.float32
    )
    input_part, grad_gain_one, grad_shift_one = norm_one_pull(normed_grad)
    input_grad = (middle_grad + input_part).reshape(local_len, seq_count, width)
    first_grads = reduce_grads(
        (
            grad_gain_one,
            grad_shift_one,
            grad_triple_weight,
            grad_pair_bias,
            grad_merge_weight,
            grad_merge_bias,
        )
    )
    placed_first = into_slots(first_grads, first_masters, tie_slots[0:6])
    placed_second = into_slots(second_grads, second_masters, tie_slots[6:12])
    return (
        output,
        input_grad,
        placed_first[0],
        placed_first[1],
        placed_first[2],
        placed_first[3],
        placed_first[4],
        placed_first[5],
        placed_second[0],
        placed_second[1],
        placed_second[2],
        placed_second[3],
        placed_second[4],
        placed_second[5],
    )


def solution(mesh):
    in_specs = (
        P("seq", "dp", None),
        P("seq", "dp", None),
        P(),
        P(None, "dp"),
        P(None, "dp"),
        P(None, "dp", None),
        P(None, "dp"),
        P(None, "dp", None),
        P(None, "dp"),
        P(None, "dp"),
        P(None, "dp"),
        P(None, "dp", None),
        P(None, "dp"),
        P(None, "dp", None),
        P(None, "dp"),
    )
    out_specs = (
        P("seq", "dp", None),
        P("seq", "dp", None),
        P(None, "dp"),
        P(None, "dp"),
        P(None, "dp", None),
        P(None, "dp"),
        P(None, "dp", None),
        P(None, "dp"),
        P(None, "dp"),
        P(None, "dp"),
        P(None, "dp", None),
        P(None, "dp"),
        P(None, "dp", None),
        P(None, "dp"),
    )
    return jax.shard_map(
        per_device, mesh=mesh, in_specs=in_specs, out_specs=out_specs, check_vma=False
    )
```

profile of v0, /device:TPU:0, one launch (start us, length us, event | category | flops | bytes accessed | tf_op | source)
XLA Modules:
  0.0 832.1 jit_solution(4565038491413289318)
XLA Ops:
  35.6 63.5 %all-reduce.17 = (bf16[1536]{0:T(1024)(128)(2,1)S(1)}, bf16[768]{0:T(1024)(128)(2,1)S(1)}, bf16[768]{0:T(1024)(128)(2,1)S(1)}, bf16[768]{0:T(1024)(128)(2,1)S(1)...) all-reduce(bf16[1536]{0:T(1024)(128)(2,1)S(1)} %dynamic-update-slic, ...), channel_id=5, replica_groups=mesh['dp'=16,'seq'=2] {'dp'}, use_global_device_ids=true, to_apply=%add.2 | all-reduce | flops 8448 | bytes 33792
  122.6 29.5 %all-gather.18.cloned.1.call-done = bf16[1024,1,1536]{2,0,1:T(8,128)(2,1)} async-done(((bf16[512,1,1536]{2,0,1:T(8,128)(2,1)}), bf16[1024,1,1536]{2,0,1:T(8,128)(2,1)}) %all-gather.18.cloned.1.call-update) | async-done | bytes 3145744 | tf_op jit(solution)/shard_map/all_gather | solution.py:127
  156.8 59.7 %while.58 = (s32[]{:T(128)}, f32[1,12,512]{2,1,0:T(8,128)}, f32[1,12,512]{2,1,0:T(8,128)}, s32[4]{0:T(128)S(1)}, bf16[1024,1,1536]{0,2,1:T(8,128)(2,1)}, /*index...) while((s32[]{:T(128)}, f32[1,12,512]{2,1,0:T(8,128)}, ...), condition=%wide.region_5.6_spmd.clone, body=%wide.region_2.5_spmd.clone.sunk | while | flops 214072064 | bytes 15268010 | solution.py:154
  216.6 39.8 %while.59 = (s32[]{:T(128)}, f32[512,1,12,64]{0,3,2,1:T(8,128)}, s32[4]{0:T(128)S(1)}, bf16[1024,1,1536]{0,2,1:T(8,128)(2,1)}, bf16[512,1,12,64]{0,3,2,1:T(8,128...) while((s32[]{:T(128)}, f32[512,1,12,64]{0,3,2,1:T(8,128)}, ...), condition=%wide.region_7.8_spmd.clone, body=%wide.region_6.7_spmd.clone.sunk | while | flops 413008640 | bytes 6609097 | solution.py:173
  231.2 5.0 bitcast_add_fusion.9
  241.4 5.0 bitcast_add_fusion.9
  251.4 5.0 bitcast_add_fusion.9
  261.7 7.3 fusion.91
  269.0 33.9 %all-gather.26.cloned.1.call-done = bf16[1,3072,768]{2,1,0:T(8,128)(2,1)} async-done(((bf16[1,192,768]{2,1,0:T(8,128)(2,1)}), bf16[1,3072,768]{2,1,0:T(8,128)(2,1)}) %all-gather.26.cloned.1.call-update) | async-done | bytes 4718608 | tf_op jit(solution)/shard_map/all_gather | solution.py:34
  302.9 10.1 %fusion.156 = (bf16[3072]{0:T(1024)(128)(2,1)}, bf16[512,3072]{1,0:T(8,128)(2,1)S(1)}) fusion(f32[512,3072]{1,0:T(8,128)} %fusion.91, f32[3072]{0:T(1024)S(1)} %copy-done.24, bf16[512,1,768]{2,0,1:T(8,128)(2,1)S(1)} %copy-done.6, bf16[1,3072,768]{2,1,0:T(8,128)(2,1)} %all-gather.26.cloned.1.call-done), kind=kOutput, calls=%fused_computation.241 | convolution fusion | flops 2450519040 | bytes 14960640 | tf_op jit(solution)/shard_map/rd,fd->rf/dot_general | solution.py:205
  320.2 42.2 %while.60 = (s32[]{:T(128)}, f32[1,12,512]{2,1,0:T(8,128)}, s32[4]{0:T(128)S(1)}, bf16[1024,1,1536]{0,2,1:T(8,128)(2,1)}, bf16[512,1,12,64]{0,3,2,1:T(8,128)(2,1...) while((s32[]{:T(128)}, f32[1,12,512]{2,1,0:T(8,128)}, ...), condition=%wide.region_14.15_spmd.clone, body=%wide.region_12.14_spmd.clone.sunk | while | flops 413801216 | bytes 16931024 | solution.py:248
  362.4 82.0 %while.57 = (s32[]{:T(128)}, bf16[4,256,1,1536]{3,1,0,2:T(8,128)(2,1)}, s32[4]{0:T(128)S(1)}, bf16[1024,1,1536]{0,2,1:T(8,128)(2,1)}, bf16[512,1,12,64]{0,3,2,1:...) while((s32[]{:T(128)}, ...), condition=%wide.region_18.19_spmd.clone, body=%wide.region_17.18_spmd.clone.sunk | while | flops 821560064 | bytes 30227152 | solution.py:291
  367.5 5.7 fusion.211
  373.1 4.7 fusion.213
  388.0 5.7 fusion.211
  393.7 4.7 fusion.213
  408.5 5.7 fusion.211
  428.9 5.7 fusion.211
  448.1 7.3 convolution_convert_fusion.1
  456.5 8.6 %convolution_convert_fusion = bf16[3072,768]{1,0:T(8,128)(2,1)} fusion(bf16[512,1,768]{2,0,1:T(8,128)(2,1)S(1)} %copy-done.7, f32[512,3072]{1,0:T(8,128)} %fusion.91, f32[3072]{0:T(1024)S(1)} %copy-done.25), kind=kOutput, calls=%fused_computation.111 | convolution fusion | flops 2434007040 | bytes 11808768 | tf_op jit(solution)/shard_map/rf,rd->fd/dot_general | solution.py:201
  465.2 63.6 %while.61 = (s32[]{:T(128)}, f32[512,1,12,64]{0,3,2,1:T(8,128)}, s32[4]{0:T(128)S(1)}, bf16[1024,1,1536]{0,2,1:T(8,128)(2,1)}, bf16[512,1,12,64]{0,3,2,1:T(8,128...) while((s32[]{:T(128)}, f32[512,1,12,64]{0,3,2,1:T(8,128)}, ...), condition=%wide.region_16.17_spmd.clone, body=%wide.region_15.16_spmd.clone.sunk | while | flops 617480960 | bytes 20396248 | solution.py:267
  473.9 6.8 bitcast_add_fusion.11
  489.5 7.3 bitcast_add_fusion.11
  505.5 7.4 bitcast_add_fusion.11
  521.5 7.3 bitcast_add_fusion.11
  530.9 5.5 convolution_convert_fusion.2
  558.6 59.5 %all-reduce.16 = (bf16[768]{0:T(1024)(128)(2,1)S(1)}, bf16[768]{0:T(1024)(128)(2,1)S(1)}, bf16[768]{0:T(1024)(128)(2,1)S(1)}, bf16[1536]{0:T(1024)(128)(2,1)S(1)...) all-reduce(bf16[768]{0:T(1024)(128)(2,1)S(1)} %dynamic-update-slice, ...), channel_id=13, replica_groups=mesh['dp'=16,'seq'=2] {'dp'}, use_global_device_ids=true, to_apply=%add.7 | all-reduce | flops 9984 | bytes 39936
  618.8 5.1 all-reduce.18
  632.1 75.1 %reduce-scatter.14.cloned.1.call-done = bf16[192,768]{1,0:T(8,128)(2,1)} async-done(((bf16[3072,768]{1,0:T(8,128)(2,1)}), bf16[192,768]{1,0:T(8,128)(2,1)}) %reduce-scatter.14.cloned.1.call-update) | async-done | bytes 294928 | tf_op jit(solution)/shard_map/reduce_scatter | solution.py:53
  707.2 71.3 %reduce-scatter.8.cloned.1.call-done = bf16[48,2304]{1,0:T(8,128)(2,1)} async-done(((bf16[768,2304]{1,0:T(8,128)(2,1)}), bf16[48,2304]{1,0:T(8,128)(2,1)}) %reduce-scatter.8.cloned.1.call-update) | async-done | bytes 221200 | tf_op jit(solution)/shard_map/reduce_scatter | solution.py:47
  778.5 9.0 %fusion.116 = bf16[512,1,768]{2,0,1:T(8,128)(2,1)} fusion(f32[512,768]{1,0:T(8,128)S(1)} %copy-done.10, bf16[1,3072,768]{2,1,0:T(8,128)(2,1)} %all-gather.26.cloned.1.call-done, f32[768]{0:T(1024)S(1)} %convert_element_type.446, f32[512,3072]{1,0:T(8,128)} %fusion.91, f32[3072]{0:T(1024)S(1)} %copy-done.25), kind=kOutput, calls=%fused_computation.157 | convolution fusion | flops 2432827392 | bytes 13384704 | tf_op jit(solution)/shard_map/dot_general | solution.py:196
  787.5 29.6 %all-reduce.22.cloned.1.call-done = (bf16[48,2304]{1,0:T(8,128)(2,1)}, bf16[48,768]{1,0:T(8,128)(2,1)}, bf16[48,3072]{1,0:T(8,128)(2,1)}, bf16[192,768]{1,0:T(8,128)(2,1)}) async-done(((bf16[48,2304]{1,0:T(8,128)(2,1)}, bf16[48,768]{1,0:T(8,128)(2,1)}, bf16[48,3072]{1,0:T(8,128)(2,1)}, bf16[192,768]{1,0:T(8,128)(2,1)}), (bf16[48,2304]{1,0:T(8,128)(2,1)}, bf16[48,768]{1,0:T(8,128)(2,1)}, ...) | async-done | bytes 884752 | tf_op jit(solution)/shard_map/psum | solution.py:63
  (392 shorter events, 259.4 us)
Async XLA Ops:
  7.2 108.3 %copy-start = (f32[2,48,3072]{2,1,0:T(8,128)S(1)}, f32[2,48,3072]{2,1,0:T(8,128)}, u32[]{:S(2)}) copy-start(f32[2,48,3072]{2,1,0:T(8,128)} %param.36) | copy-start | bytes 3538948
  7.2 95.5 %all-gather.20.cloned.1.call-start = ((), (), s32[]{:S(2)}) async-start(), calls=%async_computation.11 | async-start | bytes 3760128 | tf_op jit(solution)/shard_map/all_gather | solution.py:32
  12.5 139.7 %all-gather.18.cloned.1.call-start = ((), (), s32[]{:S(2)}) async-start(), calls=%async_computation.5 | async-start | bytes 4718592 | tf_op jit(solution)/shard_map/all_gather | solution.py:127
  99.2 7.9 copy-start.14
  99.2 7.9 copy-start.28
  100.6 6.5 copy-start.16
  109.9 148.9 %all-gather.22.cloned.1.call-start = ((), (), s32[]{:S(2)}) async-start(), calls=%async_computation.12 | async-start | bytes 1253376 | tf_op jit(solution)/shard_map/all_gather | solution.py:34
  113.5 148.2 %all-gather.24.cloned.1.call-start = ((), (), s32[]{:S(2)}) async-start(), calls=%async_computation.13 | async-start | bytes 5013504 | tf_op jit(solution)/shard_map/all_gather | solution.py:32
  116.3 186.6 %all-gather.26.cloned.1.call-start = ((), (), s32[]{:S(2)}) async-start(), calls=%async_computation.14 | async-start | bytes 5013504 | tf_op jit(solution)/shard_map/all_gather | solution.py:34
  120.2 410.6 %reduce-scatter.6.cloned.1.call-start = ((), (), s32[]{:S(2)}) async-start(), calls=%async_computation.6 | async-start | bytes 4718592 | tf_op jit(solution)/shard_map/reduce_scatter | solution.py:292
  120.6 141.1 %copy-start.30 = (f32[768]{0:T(1024)}, f32[768]{0:T(1024)S(1)}, u32[]{:S(2)}) copy-start(f32[768]{0:T(1024)S(1)} %convert_element_type.444) | copy-start | bytes 9220
  216.6 42.3 %copy-start.4 = (bf16[512,1,768]{2,0,1:T(8,128)(2,1)S(1)}, bf16[512,1,768]{2,0,1:T(8,128)(2,1)}, u32[]{:S(2)}) copy-start(bf16[512,1,768]{2,0,1:T(8,128)(2,1)} %param.25) | copy-start | bytes 2359300
  261.3 55.3 %copy-start.8 = (f32[512,768]{1,0:T(8,128)}, f32[512,768]{1,0:T(8,128)S(1)}, u32[]{:S(2)}) copy-start(f32[512,768]{1,0:T(8,128)S(1)} %get-tuple-element.788) | copy-start | bytes 4718596
  261.6 41.3 %copy-start.6 = (bf16[512,1,768]{2,0,1:T(8,128)(2,1)S(1)}, bf16[512,1,768]{2,0,1:T(8,128)(2,1)}, u32[]{:S(2)}) copy-start(bf16[512,1,768]{2,0,1:T(8,128)(2,1)} %param.26) | copy-start | bytes 2359300
  261.6 41.3 %copy-start.24 = (f32[3072]{0:T(1024)S(1)}, f32[3072]{0:T(1024)}, u32[]{:S(2)}) copy-start(f32[3072]{0:T(1024)} %convert_element_type.445) | copy-start | bytes 36868
  302.9 10.2 %copy-start.37 = (bf16[1,768,3072]{2,1,0:T(8,128)(2,1)S(1)}, bf16[1,768,3072]{2,1,0:T(8,128)(2,1)}, u32[]{:S(2)}) copy-start(bf16[1,768,3072]{2,1,0:T(8,128)(2,1)} %all-gather.24.cloned.1.call-done) | copy-start | bytes 14155780
  444.5 187.6 %reduce-scatter.10.cloned.1.call-start = ((), (), s32[]{:S(2)}) async-start(), calls=%async_computation.8 | async-start | bytes 1253376 | tf_op jit(solution)/shard_map/reduce_scatter | solution.py:53
  448.0 184.1 %reduce-scatter.12.cloned.1.call-start = ((), (), s32[]{:S(2)}) async-start(), calls=%async_computation.9 | async-start | bytes 5013504 | tf_op jit(solution)/shard_map/reduce_scatter | solution.py:47
  455.4 251.7 %reduce-scatter.14.cloned.1.call-start = ((), (), s32[]{:S(2)}) async-start(), calls=%async_computation.10 | async-start | bytes 5013504 | tf_op jit(solution)/shard_map/reduce_scatter | solution.py:53
  465.2 313.3 %reduce-scatter.8.cloned.1.call-start = ((), (), s32[]{:S(2)}) async-start(), calls=%async_computation.7 | async-start | bytes 3760128 | tf_op jit(solution)/shard_map/reduce_scatter | solution.py:47
  536.4 280.7 %all-reduce.22.cloned.1.call-start = ((), (), s32[]{:S(2)}) async-start(), calls=%async_computation.15 | async-start | bytes 1769472 | tf_op jit(solution)/shard_map/psum | solution.py:63
  551.9 6.7 copy-start.26
  551.9 6.7 copy-start.27
  551.9 6.7 copy-start.32
  552.0 6.7 copy-start.33
  552.0 72.0 %copy-start.19 = (f32[512]{0:T(512)S(1)}, f32[512]{0:T(512)}, u32[]{:S(2)}) copy-start(f32[512]{0:T(512)} %copy-done.18) | copy-start | bytes 6148
  556.6 67.4 %copy-start.3 = (f32[512,768]{1,0:T(8,128)S(1)}, f32[512,768]{1,0:T(8,128)}, u32[]{:S(2)}) copy-start(f32[512,768]{1,0:T(8,128)} %copy-done.2) | copy-start | bytes 4718596
  626.1 152.4 %copy-start.10 = (f32[512,768]{1,0:T(8,128)S(1)}, f32[512,768]{1,0:T(8,128)}, u32[]{:S(2)}) copy-start(f32[512,768]{1,0:T(8,128)} %copy-done.8) | copy-start | bytes 4718596
  778.5 42.6 %copy-start.36 = (f32[2]{0:T(128)S(1)}, f32[2]{0:T(128)}, u32[]{:S(2)}) copy-start(f32[2]{0:T(128)} %compare_convert_fusion.1) | copy-start | bytes 28
  787.5 34.8 %copy-start.35 = (f32[2]{0:T(128)S(1)}, f32[2]{0:T(128)}, u32[]{:S(2)}) copy-start(f32[2]{0:T(128)} %compare_convert_fusion.3) | copy-start | bytes 28
  818.1 6.4 copy-start.34
  818.1 7.2 copy-start.1
  (22 other events, 51.4 us)
Sparse Core Ops, SparseCore 0:
  12.6 50.3 all-gather.19
  110.0 42.0 all-gather.17
  155.0 38.3 all-gather.21
  196.1 52.1 all-gather.23
  251.0 51.8 all-gather.25
  444.6 41.9 reduce-scatter.5
  491.2 58.0 reduce-scatter.9
  553.6 75.0 reduce-scatter.11
  632.5 74.5 reduce-scatter.13
  711.4 67.0 reduce-scatter.7
  781.2 35.9 all-reduce.21
where the time goes:
time: 841 us; the launch traced here: 832 us
  waiting for transfers between devices  240 us (29%)
  matrix products  219 us (26%)
  blocking collectives  128 us (15%)
  local copies, waits for them, and re-layouts  82.8 us (10%)
  other arithmetic  80.2 us (10%)
  between operations  41.8 us (5%)
  loops' own time  39.5 us (5%)
    unnamed x2, blocking collectives  123 us
    reduce_scatter x2, waiting for transfers between devices, reduce_grads(): lax.psum_scatter(grads[4].astype(jnp.bfloat16), 'dp', scatter_dimension=0...  75.1 us
    reduce_scatter x2, waiting for transfers between devices, reduce_grads(): lax.psum_scatter(grads[2].astype(jnp.bfloat16), 'dp', scatter_dimension=0...  71.3 us
    dot_general x16, matrix products, piece_at(): jnp.einsum('qbhd,kbhd->bhqk', queries, key_rows, preferred_element_type=j...  56.5 us
    all_gather x2, waiting for transfers between devices, collect(): lax.all_gather(chosen[4], 'dp', axis=0, tiled=True)  33.9 us
    psum x1, waiting for transfers between devices, reduce_grads(): lax.psum(parts[2].astype(jnp.bfloat16), 'seq').astype(jnp.float32)  29.6 us
    all_gather x1, waiting for transfers between devices, per_device(): gathered = lax.all_gather(triple[:, :, width:], 'seq', axis=0, tiled=True)  29.5 us
    dot_general x4, matrix products, query_step(): jnp.einsum('bhqk,kbhd->qbhd', grad_low, key_rows, preferred_element_type=...  28.9 us
  transfers between devices with their start and end apart: 11, of which 5 were waited for; matrix products, arithmetic and copies ran while one was open for 28% of the time, Pallas kernels for 0%

commit v1 on v0

v1 whole, which is shorter than its diff:
```python
import functools
import math

import jax
import jax.numpy as jnp
from jax import lax
from jax.experimental import pallas as pl
from jax.experimental.pallas import tpu as pltpu
from jax.sharding import PartitionSpec as P

H = 12
GROUPS = 16
EPSILON = 1e-05
NEGATIVE = -1e30
F32 = jnp.float32
BF16 = jnp.bfloat16
VMEM_LIMIT = 56 * 1024 * 1024


def layer_norm(values, gain, shift):
    average = jnp.mean(values, axis=-1, keepdims=True)
    centered = values - average
    variance = jnp.mean(centered * centered, axis=-1, keepdims=True)
    return centered * lax.rsqrt(variance + EPSILON) * gain + shift


def dot(left, right, left_dim, right_dim):
    return lax.dot_general(
        left, right, (((left_dim,), (right_dim,)), ((), ())), preferred_element_type=F32
    )


def pair_masks():
    lane = lax.broadcasted_iota(jnp.int32, (1, 128), 1)
    low = (lane < 64).astype(F32)
    return low, 1.0 - low


def causal(scores, block):
    key = lax.broadcasted_iota(jnp.int32, (block, block), 0)
    query = lax.broadcasted_iota(jnp.int32, (block, block), 1)
    return jnp.where(key <= query, scores, NEGATIVE)


def attend_kernel(count, q_ref, k_ref, v_ref, rk_ref, rv_ref, o_ref, lse_ref, *, block):
    rows = q_ref.shape[0]
    masks = pair_masks()
    for index in range(rows // block):
        here = slice(index * block, (index + 1) * block)
        size = (index + 1) * block
        state = []
        parts = []
        for head in range(2):
            query = q_ref[here, :] * (masks[head] * 0.125).astype(BF16)
            parts.append(query)
            scores = dot(k_ref[0:size, :], query, 1, 1)
            last = causal(scores[size - block :], block)
            top = jnp.max(last, axis=0, keepdims=True)
            if index:
                scores = jnp.concatenate([scores[: size - block], last], axis=0)
                top = jnp.max(scores, axis=0, keepdims=True)
            else:
                scores = last
            lifted = jnp.exp(scores - top)
            total = jnp.sum(lifted, axis=0, keepdims=True)
            state += [top, total, dot(v_ref[0:size, :], lifted.astype(BF16), 0, 0)]

        def far(step, state):
            start = pl.multiple_of(step * rows, rows)
            keys = rk_ref[pl.ds(start, rows), :]
            values = rv_ref[pl.ds(start, rows), :]
            result = []
            for head in range(2):
                top, total, gathered = state[3 * head : 3 * head + 3]
                scores = dot(keys, parts[head], 1, 1)
                new_top = jnp.maximum(top, jnp.max(scores, axis=0, keepdims=True))
                factor = jnp.exp(top - new_top)
                lifted = jnp.exp(scores - new_top)
                total = total * factor + jnp.sum(lifted, axis=0, keepdims=True)
                gathered = gathered * factor + dot(values, lifted.astype(BF16), 0, 0)
                result += [new_top, total, gathered]
            return tuple(result)

        top0, total0, sum0, top1, total1, sum1 = lax.fori_loop(0, count[0], far, tuple(state))
        joined = jnp.concatenate([sum0[:64] / total0, sum1[64:] / total1], axis=0)
        o_ref[here, :] = jnp.transpose(joined).astype(BF16)
        lse_ref[0, 0:1, here] = top0 + jnp.log(total0)
        lse_ref[0, 1:2, here] = top1 + jnp.log(total1)


def attend(count, queries, triple, remote, block):
    rows, width = queries.shape[0], triple.shape[1] // 3
    pairs = width // 128
    far_rows = remote.shape[0]
    column = lambda size, offset: pl.BlockSpec((size, 128), lambda h, c: (0, h + offset))
    return pl.pallas_call(
        functools.partial(attend_kernel, block=block),
        grid_spec=pltpu.PrefetchScalarGridSpec(
            num_scalar_prefetch=1,
            grid=(pairs,),
            in_specs=[
                column(rows, 0),
                column(rows, pairs),
                column(rows, 2 * pairs),
                column(far_rows, 0),
                column(far_rows, pairs),
            ],
            out_specs=[column(rows, 0), pl.BlockSpec((1, 2, rows), lambda h, c: (h, 0, 0))],
        ),
        out_shape=[
            jax.ShapeDtypeStruct((rows, width), BF16),
            jax.ShapeDtypeStruct((pairs, 2, rows), F32),
        ],
        compiler_params=pltpu.CompilerParams(vmem_limit_bytes=VMEM_LIMIT),
        cost_estimate=pl.CostEstimate(
            flops=8 * rows * rows * width, bytes_accessed=rows * width * 12, transcendentals=rows * rows * 12
        ),
        name="attend",
    )(count, triple, triple, triple, remote, remote)


def attend_back_kernel(
    count, q_ref, k_ref, v_ref, rk_ref, rv_ref, do_ref, o_ref, lse_ref,
    dq_ref, dk_ref, dv_ref, rdk_ref, rdv_ref, dq_sum, dk_sum, dv_sum, *, block,
):
    rows = q_ref.shape[0]
    far_rows = rk_ref.shape[0]
    masks = pair_masks()
    blocks = rows // block

    def prepare(index):
        here = slice(index * block, (index + 1) * block)
        out_grad = do_ref[here, :]
        product = jnp.transpose(out_grad.astype(F32) * o_ref[here, :].astype(F32))
        result = []
        for head in range(2):
            query = q_ref[here, :] * (masks[head] * 0.125).astype(BF16)
            masked = out_grad * masks[head].astype(BF16)
            delta = jnp.sum(product[64 * head : 64 * head + 64], axis=0, keepdims=True)
            lse = lse_ref[0, head : head + 1, here]
            result.append((query, masked, delta, lse))
        return result

    def terms(ready, keys, values, diagonal):
        key_grad = value_grad = query_grad = 0.0
        for head in range(2):
            query, masked, delta, lse = ready[head]
            scores = dot(keys, query, 1, 1)
            if diagonal:
                size = scores.shape[0]
                last = causal(scores[size - block :], block)
                if size > block:
                    scores = jnp.concatenate([scores[: size - block], last], axis=0)
                else:
                    scores = last
            probs = jnp.exp(scores - lse)
            prob_grad = dot(values, masked, 1, 1)
            score_grad = (probs * (prob_grad - delta)).astype(BF16)
            value_grad += dot(probs.astype(BF16), masked, 1, 0)
            key_grad += dot(score_grad, query, 1, 0)
            part = keys * (masks[head] * 0.125).astype(BF16)
            query_grad += dot(part, score_grad, 0, 0)
        return key_grad, value_grad, query_grad

    for index in reversed(range(blocks)):
        here = slice(index * block, (index + 1) * block)
        size = (index + 1) * block
        key_grad, value_grad, query_grad = terms(
            prepare(index), k_ref[0:size, :], v_ref[0:size, :], True
        )
        if index == blocks - 1:
            dk_sum[...] = key_grad
            dv_sum[...] = value_grad
        else:
            dk_sum[0:size, :] += key_grad
            dv_sum[0:size, :] += value_grad
        dq_sum[:, here] = query_grad

    def far(step, unused):
        start = pl.multiple_of(step * rows, rows)
        spot = pl.ds(start, rows)
        keys = rk_ref[spot, :]
        values = rv_ref[spot, :]
        key_total = value_total = 0.0
        for index in range(blocks):
            here = slice(index * block, (index + 1) * block)
            key_grad, value_grad, query_grad = terms(prepare(index), keys, values, False)
            key_total += key_grad
            value_total += value_grad
            dq_sum[:, here] += query_grad
        rdk_ref[spot, :] = key_total.astype(BF16)
        rdv_ref[spot, :] = value_total.astype(BF16)
        return unused

    lax.fori_loop(0, count[0], far, 0)

    def clear(step, unused):
        spot = pl.ds(pl.multiple_of(step * rows, rows), rows)
        rdk_ref[spot, :] = jnp.zeros((rows, 128), BF16)
        rdv_ref[spot, :] = jnp.zeros((rows, 128), BF16)
        return unused

    lax.fori_loop(count[0], far_rows // rows, clear, 0)
    dq_ref[...] = jnp.transpose(dq_sum[...]).astype(BF16)
    dk_ref[...] = dk_sum[...]
    dv_ref[...] = dv_sum[...]


def attend_back(count, triple, remote, out_grad, attended, lse, block):
    rows, width = attended.shape
    pairs = width // 128
    far_rows = remote.shape[0]
    column = lambda size, offset: pl.BlockSpec((size, 128), lambda h, c: (0, h + offset))
    return pl.pallas_call(
        functools.partial(attend_back_kernel, block=block),
        grid_spec=pltpu.PrefetchScalarGridSpec(
            num_scalar_prefetch=1,
            grid=(pairs,),
            in_specs=[
                column(rows, 0),
                column(rows, pairs),
                column(rows, 2 * pairs),
                column(far_rows, 0),
                column(far_rows, pairs),
                column(rows, 0),
                column(rows, 0),
                pl.BlockSpec((1, 2, rows), lambda h, c: (h, 0, 0)),
            ],
            out_specs=[
                column(rows, 0),
                column(rows, 0),
                column(rows, 0),
                column(far_rows, 0),
                column(far_rows, 0),
            ],
            scratch_shapes=[
                pltpu.VMEM((128, rows), F32),
                pltpu.VMEM((rows, 128), F32),
                pltpu.VMEM((rows, 128), F32),
            ],
        ),
        out_shape=[
            jax.ShapeDtypeStruct((rows, width), BF16),
            jax.ShapeDtypeStruct((rows, width), F32),
            jax.ShapeDtypeStruct((rows, width), F32),
            jax.ShapeDtypeStruct((far_rows, width), BF16),
            jax.ShapeDtypeStruct((far_rows, width), BF16),
        ],
        compiler_params=pltpu.CompilerParams(vmem_limit_bytes=VMEM_LIMIT),
        cost_estimate=pl.CostEstimate(
            flops=20 * rows * rows * width, bytes_accessed=rows * width * 30, transcendentals=rows * rows * 12
        ),
        name="attend_back",
    )(count, triple, triple, triple, remote, remote, out_grad, attended, lse)


def pairs_of(count, target):
    return [(index, target(index)) for index in range(count)]


def swap_cores(value, count):
    return lax.ppermute(value, "dp", pairs_of(count, lambda index: index ^ 1))


def swap_seq(value):
    return lax.ppermute(value, "seq", [(0, 1), (1, 0)])


def regroup(value, dp, moves):
    pairs = []
    for index in range(0, dp, 2):
        left, right = (index + 1) * 2, index * 2 + 1
        pairs += [(left, right), (right, left)]
    return jnp.where(moves, lax.ppermute(value, ("dp", "seq"), pairs), value)


def split_columns(value, width):
    return [value[:, at : at + width] for at in range(0, value.shape[1], width)]


def gather_pack(blocks, dp):
    sizes = [block.shape[0] for block in blocks]
    packed = lax.all_gather(jnp.concatenate(blocks, axis=0), "dp", axis=0)
    if dp == GROUPS:
        return packed
    parts, at = [], 0
    for size in sizes:
        part = packed[:, at : at + size]
        parts.append(part.reshape(GROUPS, -1, part.shape[2]))
        at += size
    return jnp.concatenate(parts, axis=1)


def scatter_pack(packed, sizes, dp):
    if dp != GROUPS:
        parts, at = [], 0
        for size in sizes:
            whole = size * dp // GROUPS
            part = packed[:, at : at + whole]
            parts.append(part.reshape(dp, size, part.shape[2]))
            at += whole
        packed = jnp.concatenate(parts, axis=1)
    return lax.psum_scatter(packed, "dp", scatter_dimension=0)


def sum_seq(value, sequence_parts):
    if sequence_parts == 2:
        return value.astype(F32) + swap_seq(value).astype(F32)
    return lax.psum(value, "seq").astype(F32)


def place(grad, master, slot):
    marker = (jnp.arange(master.shape[0]) == slot).astype(F32)
    return marker.reshape((-1,) + (1,) * grad.ndim) * grad[None]


def per_device(
    inputs,
    cotangent,
    tie_slots,
    *masters,
):
    dp, sequence_parts = lax.axis_size("dp"), lax.axis_size("seq")
    length, count, width = inputs.shape
    rows = length * count
    block = math.gcd(length, 256)
    moved = sequence_parts == 2 and dp % 2 == 0
    core = lax.axis_index("dp") % 2
    moves = core != lax.axis_index("seq")
    place_index = core if moved else lax.axis_index("seq")
    chosen = [
        lax.dynamic_index_in_dim(masters[number], tie_slots[number], 0, keepdims=False).astype(BF16)
        for number in range(12)
    ]
    part = width // dp
    ff = masters[10].shape[1] * dp
    small = jnp.concatenate([chosen[number] for number in (0, 1, 3, 5, 6, 7, 9, 11)])
    widths = [chosen[number].shape[0] for number in (0, 1, 3, 5, 6, 7, 9, 11)]
    pad = 16 * GROUPS // dp
    small = jnp.pad(small.reshape(1, -1), ((0, pad - 1), (0, width - small.shape[0])))
    head_blocks = split_columns(chosen[2], width) + [chosen[4], small]
    tail_blocks = [chosen[10]] + split_columns(chosen[8], width)
    head_sizes = [piece.shape[0] for piece in head_blocks]
    tail_sizes = [piece.shape[0] for piece in tail_blocks]
    head_pack = gather_pack(head_blocks, dp)
    flat_in = inputs.reshape(rows, width)
    flat_cot = cotangent.reshape(rows, width)
    if moved:
        flat_in = regroup(flat_in, dp, moves)
        flat_cot = regroup(flat_cot, dp, moves)
    tail_pack = gather_pack(tail_blocks, dp)

    group_rows = width // GROUPS
    matrix = lambda pack, at: pack[:, at * group_rows : (at + 1) * group_rows].reshape(width, width)
    triple_weight = jnp.concatenate([matrix(head_pack, at) for at in range(3)], axis=1)
    merge_weight = matrix(head_pack, 3)
    per_group = GROUPS // dp if dp < GROUPS else dp // GROUPS
    lines = head_pack[:, 4 * group_rows :].reshape(dp, pad, width)[:, 0]
    vectors, at = [], 0
    for size in widths:
        vectors.append(lines[:, at : at + size].reshape(-1).astype(F32))
        at += size
    gain_one, shift_one, pair_bias, merge_bias, gain_two, shift_two, expand_bias, shrink_bias = vectors

    flat_in = flat_in.astype(F32)
    normed, norm_one_pull = jax.vjp(layer_norm, flat_in, gain_one, shift_one)
    normed_low = normed.astype(BF16)
    bias_full = jnp.concatenate([pair_bias[:width], jnp.zeros((width,), F32), pair_bias[width:]])
    triple = (jnp.dot(normed_low, triple_weight, preferred_element_type=F32) + bias_full).astype(BF16)
    near = triple[:, width:]
    if moved:
        remote = swap_cores(near, dp)
    else:
        remote = lax.all_gather(near, "seq", axis=0, tiled=True)
    far_count = place_index.astype(jnp.int32).reshape(1)
    attended_low, lse = attend(far_count, triple, triple, remote, block)
    middle = flat_in + jnp.dot(attended_low, merge_weight, preferred_element_type=F32) + merge_bias

    ff_rows = ff // GROUPS
    shrink_weight = tail_pack[:, :ff_rows].reshape(ff, width)
    expand_weight = jnp.concatenate(
        [
            tail_pack[:, ff_rows + at * group_rows : ff_rows + (at + 1) * group_rows].reshape(width, width)
            for at in range(ff // width)
        ],
        axis=1,
    )
    second, norm_two_pull = jax.vjp(layer_norm, middle, gain_two, shift_two)
    second_low = second.astype(BF16)
    hidden = jnp.dot(second_low, expand_weight, preferred_element_type=F32) + expand_bias
    active, gelu_pull = jax.vjp(lambda values: jax.nn.gelu(values, approximate=True), hidden)
    active_low = active.astype(BF16)
    result = middle + jnp.dot(active_low, shrink_weight, preferred_element_type=F32) + shrink_bias
    output = result.astype(BF16)
    if moved:
        output = regroup(output, dp, moves)
    grad_shrink_weight = dot(active_low, flat_cot, 0, 0)
    grad_shrink_bias = jnp.sum(flat_cot.astype(F32), axis=0)
    active_grad = dot(flat_cot, shrink_weight, 1, 1)
    hidden_grad = gelu_pull(active_grad)[0].astype(BF16)
    grad_expand_weight = dot(second_low, hidden_grad, 0, 0)
    grad_expand_bias = jnp.sum(hidden_grad.astype(F32), axis=0)
    second_grad = dot(hidden_grad, expand_weight, 1, 1)
    middle_part, grad_gain_two, grad_shift_two = norm_two_pull(second_grad)
    middle_grad = flat_cot.astype(F32) + middle_part
    grouped = lambda value: value.astype(BF16).reshape(GROUPS, -1, width)
    tail_grads = jnp.concatenate(
        [grouped(grad_shrink_weight)] + [grouped(piece) for piece in split_columns(grad_expand_weight, width)],
        axis=1,
    )
    tail_own = sum_seq(scatter_pack(tail_grads, tail_sizes, dp), sequence_parts)

    branch_grad = middle_grad.astype(BF16)
    grad_merge_weight = dot(attended_low, branch_grad, 0, 0)
    grad_merge_bias = jnp.sum(branch_grad.astype(F32), axis=0)
    attended_grad = dot(branch_grad, merge_weight, 1, 1).astype(BF16)
    query_grad, key_grad, value_grad, far_key, far_value = attend_back(
        far_count, triple, remote, attended_grad, attended_low, lse, block
    )
    far_grad = jnp.concatenate([far_key, far_value], axis=1)
    pair_grad = jnp.concatenate([key_grad, value_grad], axis=1)
    if moved:
        pair_grad = pair_grad + swap_cores(far_grad, dp).astype(F32)
    else:
        pair_grad = pair_grad + lax.psum_scatter(far_grad, "seq", scatter_dimension=0, tiled=True).astype(F32)
    triple_grad = jnp.concatenate([query_grad, pair_grad.astype(BF16)], axis=1)
    grad_triple_weight = dot(normed_low, triple_grad, 0, 0)
    column_sums = jnp.sum(triple_grad.astype(F32), axis=0)
    grad_pair_bias = jnp.concatenate([column_sums[:width], column_sums[2 * width :]])
    normed_grad = dot(triple_grad, triple_weight, 1, 1)
    input_part, grad_gain_one, grad_shift_one = norm_one_pull(normed_grad)
    input_grad = middle_grad + input_part
    if moved:
        input_grad = regroup(input_grad, dp, moves)
    small_grads = [
        grad_gain_one, grad_shift_one, grad_pair_bias, grad_merge_bias,
        grad_gain_two, grad_shift_two, grad_expand_bias, grad_shrink_bias,
    ]
    lines = jnp.concatenate([piece.reshape(dp, -1) for piece in small_grads], axis=1).astype(BF16)
    lines = jnp.pad(lines[:, None], ((0, 0), (0, pad - 1), (0, width - lines.shape[1])))
    head_grads = jnp.concatenate(
        [grouped(piece) for piece in split_columns(grad_triple_weight, width)]
        + [grouped(grad_merge_weight), lines.reshape(GROUPS, -1, width)],
        axis=1,
    )
    head_own = sum_seq(scatter_pack(head_grads, head_sizes, dp), sequence_parts)

    piece_rows = chosen[4].shape[0]
    cut = lambda pack, at, size: pack[at : at + size]
    own_triple = jnp.concatenate([cut(head_own, at * piece_rows, piece_rows) for at in range(3)], axis=1)
    own_merge = cut(head_own, 3 * piece_rows, piece_rows)
    own_small, at = [], 0
    for size in widths:
        own_small.append(head_own[4 * piece_rows, at : at + size])
        at += size
    shrink_rows = chosen[10].shape[0]
    own_shrink = tail_own[:shrink_rows]
    own_expand = jnp.concatenate(
        [cut(tail_own, shrink_rows + at * piece_rows, piece_rows) for at in range(ff // width)], axis=1
    )
    own = [
        own_small[0], own_small[1], own_triple, own_small[2], own_merge, own_small[3],
        own_small[4], own_small[5], own_expand, own_small[6], own_shrink, own_small[7],
    ]
    shape = (length, count, width)
    return (output.reshape(shape), input_grad.reshape(shape)) + tuple(
        place(grad, master, tie_slots[number]) for number, (grad, master) in enumerate(zip(own, masters))
    )


def solution(mesh):
    in_specs = (
        P("seq", "dp", None),
        P("seq", "dp", None),
        P(),
        P(None, "dp"),
        P(None, "dp"),
        P(None, "dp", None),
        P(None, "dp"),
        P(None, "dp", None),
        P(None, "dp"),
        P(None, "dp"),
        P(None, "dp"),
        P(None, "dp", None),
        P(None, "dp"),
        P(None, "dp", None),
        P(None, "dp"),
    )
    out_specs = (
        P("seq", "dp", None),
        P("seq", "dp", None),
        P(None, "dp"),
        P(None, "dp"),
        P(None, "dp", None),
        P(None, "dp"),
        P(None, "dp", None),
        P(None, "dp"),
        P(None, "dp"),
        P(None, "dp"),
        P(None, "dp", None),
        P(None, "dp"),
        P(None, "dp", None),
        P(None, "dp"),
    )
    return jax.shard_map(
        per_device, mesh=mesh, in_specs=in_specs, out_specs=out_specs, check_vma=False
    )
```

time: 841 us -> 463 us (0.55)
  matrix products: 219 us -> 44.4 us
  blocking collectives: 128 us -> 0 us
  other arithmetic: 80.2 us -> 32.8 us
  loops' own time: 39.5 us -> 0 us
  local copies, waits for them, and re-layouts: 82.8 us -> 47.7 us
  Pallas kernels: 0 us -> 23.3 us
  waiting for transfers between devices: 240 us -> 256 us
  starting transfers between devices: 0.81 us -> 16.3 us
    dot_general x48 -> x12, matrix products: 219 us -> 44.4 us  [the longest x8 28.7 us: dot(): lax.dot_general(left, right, (((left_dim,), (right_dim,)), ((), ())), pre...]
    unnamed x2 -> x0, blocking collectives: 123 us -> none
    all_gather x5 -> x2, waiting for transfers between devices: 63.4 us -> 105 us  [gather_pack(): packed = lax.all_gather(jnp.concatenate(blocks, axis=0), 'dp', axis=0)]
    another operation x5 -> x0, loops' own time: 39.5 us -> none  [the longest x1 8.19 us: per_device(): lax.scan(output_step, jnp.zeros((local_len, seq_count, head_count, head_s...]
    psum x1 -> x0, waiting for transfers between devices: 29.6 us -> none  [reduce_grads(): lax.psum(parts[2].astype(jnp.bfloat16), 'seq').astype(jnp.float32)]
    pallas_call x0 -> x2, Pallas kernels: none -> 23.3 us  [the longest x1 12.6 us: attend(): pl.pallas_call(functools.partial(attend_kernel, block=block), grid_spec=p...]
    slice x24 -> x13, local copies, waits for them, and re-layouts: 35.8 us -> 13.2 us  [the longest x1 3.67 us: per_device(): pack[:, at * group_rows:(at + 1) * group_rows].reshape(width, width)]
    reduce_sum x7 -> x3, other arithmetic: 20.2 us -> 1.05 us  [the longest x1 0.45 us: per_device(): column_sums = jnp.sum(triple_grad.astype(F32), axis=0)]
  transfers between devices with their start and end apart: 11 -> 12, of which waited for: 5 -> 7; matrix products, arithmetic and copies ran while one was open for 28% -> 15% of each run, Pallas kernels for 0% -> 3%
where the time goes in v1:
time: 463 us; the launch traced here: 458 us
  waiting for transfers between devices  256 us (55%)
  local copies, waits for them, and re-layouts  47.7 us (10%)
  matrix products  44.4 us (10%)
  between operations  38.2 us (8%)
  other arithmetic  32.8 us (7%)
  Pallas kernels  23.3 us (5%)
  starting transfers between devices  16.3 us (4%)
    reduce_scatter x2, waiting for transfers between devices, scatter_pack(): return lax.psum_scatter(packed, 'dp', scatter_dimension=0)  134 us
    all_gather x2, waiting for transfers between devices, gather_pack(): packed = lax.all_gather(jnp.concatenate(blocks, axis=0), 'dp', axis=0)  105 us
    dot_general x8, matrix products, dot(): lax.dot_general(left, right, (((left_dim,), (right_dim,)), ((), ())), pre...  28.7 us
    unnamed x85, local copies, waits for them, and re-layouts  26.3 us
    ppermute x2, waiting for transfers between devices, swap_seq(): return lax.ppermute(value, 'seq', [(0, 1), (1, 0)])  15.3 us
    pallas_call x1, Pallas kernels, attend(): pl.pallas_call(functools.partial(attend_kernel, block=block), grid_spec=p...  12.6 us
    pallas_call x1, Pallas kernels, attend_back(): pl.pallas_call(functools.partial(attend_back_kernel, block=block), grid_s...  10.7 us
    ppermute x2, starting transfers between devices, swap_cores(): return lax.ppermute(value, 'dp', pairs_of(count, lambda index: index ^ 1))  9.38 us
  transfers between devices with their start and end apart: 12, of which 7 were waited for; matrix products, arithmetic and copies ran while one was open for 15% of the time, Pallas kernels for 3%

profile of v1, /device:TPU:0, one launch (start us, length us, event | category | flops | bytes accessed | tf_op | source)
XLA Modules:
  0.0 458.4 jit_solution(12975181712389707011)
XLA Ops:
  7.2 1.8 fusion.73
  42.1 50.8 %all-gather.5.cloned.1.call-done = bf16[3328,768]{1,0:T(8,128)(2,1)} async-done(((bf16[208,768]{1,0:T(8,128)(2,1)}), bf16[3328,768]{1,0:T(8,128)(2,1)}) %all-gather.5.cloned.1.call-update) | async-done | bytes 5111824 | tf_op jit(solution)/shard_map/all_gather | solution.py:283
  94.4 3.7 fusion.66
  98.0 2.2 fusion.7.q_ref.k_ref.v_ref
  104.0 1.8 collective-permute-done.1.rk_ref.rv_ref
  106.9 12.6 %attend.1 = (bf16[512,768]{1,0:T(8,128)(2,1)}, f32[6,2,512]{2,1,0:T(2,128)}) custom-call(s32[1]{0:T(128)} %bitcast.1.count, bf16[512,2304]{1,0:T(8,128)(2,1)} %copy-done.2, bf16[512,2304]{1,0:T(8,128)(2,1)} %copy-done.2, bf16[512,2304]{1,0:T(8,128)(2,1)} %copy-done.2, bf16[512,1536]{1,0:T(8,128)(2,1)} %copy-done.4, bf16[512,1536]{1,0:T(8,128)(2,1)} %copy-done.4), custom_call_target="tpu_custom_call" | custom-call | flops 1610612736 | bytes 4718592 | tf_op jit(solution)/shard_map/attend/pallas_call | solution.py:96
  119.5 2.0 fusion.74
  121.9 54.0 %all-gather.7.cloned.1.call-done = bf16[6144,768]{1,0:T(8,128)(2,1)} async-done(((bf16[384,768]{1,0:T(8,128)(2,1)}), bf16[6144,768]{1,0:T(8,128)(2,1)}) %all-gather.7.cloned.1.call-update) | async-done | bytes 9437200 | tf_op jit(solution)/shard_map/all_gather | solution.py:283
  175.9 2.9 slice.335
  178.8 2.2 copy-done.3
  181.4 2.7 fusion.24
  184.2 6.5 %fusion.60 = (bf16[3072]{0:T(1024)(128)(2,1)S(1)}, bf16[512,3072]{1,0:T(8,128)(2,1)S(1)}) fusion(f32[512,3072]{1,0:T(8,128)S(1)} %fusion.24, f32[3072]{0:T(1024)S(1)} %reshape.490, bf16[512,768]{1,0:T(8,128)(2,1)S(1)} %get-tuple-element.78, bf16[3072,768]{1,0:T(8,128)(2,1)S(1)} %bitcast.114), kind=kOutput, calls=%fused_computation.172 | convolution fusion | flops 2450519040 | bytes 14960640 | tf_op jit(solution)/shard_map/dot_general | solution.py:28
  190.7 2.9 multiply_reduce_fusion
  193.7 2.0 fusion.64
  198.7 10.7 %attend_back.1 = (bf16[512,768]{1,0:T(8,128)(2,1)}, f32[512,768]{1,0:T(8,128)}, f32[512,768]{1,0:T(8,128)}, bf16[512,768]{1,0:T(8,128)(2,1)}, bf16[512,768]{1,0:T(8,128)(2,1)}) custom-call(s32[1]{0:T(128)} %bitcast.1.count, bf16[512,2304]{1,0:T(8,128)(2,1)} %copy-done.2, bf16[512,2304]{1,0:T(8,128)(2,1)} %copy-done.2, bf16[512,2304]{1,0:T(8,128)(2,1)} %copy-done.2, ...), custom_call_target="tpu_custom_call" | custom-call | flops 4026531840 | bytes 11796480 | tf_op jit(solution)/shard_map/attend_back/pallas_call | solution.py:214
  209.4 2.6 pad_maximum_fusion.3
  212.0 9.1 %collective-permute-start.4 = (bf16[512,1536]{1,0:T(8,128)(2,1)}, bf16[512,1536]{1,0:T(8,128)(2,1)}, u32[]{:S(2)}, u32[]{:S(2)}) collective-permute-start(bf16[512,1536]{1,0:T(8,128)(2,1)} %pad_maximum_fusion.3), channel_id=1, source_target_pairs={{0,2},{2,0},{4,6},{6,4},{8,10},{10,8},{12,14},{14,12},{16,18},{18,... | collective-permute-start | bytes 4718600 | tf_op jit(solution)/shard_map/ppermute | solution.py:262
  221.6 3.4 convolution_convert_fusion.3
  225.0 1.9 fusion.8
  227.7 2.2 fusion.58
  229.8 2.2 convolution_convert_fusion.2
  236.6 2.5 constant_dynamic-update-slice_fusion.3
  243.0 6.4 %convolution_convert_fusion.1 = bf16[3072,768]{1,0:T(8,128)(2,1)S(1)} fusion(bf16[512,768]{1,0:T(8,128)(2,1)S(1)} %get-tuple-element.78, f32[512,3072]{1,0:T(8,128)} %copy-done.32, f32[3072]{0:T(1024)S(1)} %reshape.490), kind=kOutput, calls=%fused_computation.11 | convolution fusion | flops 2434007040 | bytes 11808768 | tf_op jit(solution)/shard_map/dot_general | solution.py:28
  249.5 2.9 constant_dynamic-update-slice_fusion.9
  253.8 3.4 convolution_convert_fusion
  264.8 3.4 add_add_fusion.2
  268.9 8.8 %add_convert_fusion = bf16[512,768]{1,0:T(8,128)(2,1)S(1)} fusion(f32[512,768]{1,0:T(8,128)S(1)} %copy-done.7, bf16[3072,768]{1,0:T(8,128)(2,1)} %bitcast.115, f32[768]{0:T(1024)S(1)} %reshape.491, f32[512,3072]{1,0:T(8,128)} %copy-done.32, f32[3072]{0:T(1024)S(1)} %reshape.490), kind=kOutput, calls=%fused_computation.43 | convolution fusion | flops 2432827392 | bytes 13384704 | tf_op jit(solution)/shard_map/dot_general | solution.py:393
  284.9 33.8 %reduce-scatter.3.cloned.1.call-done = bf16[1,208,768]{2,1,0:T(8,128)(2,1)} async-done(((bf16[16,208,768]{2,1,0:T(8,128)(2,1)}), bf16[1,208,768]{2,1,0:T(8,128)(2,1)}) %reduce-scatter.3.cloned.1.call-update) | async-done | bytes 319504 | tf_op jit(solution)/shard_map/reduce_scatter | solution.py:303
  322.0 2.8 copy.33
  324.8 2.6 collective-permute-done.6
  333.6 100.0 %reduce-scatter.5.cloned.1.call-done = bf16[1,384,768]{2,1,0:T(8,128)(2,1)} async-done(((bf16[16,384,768]{2,1,0:T(8,128)(2,1)}), bf16[1,384,768]{2,1,0:T(8,128)(2,1)}) %reduce-scatter.5.cloned.1.call-update) | async-done | bytes 589840 | tf_op jit(solution)/shard_map/reduce_scatter | solution.py:303
  436.0 12.7 %collective-permute-done.7 = bf16[384,768]{1,0:T(8,128)(2,1)S(1)} collective-permute-done((bf16[384,768]{1,0:T(8,128)(2,1)}, bf16[384,768]{1,0:T(8,128)(2,1)S(1)}, u32[]{:S(2)}, u32[]{:S(2)}) %collective-permute-start.7) | collective-permute-done | bytes 589856 | tf_op jit(solution)/shard_map/ppermute | solution.py:266
  (198 shorter events, 60.9 us)
Async XLA Ops:
  7.2 32.5 %copy-start = (f32[2,48,3072]{2,1,0:T(8,128)S(1)}, f32[2,48,3072]{2,1,0:T(8,128)}, u32[]{:S(2)}) copy-start(f32[2,48,3072]{2,1,0:T(8,128)} %param.26) | copy-start | bytes 3538948
  7.2 85.7 %all-gather.5.cloned.1.call-start = ((), (), s32[]{:S(2)}) async-start(), calls=%async_computation.4 | async-start | bytes 5431296 | tf_op jit(solution)/shard_map/all_gather | solution.py:283
  23.5 17.2 %copy-start.23 = (bf16[512,1,768]{2,0,1:T(8,128)(2,1)S(1)}, bf16[512,1,768]{2,0,1:T(8,128)(2,1)}, u32[]{:S(2)}) copy-start(bf16[512,1,768]{2,0,1:T(8,128)(2,1)} %param.15) | copy-start | bytes 2359300
  34.7 141.2 %all-gather.7.cloned.1.call-start = ((), (), s32[]{:S(2)}) async-start(), calls=%async_computation.5 | async-start | bytes 10027008 | tf_op jit(solution)/shard_map/all_gather | solution.py:283
  40.6 278.0 %reduce-scatter.3.cloned.1.call-start = ((), (), s32[]{:S(2)}) async-start(), calls=%async_computation.2 | async-start | bytes 5431296 | tf_op jit(solution)/shard_map/reduce_scatter | solution.py:303
  40.7 0.7 collective-permute-start
  102.1 3.6 collective-permute-start.1
  102.4 0.9 collective-permute-start.3
  106.9 12.6 %copy-start.20 = (bf16[16,48,768]{2,1,0:T(8,128)(2,1)S(1)}, bf16[16,48,768]{2,1,0:T(8,128)(2,1)}, u32[]{:S(2)}) copy-start(bf16[16,48,768]{2,1,0:T(8,128)(2,1)} %get-tuple-element.91) | copy-start | bytes 3538948
  121.5 69.2 %copy-start.5 = (f32[512,768]{1,0:T(8,128)}, f32[512,768]{1,0:T(8,128)S(1)}, u32[]{:S(2)}) copy-start(f32[512,768]{1,0:T(8,128)S(1)} %get-tuple-element.139) | copy-start | bytes 4718596
  175.9 5.1 %copy-start.3 = (bf16[6144,768]{1,0:T(8,128)(2,1)S(1)}, bf16[6144,768]{1,0:T(8,128)(2,1)}, u32[]{:S(2)}) copy-start(bf16[6144,768]{1,0:T(8,128)(2,1)} %all-gather.7.cloned.1.call-done) | copy-start | bytes 28311556
  181.0 3.2 copy-start.10
  184.1 6.6 %copy-start.32 = (f32[512,3072]{1,0:T(8,128)}, f32[512,3072]{1,0:T(8,128)S(1)}, u32[]{:S(2)}) copy-start(f32[512,3072]{1,0:T(8,128)S(1)} %fusion.24) | copy-start | bytes 18874372
  190.7 2.9 copy-start.30
  196.0 2.7 copy-start.26
  212.0 13.0 %collective-permute-start.4 = (bf16[512,1536]{1,0:T(8,128)(2,1)}, bf16[512,1536]{1,0:T(8,128)(2,1)}, u32[]{:S(2)}, u32[]{:S(2)}) collective-permute-start(bf16[512,1536]{1,0:T(8,128)(2,1)} %pad_maximum_fusion.3), channel_id=1, source_target_pairs={{0,2},{2,0},{4,6},{6,4},{8,10},{10,8},{12,14},{14,12},{16,18},{18,... | collective-permute-start | bytes 4718600 | tf_op jit(solution)/shard_map/ppermute | solution.py:262
  221.6 3.4 copy-start.11
  221.6 3.4 copy-start.12
  225.0 2.4 copy-start.19
  225.0 2.6 copy-start.25
  229.8 5.4 %copy-start.8 = (f32[512,768]{1,0:T(8,128)}, f32[512,768]{1,0:T(8,128)S(1)}, u32[]{:S(2)}) copy-start(f32[512,768]{1,0:T(8,128)S(1)} %get-tuple-element.141) | copy-start | bytes 4718596
  236.6 2.5 copy-start.9
  242.7 190.8 %reduce-scatter.5.cloned.1.call-start = ((), (), s32[]{:S(2)}) async-start(), calls=%async_computation.3 | async-start | bytes 10027008 | tf_op jit(solution)/shard_map/reduce_scatter | solution.py:303
  249.5 2.9 copy-start.6
  249.5 4.3 copy-start.31
  264.8 4.1 copy-start.7
  268.1 52.3 %collective-permute-start.5 = (f32[512,768]{1,0:T(8,128)}, f32[512,768]{1,0:T(8,128)S(1)}, u32[]{:S(2)}, u32[]{:S(2)}) collective-permute-start(f32[512,768]{1,0:T(8,128)} %add_add_fusion.2), channel_id=1, source_target_pairs={{2,1},{1,2},{6,5},{5,6},{10,9},{9,10},{14,13},{13,14},{18,17},{17,... | collective-permute-start | bytes 4718600 | tf_op jit(solution)/shard_map/ppermute | solution.py:274
  277.7 6.2 %collective-permute-start.2 = (bf16[512,768]{1,0:T(8,128)(2,1)S(1)}, bf16[512,768]{1,0:T(8,128)(2,1)S(1)}, u32[]{:S(2)}, u32[]{:S(2)}) collective-permute-start(bf16[512,768]{1,0:T(8,128)(2,1)S(1)} %add_convert_fusion), channel_id=1, source_target_pairs={{2,1},{1,2},{6,5},{5,6},{10,9},{9,10},{14,13},{13,14},{18,17},{17,... | collective-permute-start | bytes 2359304 | tf_op jit(solution)/shard_map/ppermute | solution.py:274
  318.7 8.6 %collective-permute-start.6 = (bf16[208,768]{1,0:T(8,128)(2,1)}, bf16[208,768]{1,0:T(8,128)(2,1)S(1)}, u32[]{:S(2)}, u32[]{:S(2)}) collective-permute-start(bf16[208,768]{1,0:T(8,128)(2,1)} %bitcast.139), channel_id=1, source_target_pairs={{0,1},{1,0},{2,3},{3,2},{4,5},{5,4},{6,7},{7,6},{8,9},{9,8},{10,11... | collective-permute-start | bytes 958472 | tf_op jit(solution)/shard_map/ppermute | solution.py:266
  322.0 5.3 %copy-start.29 = (bf16[1,208,768]{2,1,0:T(8,128)(2,1)S(1)}, bf16[1,208,768]{2,1,0:T(8,128)(2,1)}, u32[]{:S(2)}) copy-start(bf16[1,208,768]{2,1,0:T(8,128)(2,1)} %reduce-scatter.3.cloned.1.call-done) | copy-start | bytes 958468
  433.5 15.2 %copy-start.27 = (bf16[1,384,768]{2,1,0:T(8,128)(2,1)S(1)}, bf16[1,384,768]{2,1,0:T(8,128)(2,1)}, u32[]{:S(2)}) copy-start(bf16[1,384,768]{2,1,0:T(8,128)(2,1)} %reduce-scatter.5.cloned.1.call-done) | copy-start | bytes 1769476
  433.5 15.2 %collective-permute-start.7 = (bf16[384,768]{1,0:T(8,128)(2,1)}, bf16[384,768]{1,0:T(8,128)(2,1)S(1)}, u32[]{:S(2)}, u32[]{:S(2)}) collective-permute-start(bf16[384,768]{1,0:T(8,128)(2,1)} %bitcast.138), channel_id=1, source_target_pairs={{0,1},{1,0},{2,3},{3,2},{4,5},{5,4},{6,7},{7,6},{8,9},{9,8},{10,11... | collective-permute-start | bytes 1769480 | tf_op jit(solution)/shard_map/ppermute | solution.py:266
  (13 other events, 22.7 us)
Sparse Core Ops, SparseCore 0:
  34.8 58.0 all-gather.4
  95.8 80.0 all-gather.6
  242.9 75.7 reduce-scatter.2
  323.2 110.2 reduce-scatter.4

commit v2 on v1

--- a/solution.py
+++ b/solution.py
@@ -10,6 +10,7 @@
 
 H = 12
 GROUPS = 16
+SMALL = (0, 1, 3, 5, 6, 7, 9, 11)
 EPSILON = 1e-05
 NEGATIVE = -1e30
 F32 = jnp.float32
@@ -88,8 +89,8 @@
         lse_ref[0, 1:2, here] = top1 + jnp.log(total1)
 
 
-def attend(count, queries, triple, remote, block):
-    rows, width = queries.shape[0], triple.shape[1] // 3
+def attend(count, queries, near, remote, block):
+    rows, width = queries.shape
     pairs = width // 128
     far_rows = remote.shape[0]
     column = lambda size, offset: pl.BlockSpec((size, 128), lambda h, c: (0, h + offset))
@@ -100,8 +101,8 @@
             grid=(pairs,),
             in_specs=[
                 column(rows, 0),
+                column(rows, 0),
                 column(rows, pairs),
-                column(rows, 2 * pairs),
                 column(far_rows, 0),
                 column(far_rows, pairs),
             ],
@@ -116,7 +117,7 @@
             flops=8 * rows * rows * width, bytes_accessed=rows * width * 12, transcendentals=rows * rows * 12
         ),
         name="attend",
-    )(count, triple, triple, triple, remote, remote)
+    )(count, queries, near, near, remote, remote)
 
 
 def attend_back_kernel(
@@ -206,7 +207,7 @@
     dv_ref[...] = dv_sum[...]
 
 
-def attend_back(count, triple, remote, out_grad, attended, lse, block):
+def attend_back(count, queries, near, remote, out_grad, attended, lse, block):
     rows, width = attended.shape
     pairs = width // 128
     far_rows = remote.shape[0]
@@ -218,8 +219,8 @@
             grid=(pairs,),
             in_specs=[
                 column(rows, 0),
+                column(rows, 0),
                 column(rows, pairs),
-                column(rows, 2 * pairs),
                 column(far_rows, 0),
                 column(far_rows, pairs),
                 column(rows, 0),
@@ -251,7 +252,7 @@
             flops=20 * rows * rows * width, bytes_accessed=rows * width * 30, transcendentals=rows * rows * 12
         ),
         name="attend_back",
-    )(count, triple, triple, triple, remote, remote, out_grad, attended, lse)
+    )(count, queries, near, near, remote, remote, out_grad, attended, lse)
 
 
 def pairs_of(count, target):
@@ -312,6 +313,493 @@
 def place(grad, master, slot):
     marker = (jnp.arange(master.shape[0]) == slot).astype(F32)
     return marker.reshape((-1,) + (1,) * grad.ndim) * grad[None]
+
+
+def spot(place):
+    index = place[0]
+    return index >> 2, (index >> 1) & 1, index & 1, place[1]
+
+
+def whole(shape):
+    return pl.BlockSpec(shape, lambda *unused: (0,) * len(shape))
+
+
+ANYWHERE = pl.BlockSpec(memory_space=pl.ANY)
+
+
+def kernel_call(body, scalars, in_specs, args, out_specs, out_shape, scratch, name, flops, moved):
+    return pl.pallas_call(
+        body,
+        grid_spec=pltpu.PrefetchScalarGridSpec(
+            num_scalar_prefetch=len(scalars),
+            grid=(1,),
+            in_specs=in_specs,
+            out_specs=out_specs,
+            scratch_shapes=scratch,
+        ),
+        out_shape=out_shape,
+        compiler_params=pltpu.CompilerParams(vmem_limit_bytes=VMEM_LIMIT),
+        cost_estimate=pl.CostEstimate(flops=flops, bytes_accessed=moved, transcendentals=0),
+        name=name,
+    )(*scalars, *args)
+
+
+def pack_kernel(slots, place, *refs):
+    masters, (head, tail, lines) = refs[:12], refs[12:]
+    part, width = masters[4].shape
+    lines[...] = jnp.zeros_like(lines)
+    for row, number in enumerate(SMALL):
+        master = masters[number]
+        lines[row : row + 1, 0 : master.shape[1]] = master[pl.ds(slots[number], 1), :]
+    for at in range(3):
+        head[at * part : (at + 1) * part, :] = masters[2][:, at * width : (at + 1) * width].astype(BF16)
+    head[3 * part : 4 * part, :] = masters[4][...].astype(BF16)
+    head[4 * part :, :] = lines[...].astype(BF16)
+
+    @pl.when(place[1] == 0)
+    def shrink():
+        tail[...] = masters[10][...].astype(BF16)
+
+    @pl.when(place[1] != 0)
+    def expand():
+        for at in range(masters[8].shape[1] // width):
+            tail[at * part : (at + 1) * part, :] = masters[8][:, at * width : (at + 1) * width].astype(BF16)
+
+
+def pack(slots, place, masters):
+    specs = []
+    for number, master in enumerate(masters):
+        if master.ndim == 2:
+            specs.append(whole(master.shape))
+        else:
+            specs.append(
+                pl.BlockSpec(
+                    (None,) + master.shape[1:],
+                    functools.partial(lambda step, slots, place, number: (slots[number], 0, 0), number=number),
+                )
+            )
+    part, width = masters[4].shape[1:]
+    rows = 4 * part + 16
+    tail_rows = masters[10].shape[1]
+    return kernel_call(
+        pack_kernel, (slots, place), specs, masters,
+        [whole((rows, width)), whole((tail_rows, width))],
+        [jax.ShapeDtypeStruct((rows, width), BF16), jax.ShapeDtypeStruct((tail_rows, width), BF16)],
+        [pltpu.VMEM((16, width), F32)], "pack", 0, 4 * rows * width * 6,
+    )
+
+
+def shift_z(value):
+    return lax.ppermute(value, "dp", pairs_of(16, lambda index: (index + 4) % 16))
+
+
+def swap_x(value):
+    return lax.ppermute(value, "dp", pairs_of(16, lambda index: index ^ 2))
+
+
+def gather_ring(own):
+    pieces = []
+    for step in range(4):
+        if step:
+            own = shift_z(own)
+        pieces += [own, swap_x(own)]
+    return pieces
+
+
+def ring_slots(z, x):
+    slots = []
+    for step in range(4):
+        base = ((z - step) & 3) * 4
+        slots += [base + x * 2, base + (1 - x) * 2]
+    return slots
+
+
+def gather_head(own):
+    pieces = gather_ring(own)
+    return pieces + [swap_cores(piece, 16) for piece in pieces]
+
+
+def gather_tail(own):
+    pieces = gather_ring(own)
+    pieces = pieces + [swap_seq(piece) for piece in pieces]
+    return pieces + [swap_cores(piece, 16) for piece in pieces]
+
+
+def row_sum(value):
+    return jnp.sum(value, axis=0, keepdims=True)
+
+
+def normalise(values):
+    average = jnp.mean(values, axis=-1, keepdims=True)
+    centered = values - average
+    scale = lax.rsqrt(jnp.mean(centered * centered, axis=-1, keepdims=True) + EPSILON)
+    return centered * scale, scale
+
+
+def norm_back(grad, gain, shape, scale):
+    inner = grad * gain
+    first = jnp.mean(inner, axis=-1, keepdims=True)
+    second = jnp.mean(inner * shape, axis=-1, keepdims=True)
+    return scale * (inner - first - shape * second)
+
+
+def qkv_kernel(place, x_ref, *refs):
+    pieces, (packed, n1_ref, q_ref, kv_ref, v48, v96, v192, sems) = refs[:16], refs[16:]
+    z, x, core, half = spot(place)
+    slots = ring_slots(z, x)
+    slots = [slot + core for slot in slots] + [slot + 1 - core for slot in slots]
+    copies = [
+        pltpu.make_async_copy(piece, packed.at[slots[number]], sems.at[number])
+        for number, piece in enumerate(pieces)
+    ]
+    for copy in copies:
+        copy.start()
+    width = x_ref.shape[1]
+    part = width // GROUPS
+    shape, unused = normalise(x_ref[...].astype(F32))
+    for copy in copies:
+        copy.wait()
+    for group in range(GROUPS):
+        lines = packed[group, 4 * part : 4 * part + 16, :].astype(F32)[0:8]
+        for out in (v48, v96, v192):
+            size = out.shape[1] // GROUPS
+            out[:, group * size : (group + 1) * size] = lines[:, :size]
+    normed = (shape * v48[0:1, :] + v48[1:2, :]).astype(BF16)
+    n1_ref[...] = normed
+    for at in range(3):
+        weight = packed[:, at * part : (at + 1) * part, :].reshape(width, width)
+        result = dot(normed, weight, 1, 0)
+        if at == 0:
+            q_ref[...] = (result + v96[2:3, :width]).astype(BF16)
+        elif at == 1:
+            kv_ref[:, :width] = result.astype(BF16)
+        else:
+            kv_ref[:, width:] = (result + v96[2:3, width:]).astype(BF16)
+
+
+def qkv(place, values, pieces):
+    rows, width = values.shape
+    shapes = [
+        ((GROUPS,) + pieces[0].shape, BF16), ((rows, width), BF16), ((rows, width), BF16), ((rows, 2 * width), BF16),
+        ((8, width), F32), ((8, 2 * width), F32), ((8, 4 * width), F32),
+    ]
+    return kernel_call(
+        qkv_kernel, (place,), [whole(values.shape)] + [ANYWHERE] * 16, [values] + pieces,
+        [whole(shape) for shape, unused in shapes],
+        [jax.ShapeDtypeStruct(shape, dtype) for shape, dtype in shapes],
+        [pltpu.SemaphoreType.DMA((16,))], "qkv", 6 * rows * width * width, 20 * width * width,
+    )
+
+
+def merge_kernel(x_ref, o_ref, weight, v48, m_ref, n2_ref):
+    width = x_ref.shape[1]
+    middle = x_ref[...].astype(F32) + dot(o_ref[...], weight[...].reshape(width, width), 1, 0) + v48[3:4, :]
+    m_ref[...] = middle
+    shape, unused = normalise(middle)
+    n2_ref[...] = (shape * v48[4:5, :] + v48[5:6, :]).astype(BF16)
+
+
+def merge_spec(packed):
+    part = packed.shape[2] // GROUPS
+    return pl.BlockSpec((GROUPS, part, packed.shape[2]), lambda *unused: (0, 3, 0))
+
+
+def merge(values, attended, packed, v48):
+    rows, width = values.shape
+    return kernel_call(
+        merge_kernel, (), [whole(values.shape), whole(values.shape), merge_spec(packed), whole(v48.shape)],
+        [values, attended, packed, v48], [whole(values.shape)] * 2,
+        [jax.ShapeDtypeStruct((rows, width), F32), jax.ShapeDtypeStruct((rows, width), BF16)],
+        [], "merge", 2 * rows * width * width, 12 * rows * width,
+    )
+
+
+def gelu_pair(value):
+    scale, cubic = math.sqrt(2 / math.pi), 0.044715
+    square = value * value
+    bent = jnp.tanh(scale * value * (1.0 + cubic * square))
+    half = 0.5 * (1.0 + bent)
+    slope = half + 0.5 * value * (1.0 - bent * bent) * (scale * (1.0 + 3.0 * cubic * square))
+    return value * half, slope
+
+
+def ffn_kernel(place, *refs):
+    pieces, refs = refs[:32], refs[32:]
+    m_ref, n2_ref, gy_ref, merge_weight, v48, v192, out_ref, dm_ref, dz_ref, do_ref, g48, g192 = refs[:12]
+    outs, (weights, grads, y, dn2, n2_t, u, df, in_sems, out_sems) = refs[12:20], refs[20:]
+    z, x, core, half = spot(place)
+    slots = ring_slots(z, x)
+    spots = [(slot + core, half) for slot in slots] + [(slot + core, 1 - half) for slot in slots]
+    spots += [(slot + 1 - core, half) for slot in slots] + [(slot + 1 - core, 1 - half) for slot in slots]
+    copies = [
+        pltpu.make_async_copy(piece, weights.at[spots[number][0], spots[number][1]], in_sems.at[number])
+        for number, piece in enumerate(pieces)
+    ]
+    for copy in copies:
+        copy.start()
+    width = m_ref.shape[1]
+    part = width // GROUPS
+    n2_t[...] = jnp.transpose(n2_ref[...])
+    y[...] = jnp.zeros_like(y)
+    dn2[...] = jnp.zeros_like(dn2)
+    for copy in copies:
+        copy.wait()
+
+    def step(at, unused):
+        first = pl.multiple_of(at * 4, 4)
+        lines = pl.ds(pl.multiple_of(at * part, 16), part)
+        chunk = 256
+        for column in range(0, width, chunk):
+            place_in = pl.ds(pl.multiple_of(at * width + column, 128), chunk)
+            expand = weights[:, 1, lines, column : column + chunk].reshape(width, chunk)
+            hidden = dot(n2_ref[...], expand, 1, 0) + v192[6:7, place_in]
+            shrink = weights[pl.ds(first, 4), 0].reshape(width, width)[column : column + chunk]
+            active, slope = gelu_pair(hidden)
+            u[:, column : column + chunk] = active.astype(BF16)
+            hidden_grad = (dot(gy_ref[...], shrink, 1, 1) * slope).astype(BF16)
+            df[:, column : column + chunk] = hidden_grad
+            g192[0:1, place_in] = row_sum(hidden_grad.astype(F32))
+        shrink = weights[pl.ds(first, 4), 0].reshape(width, width)
+        expand = weights[:, 1, lines, :].reshape(width, width)
+        y[...] += dot(u[...], shrink, 1, 0)
+        dn2[...] += dot(df[...], expand, 1, 1)
+        grads[pl.ds(first, 4), 0] = dot(u[...], gy_ref[...], 0, 0).astype(BF16).reshape(4, 4 * part, width)
+        grads[:, 1, lines, :] = dot(n2_t[...], df[...], 1, 0).astype(BF16).reshape(GROUPS, part, width)
+        return unused
+
+    lax.fori_loop(0, 4, step, 0)
+    copies = []
+    for order in range(4):
+        base = ((z - order) & 3) * 4
+        for number, out in ((0, outs[2 * order]), (1, outs[2 * order + 1])):
+            side = core if number == 0 else 1 - core
+            for kind in range(2):
+                for column in range(2):
+                    source = base + (x if column == 0 else 1 - x) * 2 + side
+                    copies.append(
+                        pltpu.make_async_copy(
+                            grads.at[source, half if kind == 0 else 1 - half],
+                            out.at[kind, column],
+                            out_sems.at[len(copies)],
+                        )
+                    )
+    for copy in copies:
+        copy.start()
+    middle = m_ref[...]
+    out_ref[...] = (middle + y[...] + v48[7:8, :]).astype(BF16)
+    shape, scale = normalise(middle)
+    second_grad = dn2[...]
+    out_grad = gy_ref[...].astype(F32)
+    middle_grad = out_grad + norm_back(second_grad, v48[4:5, :], shape, scale)
+    dm_ref[...] = middle_grad
+    low = middle_grad.astype(BF16)
+    dz_ref[...] = low
+    g48[...] = jnp.zeros_like(g48)
+    g48[3:4, :] = row_sum(low.astype(F32))
+    g48[4:5, :] = row_sum(shape * second_grad)
+    g48[5:6, :] = row_sum(second_grad)
+    g48[7:8, :] = row_sum(out_grad)
+    do_ref[...] = dot(low, merge_weight[...].reshape(width, width), 1, 1).astype(BF16)
+    for copy in copies:
+        copy.wait()
+
+
+def ffn(place, pieces, middle, second, out_grad, packed, v48, v192):
+    rows, width = middle.shape
+    ff = 4 * width
+    tail_rows = pieces[0].shape[0]
+    shapes = [
+        ((rows, width), BF16), ((rows, width), F32), ((rows, width), BF16), ((rows, width), BF16),
+        ((8, width), F32), ((8, ff), F32),
+    ]
+    part = jax.ShapeDtypeStruct((2, 2, tail_rows, width), BF16)
+    pack_shape = (GROUPS, 2, tail_rows, width)
+    results = kernel_call(
+        ffn_kernel, (place,),
+        [ANYWHERE] * 32
+        + [whole(middle.shape), whole(second.shape), whole(out_grad.shape), merge_spec(packed), whole(v48.shape), whole(v192.shape)],
+        pieces + [middle, second, out_grad, packed, v48, v192],
+        [whole(shape) for shape, unused in shapes] + [ANYWHERE] * 8,
+        [jax.ShapeDtypeStruct(shape, dtype) for shape, dtype in shapes] + [part] * 8,
+        [
+            pltpu.VMEM(pack_shape, BF16), pltpu.VMEM(pack_shape, BF16),
+            pltpu.VMEM((rows, width), F32), pltpu.VMEM((rows, width), F32), pltpu.VMEM((width, rows), BF16),
+            pltpu.VMEM((rows, width), BF16), pltpu.VMEM((rows, width), BF16),
+            pltpu.SemaphoreType.DMA((32,)), pltpu.SemaphoreType.DMA((32,)),
+        ],
+        "ffn", 12 * rows * width * ff, 8 * width * ff,
+    )
+    return results[:6], results[6:]
+
+
+def close_kernel(
+    place, n1_ref, x_ref, q_ref, k_ref, v_ref, far_k, far_v, o_ref, dz_ref, dm_ref, packed, v48, g48_in, g192,
+    *refs,
+):
+    grad_ref, outs, (grads, g48, g96, dt, sems) = refs[0], refs[1:9], refs[9:]
+    z, x, core, half = spot(place)
+    width = x_ref.shape[1]
+    part = width // GROUPS
+    normed_t = jnp.transpose(n1_ref[...])
+    normed_grad = None
+    for at in range(3):
+        if at == 0:
+            dt[...] = q_ref[...]
+        else:
+            near, far = (k_ref, far_k) if at == 1 else (v_ref, far_v)
+            dt[...] = (near[...] + far[...].astype(F32)).astype(BF16)
+        if at != 1:
+            g96[2:3, (at // 2) * width : (at // 2 + 1) * width] = row_sum(dt[...].astype(F32))
+        weight = packed[:, at * part : (at + 1) * part, :].reshape(width, width)
+        term = dot(dt[...], weight, 1, 1)
+        normed_grad = term if normed_grad is None else normed_grad + term
+        grads[:, at * part : (at + 1) * part, :] = dot(normed_t, dt[...], 1, 0).astype(BF16).reshape(GROUPS, part, width)
+    grads[:, 3 * part : 4 * part, :] = dot(o_ref[...], dz_ref[...], 0, 0).astype(BF16).reshape(GROUPS, part, width)
+    shape, scale = normalise(x_ref[...].astype(F32))
+    g48[...] = g48_in[...]
+    g48[0:1, :] = row_sum(shape * normed_grad)
+    g48[1:2, :] = row_sum(normed_grad)
+    row = lax.broadcasted_iota(jnp.int32, (16, 1), 0)
+    for group in range(GROUPS):
+        lines = jnp.concatenate([g48[:, group * part : (group + 1) * part], jnp.zeros((8, part), F32)], axis=0)
+        grads[group, 4 * part :, :] = jnp.zeros((16, width), BF16)
+        pair = g96[2:3, group * 2 * part : (group + 1) * 2 * part]
+        wide = g192[0:1, group * 4 * part : (group + 1) * 4 * part]
+        spread = jnp.where(row == 6, wide, 0.0)
+        left = jnp.where(row == 2, pair, 0.0)
+        grads[group, 4 * part :, 0 : 4 * part] = spread.astype(BF16)
+        grads[group, 4 * part :, 0 : 2 * part] = (spread[:, : 2 * part] + left).astype(BF16)
+        keep = jnp.where((row == 2) | (row == 6), 0.0, lines) + spread[:, :part] + left[:, :part]
+        grads[group, 4 * part :, 0:part] = keep.astype(BF16)
+    copies = []
+    for order in range(4):
+        base = ((z - order) & 3) * 4
+        for number, out in ((0, outs[2 * order]), (1, outs[2 * order + 1])):
+            side = core if number == 0 else 1 - core
+            for column in range(2):
+                source = base + (x if column == 0 else 1 - x) * 2 + side
+                copies.append(pltpu.make_async_copy(grads.at[source], out.at[column], sems.at[len(copies)]))
+    for copy in copies:
+        copy.start()
+    grad_ref[...] = (dm_ref[...] + norm_back(normed_grad, v48[0:1, :], shape, scale)).astype(BF16)
+    for copy in copies:
+        copy.wait()
+
+
+def close(place, args):
+    rows, width = args[0].shape
+    packed = args[10]
+    head_rows = packed.shape[1]
+    part = jax.ShapeDtypeStruct((2, head_rows, width), BF16)
+    results = kernel_call(
+        close_kernel, (place,), [whole(arg.shape) for arg in args], args,
+        [whole((rows, width))] + [ANYWHERE] * 8,
+        [jax.ShapeDtypeStruct((rows, width), BF16)] + [part] * 8,
+        [
+            pltpu.VMEM(packed.shape, BF16), pltpu.VMEM((8, width), F32), pltpu.VMEM((8, 2 * width), F32),
+            pltpu.VMEM((rows, width), BF16), pltpu.SemaphoreType.DMA((16,)),
+        ],
+        "close", 14 * rows * width * width, 20 * width * width,
+    )
+    return results[0], results[1:]
+
+
+def scatter_head(parts):
+    moving = None
+    for order in (1, 2, 3, 0):
+        keep, send = parts[2 * order], parts[2 * order + 1]
+        came = swap_cores(send, 16)
+        value = keep[0] + came[0] + swap_x(keep[1] + came[1])
+        if moving is not None:
+            value = value + shift_z(moving)
+        moving = value
+    return moving
+
+
+def scatter_tail(parts):
+    moving = None
+    for order in (1, 2, 3, 0):
+        keep, send = parts[2 * order], parts[2 * order + 1]
+        came = swap_cores(send, 16)
+        other = swap_seq(keep[1] + came[1])
+        value = keep[0, 0] + came[0, 0] + other[0] + swap_x(keep[0, 1] + came[0, 1] + other[1])
+        if moving is not None:
+            value = value + shift_z(moving)
+        moving = value
+    return moving
+
+
+def unpack_kernel(slots, place, head, head_far, tail, tail_far, *outs):
+    part, width = outs[4].shape[1:]
+    total = head[...].astype(F32) + head_far[...].astype(F32)
+    near, far = tail[...].astype(F32), tail_far[...].astype(F32)
+    first = place[1] == 0
+    shrink = jnp.where(first, near, far)
+    expand = jnp.where(first, far, near)
+    for row, number in enumerate(SMALL):
+        out = outs[number]
+        size = out.shape[1]
+        line = total[4 * part + row : 4 * part + row + 1, :size]
+        row_at = lax.broadcasted_iota(jnp.int32, out.shape, 0)
+        out[...] = jnp.where(row_at == slots[number], line, 0.0)
+    for slot in range(outs[2].shape[0]):
+        chosen = lambda number, value: jnp.where(slots[number] == slot, value, 0.0)
+        for at in range(3):
+            outs[2][slot, :, at * width : (at + 1) * width] = chosen(2, total[at * part : (at + 1) * part])
+        outs[4][slot] = chosen(4, total[3 * part : 4 * part])
+        for at in range(outs[8].shape[2] // width):
+            outs[8][slot, :, at * width : (at + 1) * width] = chosen(8, expand[at * part : (at + 1) * part])
+        outs[10][slot] = chosen(10, shrink)
+
+
+def unpack(slots, place, parts, masters):
+    return kernel_call(
+        unpack_kernel, (slots, place), [whole(part.shape) for part in parts], parts,
+        [whole(master.shape) for master in masters],
+        [jax.ShapeDtypeStruct(master.shape, F32) for master in masters],
+        [], "unpack", 0, 8 * 1024 * 1024,
+    )
+
+
+def per_device_fast(inputs, cotangent, tie_slots, *masters):
+    length, count, width = inputs.shape
+    block = math.gcd(length, 256)
+    index, half = lax.axis_index("dp"), lax.axis_index("seq")
+    place = jnp.stack([index, half]).astype(jnp.int32)
+    core = index % 2
+    moves = core != half
+    head, tail = pack(tie_slots, place, masters)
+    head_pieces = gather_head(head)
+    tail_pieces = gather_tail(tail)
+    values = regroup(inputs.reshape(length, width), 16, moves)
+    out_grad = regroup(cotangent.reshape(length, width), 16, moves)
+    packed, normed, queries, near, v48, v96, v192 = qkv(place, values, head_pieces)
+    remote = swap_cores(near, 16)
+    far_count = core.astype(jnp.int32).reshape(1)
+    attended, lse = attend(far_count, queries, near, remote, block)
+    middle, second = merge(values, attended, packed, v48)
+    (output, middle_grad, branch_grad, attended_grad, g48, g192), tail_parts = ffn(
+        place, tail_pieces, middle, second, out_grad, packed, v48, v192
+    )
+    tail_sum = scatter_tail(tail_parts)
+    output = regroup(output, 16, moves)
+    query_grad, key_grad, value_grad, far_key, far_value = attend_back(
+        far_count, queries, near, remote, attended_grad, attended, lse, block
+    )
+    input_grad, head_parts = close(
+        place,
+        [
+            normed, values, query_grad, key_grad, value_grad, swap_cores(far_key, 16), swap_cores(far_value, 16),
+            attended, branch_grad, middle_grad, packed, v48, g48, g192,
+        ],
+    )
+    input_grad = regroup(input_grad, 16, moves).astype(F32)
+    head_sum = scatter_head(head_parts)
+    grads = unpack(
+        tie_slots, place, [head_sum, swap_seq(head_sum), tail_sum, swap_seq(tail_sum)], masters
+    )
+    shape = (length, count, width)
+    return (output.reshape(shape), input_grad.reshape(shape)) + tuple(grads)
 
 
 def per_device(
@@ -334,8 +822,8 @@
     ]
     part = width // dp
     ff = masters[10].shape[1] * dp
-    small = jnp.concatenate([chosen[number] for number in (0, 1, 3, 5, 6, 7, 9, 11)])
-    widths = [chosen[number].shape[0] for number in (0, 1, 3, 5, 6, 7, 9, 11)]
+    small = jnp.concatenate([chosen[number] for number in SMALL])
+    widths = [chosen[number].shape[0] for number in SMALL]
     pad = 16 * GROUPS // dp
     small = jnp.pad(small.reshape(1, -1), ((0, pad - 1), (0, width - small.shape[0])))
     head_blocks = split_columns(chosen[2], width) + [chosen[4], small]
@@ -367,13 +855,13 @@
     normed_low = normed.astype(BF16)
     bias_full = jnp.concatenate([pair_bias[:width], jnp.zeros((width,), F32), pair_bias[width:]])
     triple = (jnp.dot(normed_low, triple_weight, preferred_element_type=F32) + bias_full).astype(BF16)
-    near = triple[:, width:]
+    queries, near = triple[:, :width], triple[:, width:]
     if moved:
         remote = swap_cores(near, dp)
     else:
         remote = lax.all_gather(near, "seq", axis=0, tiled=True)
     far_count = place_index.astype(jnp.int32).reshape(1)
-    attended_low, lse = attend(far_count, triple, triple, remote, block)
+    attended_low, lse = attend(far_count, queries, near, remote, block)
     middle = flat_in + jnp.dot(attended_low, merge_weight, preferred_element_type=F32) + merge_bias
 
     ff_rows = ff // GROUPS
@@ -415,7 +903,7 @@
     grad_merge_bias = jnp.sum(branch_grad.astype(F32), axis=0)
     attended_grad = dot(branch_grad, merge_weight, 1, 1).astype(BF16)
     query_grad, key_grad, value_grad, far_key, far_value = attend_back(
-        far_count, triple, remote, attended_grad, attended_low, lse, block
+        far_count, queries, near, remote, attended_grad, attended_low, lse, block
     )
     far_grad = jnp.concatenate([far_key, far_value], axis=1)
     pair_grad = jnp.concatenate([key_grad, value_grad], axis=1)
@@ -502,6 +990,8 @@
         P(None, "dp", None),
         P(None, "dp"),
     )
+    sizes = dict(mesh.shape)
+    body = per_device_fast if (sizes["dp"], sizes["seq"]) == (16, 2) else per_device
     return jax.shard_map(
-        per_device, mesh=mesh, in_specs=in_specs, out_specs=out_specs, check_vma=False
-    )
+        body, mesh=mesh, in_specs=in_specs, out_specs=out_specs, check_vma=False
+    )

time: 463 us -> 341 us (0.74)
  waiting for transfers between devices: 256 us -> 173 us
  Pallas kernels: 23.3 us -> 88.1 us
  starting transfers between devices: 16.3 us -> 67.4 us
  matrix products: 44.4 us -> 0 us
  local copies, waits for them, and re-layouts: 47.7 us -> 6.5 us
  between operations: 38.2 us -> 1.45 us
  other arithmetic: 32.8 us -> 4.25 us
    reduce_scatter x2 -> x0, waiting for transfers between devices: 134 us -> none  [scatter_pack(): return lax.psum_scatter(packed, 'dp', scatter_dimension=0)]
    all_gather x2 -> x0, waiting for transfers between devices: 105 us -> none  [gather_pack(): packed = lax.all_gather(jnp.concatenate(blocks, axis=0), 'dp', axis=0)]
    ppermute x0 -> x28, waiting for transfers between devices: none -> 83.5 us  [the longest x12 62.4 us: shift_z(): lax.ppermute(value, 'dp', pairs_of(16, lambda index: (index + 4) % 16))]
    ppermute x2 -> x14, waiting for transfers between devices: 15.3 us -> 87.2 us  [swap_seq(): return lax.ppermute(value, 'seq', [(0, 1), (1, 0)])]
    pallas_call x0 -> x6, Pallas kernels: none -> 64.9 us  [kernel_call(): pl.pallas_call(body, grid_spec=pltpu.PrefetchScalarGridSpec(num_scalar_pr...]
    dot_general x12 -> x0, matrix products: 44.4 us -> none  [the longest x8 28.7 us: dot(): lax.dot_general(left, right, (((left_dim,), (right_dim,)), ((), ())), pre...]
    ppermute x0 -> x28, starting transfers between devices: none -> 22.3 us  [the longest x16 18.6 us: swap_x(): return lax.ppermute(value, 'dp', pairs_of(16, lambda index: index ^ 2))]
    unnamed x85 -> x105, local copies, waits for them, and re-layouts: 26.3 us -> 6.5 us
  transfers between devices with their start and end apart: 12 -> 81, of which waited for: 7 -> 32; matrix products, arithmetic and copies ran while one was open for 15% -> 2% of each run, Pallas kernels for 3% -> 12%
where the time goes in v2:
time: 341 us
  waiting for transfers between devices  173 us (51%)
  Pallas kernels  88.1 us (26%)
  starting transfers between devices  67.4 us (20%)
  local copies, waits for them, and re-layouts  6.5 us (2%)
  other arithmetic  4.25 us (1%)
    ppermute x14, waiting for transfers between devices, swap_seq(): return lax.ppermute(value, 'seq', [(0, 1), (1, 0)])  87.2 us
    pallas_call x6, Pallas kernels, kernel_call(): pl.pallas_call(body, grid_spec=pltpu.PrefetchScalarGridSpec(num_scalar_pr...  64.9 us
    ppermute x12, waiting for transfers between devices, shift_z(): lax.ppermute(value, 'dp', pairs_of(16, lambda index: (index + 4) % 16))  62.4 us
    ppermute x35, starting transfers between devices, swap_cores(): return lax.ppermute(value, 'dp', pairs_of(count, lambda index: index ^ 1))  28.1 us
    ppermute x16, waiting for transfers between devices, swap_x(): return lax.ppermute(value, 'dp', pairs_of(16, lambda index: index ^ 2))  21.1 us
    ppermute x16, starting transfers between devices, swap_x(): return lax.ppermute(value, 'dp', pairs_of(16, lambda index: index ^ 2))  18.6 us
    ppermute x14, starting transfers between devices, swap_seq(): return lax.ppermute(value, 'seq', [(0, 1), (1, 0)])  14.2 us
    pallas_call x1, Pallas kernels, attend(): pl.pallas_call(functools.partial(attend_kernel, block=block), grid_spec=p...  12.5 us
  transfers between devices with their start and end apart: 81, of which 32 were waited for; matrix products, arithmetic and copies ran while one was open for 2% of the time, Pallas kernels for 12%

profile of v2, /device:TPU:0, one launch (start us, length us, event | category | flops | bytes accessed | tf_op | source)
XLA Modules:
  0.0 340.8 jit_solution(13347943329641498361)
XLA Ops:
  1.3 3.3 pack.1
  4.5 3.0 collective-permute-start.7
  15.4 4.0 %collective-permute-done.1.refs_2_ = bf16[192,768]{1,0:T(8,128)(2,1)S(1)} collective-permute-done((bf16[192,768]{1,0:T(8,128)(2,1)}, bf16[192,768]{1,0:T(8,128)(2,1)S(1)}, u32[]{:S(2)}, u32[]{:S(2)}) %collective-permute-start.1) | collective-permute-done | bytes 294944 | tf_op jit(solution)/shard_map/ppermute | solution.py:393
  20.2 4.7 %collective-permute-done.33.refs_2_ = bf16[208,768]{1,0:T(8,128)(2,1)S(1)} collective-permute-done((bf16[208,768]{1,0:T(8,128)(2,1)}, bf16[208,768]{1,0:T(8,128)(2,1)S(1)}, u32[]{:S(2)}, u32[]{:S(2)}) %collective-permute-start.33) | collective-permute-done | bytes 319520 | tf_op jit(solution)/shard_map/ppermute | solution.py:393
  26.7 10.0 %collective-permute-done.35.refs_4_ = bf16[208,768]{1,0:T(8,128)(2,1)} collective-permute-done((bf16[208,768]{1,0:T(8,128)(2,1)S(1)}, bf16[208,768]{1,0:T(8,128)(2,1)}, u32[]{:S(2)}, u32[]{:S(2)}) %collective-permute-start.35) | collective-permute-done | bytes 319520 | tf_op jit(solution)/shard_map/ppermute | solution.py:393
  38.8 9.2 %collective-permute-done.37.refs_6_ = bf16[208,768]{1,0:T(8,128)(2,1)} collective-permute-done((bf16[208,768]{1,0:T(8,128)(2,1)}, bf16[208,768]{1,0:T(8,128)(2,1)}, u32[]{:S(2)}, u32[]{:S(2)}) %collective-permute-start.37) | collective-permute-done | bytes 319520 | tf_op jit(solution)/shard_map/ppermute | solution.py:393
  50.7 8.0 %collective-permute-done.38.refs_7_ = bf16[208,768]{1,0:T(8,128)(2,1)} collective-permute-done((bf16[208,768]{1,0:T(8,128)(2,1)}, bf16[208,768]{1,0:T(8,128)(2,1)}, u32[]{:S(2)}, u32[]{:S(2)}) %collective-permute-start.38) | collective-permute-done | bytes 319520 | tf_op jit(solution)/shard_map/ppermute | solution.py:397
  61.7 8.2 %qkv.1 = (bf16[16,208,768]{2,1,0:T(8,128)(2,1)}, bf16[512,768]{1,0:T(8,128)(2,1)}, bf16[512,768]{1,0:T(8,128)(2,1)}, bf16[512,1536]{1,0:T(8,128)(2,1)}, f32[8,76...) custom-call(s32[2]{0:T(128)} %pad_add_fusion.place, bf16[512,768]{1,0:T(8,128)(2,1)} %get-tuple-element.133.x_ref, ...), custom_call_target="tpu_custom_call" | custom-call | flops 1811939328 | bytes 11796480 | tf_op jit(solution)/shard_map/qkv/pallas_call | solution.py:331
  72.2 7.2 %collective-permute-done.9.refs_10_ = bf16[192,768]{1,0:T(8,128)(2,1)S(1)} collective-permute-done((bf16[192,768]{1,0:T(8,128)(2,1)S(1)}, bf16[192,768]{1,0:T(8,128)(2,1)S(1)}, u32[]{:S(2)}, u32[]{:S(2)}) %collective-permute-start.9) | collective-permute-done | bytes 294944 | tf_op jit(solution)/shard_map/ppermute | solution.py:267
  83.5 5.9 %collective-permute-done.8.refs_9_ = bf16[192,768]{1,0:T(8,128)(2,1)S(1)} collective-permute-done((bf16[192,768]{1,0:T(8,128)(2,1)S(1)}, bf16[192,768]{1,0:T(8,128)(2,1)S(1)}, u32[]{:S(2)}, u32[]{:S(2)}) %collective-permute-start.8) | collective-permute-done | bytes 294944 | tf_op jit(solution)/shard_map/ppermute | solution.py:267
  90.9 3.3 collective-permute-done.11.refs_12_
  94.7 3.1 collective-permute-done.5.refs_6_
  98.5 3.3 collective-permute-done.10.refs_11_
  105.4 3.1 collective-permute-done.6.refs_7_
  109.0 4.1 %collective-permute-done.13.refs_14_ = bf16[192,768]{1,0:T(8,128)(2,1)S(1)} collective-permute-done((bf16[192,768]{1,0:T(8,128)(2,1)S(1)}, bf16[192,768]{1,0:T(8,128)(2,1)S(1)}, u32[]{:S(2)}, u32[]{:S(2)}) %collective-permute-start.13) | collective-permute-done | bytes 294944 | tf_op jit(solution)/shard_map/ppermute | solution.py:267
  113.6 5.9 %collective-permute-done.12.refs_13_ = bf16[192,768]{1,0:T(8,128)(2,1)} collective-permute-done((bf16[192,768]{1,0:T(8,128)(2,1)S(1)}, bf16[192,768]{1,0:T(8,128)(2,1)}, u32[]{:S(2)}, u32[]{:S(2)}) %collective-permute-start.12) | collective-permute-done | bytes 294944 | tf_op jit(solution)/shard_map/ppermute | solution.py:267
  119.5 3.2 collective-permute-done.14.refs_15_
  123.9 12.5 %attend.1 = (bf16[512,768]{1,0:T(8,128)(2,1)}, f32[6,2,512]{2,1,0:T(2,128)}) custom-call(s32[1]{0:T(128)} %bitcast.3.count, bf16[512,768]{1,0:T(8,128)(2,1)} %get-tuple-element.68.q_ref, bf16[512,1536]{1,0:T(8,128)(2,1)} %get-tuple-element.69.k_ref.v_ref, bf16[512,1536]{1,0:T(8,128)(2,1)} %get-tuple-element.69.k_ref.v_ref, bf16[512,1536]{1,0:T(8,128)(2,1)} %copy-done, ...), custom_call_target="tpu_custom_call" | custom-call | flops 1610612736 | bytes 4718592 | tf_op jit(solution)/shard_map/attend/pallas_call | solution.py:97
  136.6 4.0 %merge.1 = (f32[512,768]{1,0:T(8,128)}, bf16[512,768]{1,0:T(8,128)(2,1)}) custom-call(bf16[512,768]{1,0:T(8,128)(2,1)} %get-tuple-element.133.x_ref, bf16[512,768]{1,0:T(8,128)(2,1)} %get-tuple-element.70.o_ref, bf16[16,208,768]{2,1,0:T(8,128)(2,1)} %get-tuple-element.71.weight.refs_35_.packed, f32[8,768]{1,0:T(8,128)} %get-tuple-element.72.v48.refs_36_), custom_call_target="tpu_custom_call" | custom-call | flops 603979776 | bytes 4718592 | tf_op jit(solution)/shard_map/merge/pallas_call | solution.py:331
  140.7 30.6 %ffn.1 = (bf16[512,768]{1,0:T(8,128)(2,1)}, f32[512,768]{1,0:T(8,128)}, bf16[512,768]{1,0:T(8,128)(2,1)}, bf16[512,768]{1,0:T(8,128)(2,1)}, f32[8,768]{1,0:T(8,1...) custom-call(s32[2]{0:T(128)} %pad_add_fusion.place, ...), custom_call_target="tpu_custom_call" | custom-call | flops 14495514624 | bytes 18874368 | tf_op jit(solution)/shard_map/ffn/pallas_call | solution.py:331
  171.3 10.8 %attend_back.1 = (bf16[512,768]{1,0:T(8,128)(2,1)}, f32[512,768]{1,0:T(8,128)}, f32[512,768]{1,0:T(8,128)}, bf16[512,768]{1,0:T(8,128)(2,1)}, bf16[512,768]{1,0:T(8,128)(2,1)}) custom-call(s32[1]{0:T(128)} %bitcast.3.count, bf16[512,768]{1,0:T(8,128)(2,1)} %get-tuple-element.68.q_ref, bf16[512,1536]{1,0:T(8,128)(2,1)} %get-tuple-element.69.k_ref.v_ref, ...), custom_call_target="tpu_custom_call" | custom-call | flops 4026531840 | bytes 11796480 | tf_op jit(solution)/shard_map/attend_back/pallas_call | solution.py:215
  182.1 21.3 %collective-permute-start.50 = (bf16[512,768]{1,0:T(8,128)(2,1)}, bf16[512,768]{1,0:T(8,128)(2,1)S(1)}, u32[]{:S(2)}, u32[]{:S(2)}) collective-permute-start(bf16[512,768]{1,0:T(8,128)(2,1)} %get-tuple-element.83), channel_id=1, source_target_pairs={{0,2},{2,0},{4,6},{6,4},{8,10},{10,8},{12,14},{14,12},{16,18},{18,... | collective-permute-start | bytes 2359304 | tf_op jit(solution)/shard_map/ppermute | solution.py:263
  207.5 14.8 %close.1 = (bf16[512,768]{1,0:T(8,128)(2,1)}, bf16[2,208,768]{2,1,0:T(8,128)(2,1)}, bf16[2,208,768]{2,1,0:T(8,128)(2,1)}, bf16[2,208,768]{2,1,0:T(8,128)(2,1)}, ...) custom-call(s32[2]{0:T(128)} %pad_add_fusion.place, ...), custom_call_target="tpu_custom_call" | custom-call | flops 4227858432 | bytes 11796480 | tf_op jit(solution)/shard_map/close/pallas_call | solution.py:331
  229.8 36.3 %collective-permute-done.75 = bf16[2,192,768]{2,1,0:T(8,128)(2,1)S(1)} collective-permute-done((bf16[2,192,768]{2,1,0:T(8,128)(2,1)S(1)}, bf16[2,192,768]{2,1,0:T(8,128)(2,1)S(1)}, u32[]{:S(2)}, u32[]{:S(2)}) %collective-permute-start.75) | collective-permute-done | bytes 589856 | tf_op jit(solution)/shard_map/ppermute | solution.py:267
  268.3 9.9 %collective-permute-done.72 = bf16[2,192,768]{2,1,0:T(8,128)(2,1)S(1)} collective-permute-done((bf16[2,192,768]{2,1,0:T(8,128)(2,1)S(1)}, bf16[2,192,768]{2,1,0:T(8,128)(2,1)S(1)}, u32[]{:S(2)}, u32[]{:S(2)}) %collective-permute-start.72) | collective-permute-done | bytes 589856 | tf_op jit(solution)/shard_map/ppermute | solution.py:267
  282.3 8.1 %collective-permute-done.61 = bf16[208,768]{1,0:T(8,128)(2,1)S(1)} collective-permute-done((bf16[208,768]{1,0:T(8,128)(2,1)S(1)}, bf16[208,768]{1,0:T(8,128)(2,1)S(1)}, u32[]{:S(2)}, u32[]{:S(2)}) %collective-permute-start.61) | collective-permute-done | bytes 319520 | tf_op jit(solution)/shard_map/ppermute | solution.py:393
  295.5 4.7 %collective-permute-done.56 = bf16[208,768]{1,0:T(8,128)(2,1)S(1)} collective-permute-done((bf16[208,768]{1,0:T(8,128)(2,1)S(1)}, bf16[208,768]{1,0:T(8,128)(2,1)S(1)}, u32[]{:S(2)}, u32[]{:S(2)}) %collective-permute-start.56) | collective-permute-done | bytes 319520 | tf_op jit(solution)/shard_map/ppermute | solution.py:397
  300.9 6.6 %collective-permute-done.62 = bf16[208,768]{1,0:T(8,128)(2,1)S(1)} collective-permute-done((bf16[208,768]{1,0:T(8,128)(2,1)S(1)}, bf16[208,768]{1,0:T(8,128)(2,1)S(1)}, u32[]{:S(2)}, u32[]{:S(2)}) %collective-permute-start.62) | collective-permute-done | bytes 319520 | tf_op jit(solution)/shard_map/ppermute | solution.py:393
  315.5 8.1 %collective-permute-done.63 = bf16[208,768]{1,0:T(8,128)(2,1)S(1)} collective-permute-done((bf16[208,768]{1,0:T(8,128)(2,1)S(1)}, bf16[208,768]{1,0:T(8,128)(2,1)S(1)}, u32[]{:S(2)}, u32[]{:S(2)}) %collective-permute-start.63) | collective-permute-done | bytes 319520 | tf_op jit(solution)/shard_map/ppermute | solution.py:393
  327.6 2.8 copy.29
  332.9 3.2 collective-permute-done.80.tail_far
  336.8 4.0 %unpack.1 = (f32[2,48]{1,0:T(2,128)}, f32[2,48]{1,0:T(2,128)}, f32[2,48,2304]{2,1,0:T(8,128)}, f32[2,96]{1,0:T(2,128)}, f32[2,48,768]{2,1,0:T(8,128)}, /*index=5...) custom-call(s32[12]{0:T(128)} %slots.3, ...), custom_call_target="tpu_custom_call" | custom-call | bytes 8388608 | tf_op jit(solution)/shard_map/unpack/pallas_call | solution.py:331
  (267 shorter events, 72.3 us)
Async XLA Ops:
  9.1 15.8 %collective-permute-start.33 = (bf16[208,768]{1,0:T(8,128)(2,1)}, bf16[208,768]{1,0:T(8,128)(2,1)S(1)}, u32[]{:S(2)}, u32[]{:S(2)}) collective-permute-start(bf16[208,768]{1,0:T(8,128)(2,1)} %get-tuple-element.67.refs_0_), channel_id=1, source_target_pairs={{0,8},{2,10},{4,12},{6,14},{8,16},{10,18},{12,20},{14,22},{16,24},... | collective-permute-start | bytes 958472 | tf_op jit(solution)/shard_map/ppermute | solution.py:393
  10.6 14.3 %collective-permute-start.39 = (bf16[208,768]{1,0:T(8,128)(2,1)}, bf16[208,768]{1,0:T(8,128)(2,1)S(1)}, u32[]{:S(2)}, u32[]{:S(2)}) collective-permute-start(bf16[208,768]{1,0:T(8,128)(2,1)} %get-tuple-element.67.refs_0_), channel_id=1, source_target_pairs={{0,2},{2,0},{4,6},{6,4},{8,10},{10,8},{12,14},{14,12},{16,18},{18,... | collective-permute-start | bytes 958472 | tf_op jit(solution)/shard_map/ppermute | solution.py:263
  10.6 14.4 %collective-permute-start.32 = (bf16[208,768]{1,0:T(8,128)(2,1)}, bf16[208,768]{1,0:T(8,128)(2,1)S(1)}, u32[]{:S(2)}, u32[]{:S(2)}) collective-permute-start(bf16[208,768]{1,0:T(8,128)(2,1)} %get-tuple-element.67.refs_0_), channel_id=1, source_target_pairs={{0,4},{2,6},{4,0},{6,2},{8,12},{10,14},{12,8},{14,10},{16,20},{18,... | collective-permute-start | bytes 958472 | tf_op jit(solution)/shard_map/ppermute | solution.py:397
  14.7 23.6 %collective-permute-start.48 = (bf16[512,768]{1,0:T(8,128)(2,1)S(1)}, bf16[512,768]{1,0:T(8,128)(2,1)S(1)}, u32[]{:S(2)}, u32[]{:S(2)}) collective-permute-start(bf16[512,768]{1,0:T(8,128)(2,1)S(1)} %bitcast.128), channel_id=1, source_target_pairs={{2,1},{1,2},{6,5},{5,6},{10,9},{9,10},{14,13},{13,14},{18,17},{17,... | collective-permute-start | bytes 2359304 | tf_op jit(solution)/shard_map/ppermute | solution.py:275
  19.4 28.6 %collective-permute-start.31 = (bf16[512,768]{1,0:T(8,128)(2,1)S(1)}, bf16[512,768]{1,0:T(8,128)(2,1)S(1)}, u32[]{:S(2)}, u32[]{:S(2)}) collective-permute-start(bf16[512,768]{1,0:T(8,128)(2,1)S(1)} %bitcast.129), channel_id=1, source_target_pairs={{2,1},{1,2},{6,5},{5,6},{10,9},{9,10},{14,13},{13,14},{18,17},{17,... | collective-permute-start | bytes 2359304 | tf_op jit(solution)/shard_map/ppermute | solution.py:275
  49.8 20.3 %collective-permute-start.15 = (bf16[192,768]{1,0:T(8,128)(2,1)}, bf16[192,768]{1,0:T(8,128)(2,1)S(1)}, u32[]{:S(2)}, u32[]{:S(2)}) collective-permute-start(bf16[192,768]{1,0:T(8,128)(2,1)} %get-tuple-element.66.refs_0_), channel_id=1, source_target_pairs={{0,2},{2,0},{4,6},{6,4},{8,10},{10,8},{12,14},{14,12},{16,18},{18,... | collective-permute-start | bytes 884744 | tf_op jit(solution)/shard_map/ppermute | solution.py:263
  50.2 20.5 %collective-permute-start = (bf16[192,768]{1,0:T(8,128)(2,1)}, bf16[192,768]{1,0:T(8,128)(2,1)S(1)}, u32[]{:S(2)}, u32[]{:S(2)}) collective-permute-start(bf16[192,768]{1,0:T(8,128)(2,1)} %get-tuple-element.66.refs_0_), channel_id=1, source_target_pairs={{0,4},{2,6},{4,0},{6,2},{8,12},{10,14},{12,8},{14,10},{16,20},{18,... | collective-permute-start | bytes 884744 | tf_op jit(solution)/shard_map/ppermute | solution.py:397
  50.7 20.0 %collective-permute-start.23 = (bf16[192,768]{1,0:T(8,128)(2,1)}, bf16[192,768]{1,0:T(8,128)(2,1)S(1)}, u32[]{:S(2)}, u32[]{:S(2)}) collective-permute-start(bf16[192,768]{1,0:T(8,128)(2,1)} %copy-done.27), channel_id=1, source_target_pairs={{0,2},{2,0},{4,6},{6,4},{8,10},{10,8},{12,14},{14,12},{16,18},{18,... | collective-permute-start | bytes 884744 | tf_op jit(solution)/shard_map/ppermute | solution.py:263
  69.8 52.9 %collective-permute-start.47 = (bf16[512,1536]{1,0:T(8,128)(2,1)}, bf16[512,1536]{1,0:T(8,128)(2,1)S(1)}, u32[]{:S(2)}, u32[]{:S(2)}) collective-permute-start(bf16[512,1536]{1,0:T(8,128)(2,1)} %get-tuple-element.69.k_ref.v_ref), channel_id=1, source_target_pairs={{0,2},{2,0},{4,6},{6,4},{8,10},{10,8},{12,14},{14,12},{16,18},{18,... | collective-permute-start | bytes 4718600 | tf_op jit(solution)/shard_map/ppermute | solution.py:263
  103.8 15.7 %collective-permute-start.12 = (bf16[192,768]{1,0:T(8,128)(2,1)S(1)}, bf16[192,768]{1,0:T(8,128)(2,1)}, u32[]{:S(2)}, u32[]{:S(2)}) collective-permute-start(bf16[192,768]{1,0:T(8,128)(2,1)S(1)} %collective-permute-done.4.refs_5_), channel_id=1, source_target_pairs={{0,1},{1,0},{2,3},{3,2},{4,5},{5,4},{6,7},{7,6},{8,9},{9,8},{10,11... | collective-permute-start | bytes 884744 | tf_op jit(solution)/shard_map/ppermute | solution.py:267
  113.1 27.6 %collective-permute-start.26 = (bf16[192,768]{1,0:T(8,128)(2,1)S(1)}, bf16[192,768]{1,0:T(8,128)(2,1)}, u32[]{:S(2)}, u32[]{:S(2)}) collective-permute-start(bf16[192,768]{1,0:T(8,128)(2,1)S(1)} %collective-permute-done.10.refs_11_), channel_id=1, source_target_pairs={{0,2},{2,0},{4,6},{6,4},{8,10},{10,8},{12,14},{14,12},{16,18},{18,... | collective-permute-start | bytes 884744 | tf_op jit(solution)/shard_map/ppermute | solution.py:263
  113.1 27.5 %collective-permute-start.22 = (bf16[192,768]{1,0:T(8,128)(2,1)S(1)}, bf16[192,768]{1,0:T(8,128)(2,1)}, u32[]{:S(2)}, u32[]{:S(2)}) collective-permute-start(bf16[192,768]{1,0:T(8,128)(2,1)S(1)} %collective-permute-done.6.refs_7_), channel_id=1, source_target_pairs={{0,2},{2,0},{4,6},{6,4},{8,10},{10,8},{12,14},{14,12},{16,18},{18,... | collective-permute-start | bytes 884744 | tf_op jit(solution)/shard_map/ppermute | solution.py:263
  119.5 21.1 %collective-permute-start.29 = (bf16[192,768]{1,0:T(8,128)(2,1)S(1)}, bf16[192,768]{1,0:T(8,128)(2,1)}, u32[]{:S(2)}, u32[]{:S(2)}) collective-permute-start(bf16[192,768]{1,0:T(8,128)(2,1)S(1)} %collective-permute-done.13.refs_14_), channel_id=1, source_target_pairs={{0,2},{2,0},{4,6},{6,4},{8,10},{10,8},{12,14},{14,12},{16,18},{18,... | collective-permute-start | bytes 884744 | tf_op jit(solution)/shard_map/ppermute | solution.py:263
  122.7 17.9 %collective-permute-start.28 = (bf16[192,768]{1,0:T(8,128)(2,1)}, bf16[192,768]{1,0:T(8,128)(2,1)}, u32[]{:S(2)}, u32[]{:S(2)}) collective-permute-start(bf16[192,768]{1,0:T(8,128)(2,1)} %collective-permute-done.12.refs_13_), channel_id=1, source_target_pairs={{0,2},{2,0},{4,6},{6,4},{8,10},{10,8},{12,14},{14,12},{16,18},{18,... | collective-permute-start | bytes 884744 | tf_op jit(solution)/shard_map/ppermute | solution.py:263
  122.8 17.9 %collective-permute-start.30 = (bf16[192,768]{1,0:T(8,128)(2,1)}, bf16[192,768]{1,0:T(8,128)(2,1)}, u32[]{:S(2)}, u32[]{:S(2)}) collective-permute-start(bf16[192,768]{1,0:T(8,128)(2,1)} %collective-permute-done.14.refs_15_), channel_id=1, source_target_pairs={{0,2},{2,0},{4,6},{6,4},{8,10},{10,8},{12,14},{14,12},{16,18},{18,... | collective-permute-start | bytes 884744 | tf_op jit(solution)/shard_map/ppermute | solution.py:263
  182.1 23.4 %collective-permute-start.50 = (bf16[512,768]{1,0:T(8,128)(2,1)}, bf16[512,768]{1,0:T(8,128)(2,1)S(1)}, u32[]{:S(2)}, u32[]{:S(2)}) collective-permute-start(bf16[512,768]{1,0:T(8,128)(2,1)} %get-tuple-element.83), channel_id=1, source_target_pairs={{0,2},{2,0},{4,6},{6,4},{8,10},{10,8},{12,14},{14,12},{16,18},{18,... | collective-permute-start | bytes 2359304 | tf_op jit(solution)/shard_map/ppermute | solution.py:263
  203.4 19.3 %collective-permute-start.65 = (bf16[2,2,192,768]{3,2,1,0:T(8,128)(2,1)}, bf16[2,2,192,768]{3,2,1,0:T(8,128)(2,1)S(1)}, u32[]{:S(2)}, u32[]{:S(2)}) collective-permute-start(bf16[2,2,192,768]{3,2,1,0:T(8,128)(2,1)} %get-tuple-element.99), channel_id=1, source_target_pairs={{0,2},{2,0},{4,6},{6,4},{8,10},{10,8},{12,14},{14,12},{16,18},{18,... | collective-permute-start | bytes 3538952 | tf_op jit(solution)/shard_map/ppermute | solution.py:263
  203.9 19.1 %collective-permute-start.68 = (bf16[2,2,192,768]{3,2,1,0:T(8,128)(2,1)}, bf16[2,2,192,768]{3,2,1,0:T(8,128)(2,1)S(1)}, u32[]{:S(2)}, u32[]{:S(2)}) collective-permute-start(bf16[2,2,192,768]{3,2,1,0:T(8,128)(2,1)} %get-tuple-element.101), channel_id=1, source_target_pairs={{0,2},{2,0},{4,6},{6,4},{8,10},{10,8},{12,14},{14,12},{16,18},{18,... | collective-permute-start | bytes 3538952 | tf_op jit(solution)/shard_map/ppermute | solution.py:263
  203.9 19.7 %collective-permute-start.71 = (bf16[2,2,192,768]{3,2,1,0:T(8,128)(2,1)}, bf16[2,2,192,768]{3,2,1,0:T(8,128)(2,1)S(1)}, u32[]{:S(2)}, u32[]{:S(2)}) collective-permute-start(bf16[2,2,192,768]{3,2,1,0:T(8,128)(2,1)} %get-tuple-element.103), channel_id=1, source_target_pairs={{0,2},{2,0},{4,6},{6,4},{8,10},{10,8},{12,14},{14,12},{16,18},{18,... | collective-permute-start | bytes 3538952 | tf_op jit(solution)/shard_map/ppermute | solution.py:263
  205.5 19.1 %collective-permute-start.74 = (bf16[2,2,192,768]{3,2,1,0:T(8,128)(2,1)S(1)}, bf16[2,2,192,768]{3,2,1,0:T(8,128)(2,1)S(1)}, u32[]{:S(2)}, u32[]{:S(2)}) collective-permute-start(bf16[2,2,192,768]{3,2,1,0:T(8,128)(2,1)S(1)} %copy-done.17), channel_id=1, source_target_pairs={{0,2},{2,0},{4,6},{6,4},{8,10},{10,8},{12,14},{14,12},{16,18},{18,... | collective-permute-start | bytes 3538952 | tf_op jit(solution)/shard_map/ppermute | solution.py:263
  224.5 70.8 %collective-permute-start.66 = (bf16[2,192,768]{2,1,0:T(8,128)(2,1)S(1)}, bf16[2,192,768]{2,1,0:T(8,128)(2,1)S(1)}, u32[]{:S(2)}, u32[]{:S(2)}) collective-permute-start(bf16[2,192,768]{2,1,0:T(8,128)(2,1)S(1)} %fusion.3), channel_id=1, source_target_pairs={{0,1},{1,0},{2,3},{3,2},{4,5},{5,4},{6,7},{7,6},{8,9},{9,8},{10,11... | collective-permute-start | bytes 1769480 | tf_op jit(solution)/shard_map/ppermute | solution.py:267
  225.2 56.2 %collective-permute-start.69 = (bf16[2,192,768]{2,1,0:T(8,128)(2,1)S(1)}, bf16[2,192,768]{2,1,0:T(8,128)(2,1)S(1)}, u32[]{:S(2)}, u32[]{:S(2)}) collective-permute-start(bf16[2,192,768]{2,1,0:T(8,128)(2,1)S(1)} %fusion.2), channel_id=1, source_target_pairs={{0,1},{1,0},{2,3},{3,2},{4,5},{5,4},{6,7},{7,6},{8,9},{9,8},{10,11... | collective-permute-start | bytes 1769480 | tf_op jit(solution)/shard_map/ppermute | solution.py:267
  226.9 39.2 %collective-permute-start.75 = (bf16[2,192,768]{2,1,0:T(8,128)(2,1)S(1)}, bf16[2,192,768]{2,1,0:T(8,128)(2,1)S(1)}, u32[]{:S(2)}, u32[]{:S(2)}) collective-permute-start(bf16[2,192,768]{2,1,0:T(8,128)(2,1)S(1)} %fusion), channel_id=1, source_target_pairs={{0,1},{1,0},{2,3},{3,2},{4,5},{5,4},{6,7},{7,6},{8,9},{9,8},{10,11... | collective-permute-start | bytes 1769480 | tf_op jit(solution)/shard_map/ppermute | solution.py:267
  227.5 50.6 %collective-permute-start.72 = (bf16[2,192,768]{2,1,0:T(8,128)(2,1)S(1)}, bf16[2,192,768]{2,1,0:T(8,128)(2,1)S(1)}, u32[]{:S(2)}, u32[]{:S(2)}) collective-permute-start(bf16[2,192,768]{2,1,0:T(8,128)(2,1)S(1)} %fusion.1), channel_id=1, source_target_pairs={{0,1},{1,0},{2,3},{3,2},{4,5},{5,4},{6,7},{7,6},{8,9},{9,8},{10,11... | collective-permute-start | bytes 1769480 | tf_op jit(solution)/shard_map/ppermute | solution.py:267
  229.1 37.5 %collective-permute-start.60 = (bf16[208,768]{1,0:T(8,128)(2,1)S(1)}, bf16[208,768]{1,0:T(8,128)(2,1)S(1)}, u32[]{:S(2)}, u32[]{:S(2)}) collective-permute-start(bf16[208,768]{1,0:T(8,128)(2,1)S(1)} %fusion.4), channel_id=1, source_target_pairs={{0,4},{2,6},{4,0},{6,2},{8,12},{10,14},{12,8},{14,10},{16,20},{18,... | collective-permute-start | bytes 958472 | tf_op jit(solution)/shard_map/ppermute | solution.py:397
  266.0 15.5 %collective-permute-start.58 = (bf16[208,768]{1,0:T(8,128)(2,1)S(1)}, bf16[208,768]{1,0:T(8,128)(2,1)S(1)}, u32[]{:S(2)}, u32[]{:S(2)}) collective-permute-start(bf16[208,768]{1,0:T(8,128)(2,1)S(1)} %fusion.7), channel_id=1, source_target_pairs={{0,4},{2,6},{4,0},{6,2},{8,12},{10,14},{12,8},{14,10},{16,20},{18,... | collective-permute-start | bytes 958472 | tf_op jit(solution)/shard_map/ppermute | solution.py:397
  281.6 30.0 %collective-permute-start.49 = (bf16[512,768]{1,0:T(8,128)(2,1)S(1)}, bf16[512,768]{1,0:T(8,128)(2,1)S(1)}, u32[]{:S(2)}, u32[]{:S(2)}) collective-permute-start(bf16[512,768]{1,0:T(8,128)(2,1)S(1)} %copy-done.9), channel_id=1, source_target_pairs={{2,1},{1,2},{6,5},{5,6},{10,9},{9,10},{14,13},{13,14},{18,17},{17,... | collective-permute-start | bytes 2359304 | tf_op jit(solution)/shard_map/ppermute | solution.py:275
  291.1 17.4 %collective-permute-start.70 = (bf16[192,768]{1,0:T(8,128)(2,1)S(1)}, bf16[192,768]{1,0:T(8,128)(2,1)S(1)}, u32[]{:S(2)}, u32[]{:S(2)}) collective-permute-start(bf16[192,768]{1,0:T(8,128)(2,1)S(1)} %fusion.30), channel_id=1, source_target_pairs={{0,4},{2,6},{4,0},{6,2},{8,12},{10,14},{12,8},{14,10},{16,20},{18,... | collective-permute-start | bytes 884744 | tf_op jit(solution)/shard_map/ppermute | solution.py:397
  295.4 16.1 %collective-permute-start.78 = (bf16[192,768]{1,0:T(8,128)(2,1)S(1)}, bf16[192,768]{1,0:T(8,128)(2,1)S(1)}, u32[]{:S(2)}, u32[]{:S(2)}) collective-permute-start(bf16[192,768]{1,0:T(8,128)(2,1)S(1)} %fusion.28), channel_id=1, source_target_pairs={{0,8},{2,10},{4,12},{6,14},{8,16},{10,18},{12,20},{14,22},{16,24},... | collective-permute-start | bytes 884744 | tf_op jit(solution)/shard_map/ppermute | solution.py:393
  300.2 27.2 %collective-permute-start.52 = (bf16[512,768]{1,0:T(8,128)(2,1)S(1)}, bf16[512,768]{1,0:T(8,128)(2,1)S(1)}, u32[]{:S(2)}, u32[]{:S(2)}) collective-permute-start(bf16[512,768]{1,0:T(8,128)(2,1)S(1)} %copy-done.10), channel_id=1, source_target_pairs={{2,1},{1,2},{6,5},{5,6},{10,9},{9,10},{14,13},{13,14},{18,17},{17,... | collective-permute-start | bytes 2359304 | tf_op jit(solution)/shard_map/ppermute | solution.py:275
  308.5 15.8 %collective-permute-start.67 = (bf16[192,768]{1,0:T(8,128)(2,1)S(1)}, bf16[192,768]{1,0:T(8,128)(2,1)S(1)}, u32[]{:S(2)}, u32[]{:S(2)}) collective-permute-start(bf16[192,768]{1,0:T(8,128)(2,1)S(1)} %fusion.36), channel_id=1, source_target_pairs={{0,4},{2,6},{4,0},{6,2},{8,12},{10,14},{12,8},{14,10},{16,20},{18,... | collective-permute-start | bytes 884744 | tf_op jit(solution)/shard_map/ppermute | solution.py:397
  311.6 15.2 %collective-permute-start.79 = (bf16[192,768]{1,0:T(8,128)(2,1)S(1)}, bf16[192,768]{1,0:T(8,128)(2,1)S(1)}, u32[]{:S(2)}, u32[]{:S(2)}) collective-permute-start(bf16[192,768]{1,0:T(8,128)(2,1)S(1)} %fusion.34), channel_id=1, source_target_pairs={{0,8},{2,10},{4,12},{6,14},{8,16},{10,18},{12,20},{14,22},{16,24},... | collective-permute-start | bytes 884744 | tf_op jit(solution)/shard_map/ppermute | solution.py:393
  (101 other events, 1690.8 us)

commit v3 on v2

--- a/solution.py
+++ b/solution.py
@@ -15,7 +15,8 @@
 NEGATIVE = -1e30
 F32 = jnp.float32
 BF16 = jnp.bfloat16
-VMEM_LIMIT = 56 * 1024 * 1024
+MEGA = 1024 * 1024
+VMEM = {"pack": 60, "qkv": 28, "merge": 14, "ffn": 52, "close": 40, "unpack": 36}
 
 
 def layer_norm(values, gain, shift):
@@ -89,9 +90,10 @@
         lse_ref[0, 1:2, here] = top1 + jnp.log(total1)
 
 
-def attend(count, queries, near, remote, block):
+def attend(count, queries, near, remote, block, first=0, pairs=None):
     rows, width = queries.shape
-    pairs = width // 128
+    total = width // 128
+    pairs = pairs or total
     far_rows = remote.shape[0]
     column = lambda size, offset: pl.BlockSpec((size, 128), lambda h, c: (0, h + offset))
     return pl.pallas_call(
@@ -100,21 +102,21 @@
             num_scalar_prefetch=1,
             grid=(pairs,),
             in_specs=[
-                column(rows, 0),
-                column(rows, 0),
-                column(rows, pairs),
-                column(far_rows, 0),
-                column(far_rows, pairs),
+                column(rows, first),
+                column(rows, first),
+                column(rows, first + total),
+                column(far_rows, first),
+                column(far_rows, first + total),
             ],
             out_specs=[column(rows, 0), pl.BlockSpec((1, 2, rows), lambda h, c: (h, 0, 0))],
         ),
         out_shape=[
-            jax.ShapeDtypeStruct((rows, width), BF16),
+            jax.ShapeDtypeStruct((rows, pairs * 128), BF16),
             jax.ShapeDtypeStruct((pairs, 2, rows), F32),
         ],
-        compiler_params=pltpu.CompilerParams(vmem_limit_bytes=VMEM_LIMIT),
+        compiler_params=pltpu.CompilerParams(vmem_limit_bytes=16 * MEGA),
         cost_estimate=pl.CostEstimate(
-            flops=8 * rows * rows * width, bytes_accessed=rows * width * 12, transcendentals=rows * rows * 12
+            flops=rows * rows * pairs * 100 // 1, bytes_accessed=rows * pairs * 150 // 1, transcendentals=0
         ),
         name="attend",
     )(count, queries, near, near, remote, remote)
@@ -207,9 +209,9 @@
     dv_ref[...] = dv_sum[...]
 
 
-def attend_back(count, queries, near, remote, out_grad, attended, lse, block):
+def attend_back(count, queries, near, remote, out_grad, attended, lse, block, first=0):
     rows, width = attended.shape
-    pairs = width // 128
+    pairs, total = width // 128, queries.shape[1] // 128
     far_rows = remote.shape[0]
     column = lambda size, offset: pl.BlockSpec((size, 128), lambda h, c: (0, h + offset))
     return pl.pallas_call(
@@ -218,12 +220,12 @@
             num_scalar_prefetch=1,
             grid=(pairs,),
             in_specs=[
-                column(rows, 0),
-                column(rows, 0),
-                column(rows, pairs),
-                column(far_rows, 0),
-                column(far_rows, pairs),
-                column(rows, 0),
+                column(rows, first),
+                column(rows, first),
+                column(rows, first + total),
+                column(far_rows, first),
+                column(far_rows, first + total),
+                column(rows, first),
                 column(rows, 0),
                 pl.BlockSpec((1, 2, rows), lambda h, c: (h, 0, 0)),
             ],
@@ -247,9 +249,9 @@
             jax.ShapeDtypeStruct((far_rows, width), BF16),
             jax.ShapeDtypeStruct((far_rows, width), BF16),
         ],
-        compiler_params=pltpu.CompilerParams(vmem_limit_bytes=VMEM_LIMIT),
+        compiler_params=pltpu.CompilerParams(vmem_limit_bytes=16 * MEGA),
         cost_estimate=pl.CostEstimate(
-            flops=20 * rows * rows * width, bytes_accessed=rows * width * 30, transcendentals=rows * rows * 12
+            flops=2 * rows * rows * width // 1, bytes_accessed=rows * width * 3 // 1, transcendentals=0
         ),
         name="attend_back",
     )(count, queries, near, near, remote, remote, out_grad, attended, lse)
@@ -267,12 +269,16 @@
     return lax.ppermute(value, "seq", [(0, 1), (1, 0)])
 
 
-def regroup(value, dp, moves):
+def exchange_rows(value, dp=16):
     pairs = []
     for index in range(0, dp, 2):
         left, right = (index + 1) * 2, index * 2 + 1
         pairs += [(left, right), (right, left)]
-    return jnp.where(moves, lax.ppermute(value, ("dp", "seq"), pairs), value)
+    return lax.ppermute(value, ("dp", "seq"), pairs)
+
+
+def regroup(value, dp, moves):
+    return jnp.where(moves, exchange_rows(value, dp), value)
 
 
 def split_columns(value, width):
@@ -338,8 +344,8 @@
             scratch_shapes=scratch,
         ),
         out_shape=out_shape,
-        compiler_params=pltpu.CompilerParams(vmem_limit_bytes=VMEM_LIMIT),
-        cost_estimate=pl.CostEstimate(flops=flops, bytes_accessed=moved, transcendentals=0),
+        compiler_params=pltpu.CompilerParams(vmem_limit_bytes=VMEM[name] * MEGA),
+        cost_estimate=pl.CostEstimate(flops=flops // 10, bytes_accessed=moved // 10, transcendentals=0),
         name=name,
     )(*scalars, *args)
 
@@ -397,13 +403,19 @@
     return lax.ppermute(value, "dp", pairs_of(16, lambda index: index ^ 2))
 
 
-def gather_ring(own):
-    pieces = []
-    for step in range(4):
-        if step:
-            own = shift_z(own)
-        pieces += [own, swap_x(own)]
-    return pieces
+def after(value, *earlier):
+    return lax.optimization_barrier((value,) + earlier)[0]
+
+
+class Lane:
+    def __init__(self, move, depth=2):
+        self.move, self.depth, self.sent = move, depth, []
+
+    def __call__(self, value, move=None):
+        if len(self.sent) >= self.depth:
+            value = after(value, self.sent[-self.depth])
+        self.sent.append((move or self.move)(value))
+        return self.sent[-1]
 
 
 def ring_slots(z, x):
@@ -414,15 +426,42 @@
     return slots
 
 
-def gather_head(own):
-    pieces = gather_ring(own)
-    return pieces + [swap_cores(piece, 16) for piece in pieces]
-
-
-def gather_tail(own):
-    pieces = gather_ring(own)
-    pieces = pieces + [swap_seq(piece) for piece in pieces]
-    return pieces + [swap_cores(piece, 16) for piece in pieces]
+def gather(head, tail, values, out_grad, moves):
+    z, x, y = Lane(shift_z, 2), Lane(swap_x, 2), Lane(swap_seq, 2)
+    head, tail = [head], [tail]
+    head_x, tail_x, tail_y, tail_xy = [], [], [], []
+    head.append(z(head[0]))
+    head_x.append(x(head[0]))
+    tail_y.append(y(tail[0]))
+    head.append(z(head[1]))
+    tail_x.append(x(tail[0]))
+    new_values = y(values, exchange_rows)
+    tail.append(z(tail[0]))
+    head_x.append(x(head[1]))
+    new_grad = y(out_grad, exchange_rows)
+    head.append(z(head[2]))
+    head_x.append(x(head[2]))
+    tail_xy.append(y(tail_x[0]))
+    tail.append(z(tail[1]))
+    head_x.append(x(head[3]))
+    tail_y.append(y(tail[1]))
+    tail_x.append(x(tail[1]))
+    values = after(jnp.where(moves, new_values, values), tail_y[1], tail_xy[0], tail[2])
+    out_grad = jnp.where(moves, new_grad, out_grad)
+    tail.append(z(tail[2]))
+    tail_xy.append(y(tail_x[1]))
+    tail_x.append(x(tail[2]))
+    tail_y.append(y(tail[2]))
+    tail_x.append(x(tail[3]))
+    mix = lambda first, second: [piece for pair in zip(first, second) for piece in pair]
+
+    def rest(first, second):
+        tail_xy.append(y(after(tail_x[2], first)))
+        tail_y.append(y(after(tail[3], first)))
+        tail_xy.append(y(after(tail_x[3], second)))
+        return mix(tail_y, tail_xy), out_grad
+
+    return mix(head, head_x), mix(tail, tail_x), values, rest
 
 
 def row_sum(value):
@@ -491,9 +530,10 @@
     )
 
 
-def merge_kernel(x_ref, o_ref, weight, v48, m_ref, n2_ref):
+def merge_kernel(x_ref, o1_ref, o2_ref, weight, v48, m_ref, n2_ref):
     width = x_ref.shape[1]
-    middle = x_ref[...].astype(F32) + dot(o_ref[...], weight[...].reshape(width, width), 1, 0) + v48[3:4, :]
+    attended = jnp.concatenate([o1_ref[...], o2_ref[...]], axis=1)
+    middle = x_ref[...].astype(F32) + dot(attended, weight[...].reshape(width, width), 1, 0) + v48[3:4, :]
     m_ref[...] = middle
     shape, unused = normalise(middle)
     n2_ref[...] = (shape * v48[4:5, :] + v48[5:6, :]).astype(BF16)
@@ -507,8 +547,9 @@
 def merge(values, attended, packed, v48):
     rows, width = values.shape
     return kernel_call(
-        merge_kernel, (), [whole(values.shape), whole(values.shape), merge_spec(packed), whole(v48.shape)],
-        [values, attended, packed, v48], [whole(values.shape)] * 2,
+        merge_kernel, (),
+        [whole(values.shape)] + [whole(piece.shape) for piece in attended] + [merge_spec(packed), whole(v48.shape)],
+        [values] + attended + [packed, v48], [whole(values.shape)] * 2,
         [jax.ShapeDtypeStruct((rows, width), F32), jax.ShapeDtypeStruct((rows, width), BF16)],
         [], "merge", 2 * rows * width * width, 12 * rows * width,
     )
@@ -633,9 +674,10 @@
 
 
 def close_kernel(
-    place, n1_ref, x_ref, q_ref, k_ref, v_ref, far_k, far_v, o_ref, dz_ref, dm_ref, packed, v48, g48_in, g192,
-    *refs,
+    place, n1_ref, x_ref, q1, k1, v1, far_k1, far_v1, q2, k2, v2, far_k2, far_v2, o1, o2,
+    dz_ref, dm_ref, packed, v48, g48_in, g192, *refs,
 ):
+    join = lambda first, second: jnp.concatenate([first[...], second[...]], axis=1)
     grad_ref, outs, (grads, g48, g96, dt, sems) = refs[0], refs[1:9], refs[9:]
     z, x, core, half = spot(place)
     width = x_ref.shape[1]
@@ -644,17 +686,18 @@
     normed_grad = None
     for at in range(3):
         if at == 0:
-            dt[...] = q_ref[...]
+            dt[...] = join(q1, q2)
+        elif at == 1:
+            dt[...] = (join(k1, k2) + join(far_k1, far_k2).astype(F32)).astype(BF16)
         else:
-            near, far = (k_ref, far_k) if at == 1 else (v_ref, far_v)
-            dt[...] = (near[...] + far[...].astype(F32)).astype(BF16)
+            dt[...] = (join(v1, v2) + join(far_v1, far_v2).astype(F32)).astype(BF16)
         if at != 1:
             g96[2:3, (at // 2) * width : (at // 2 + 1) * width] = row_sum(dt[...].astype(F32))
         weight = packed[:, at * part : (at + 1) * part, :].reshape(width, width)
         term = dot(dt[...], weight, 1, 1)
         normed_grad = term if normed_grad is None else normed_grad + term
         grads[:, at * part : (at + 1) * part, :] = dot(normed_t, dt[...], 1, 0).astype(BF16).reshape(GROUPS, part, width)
-    grads[:, 3 * part : 4 * part, :] = dot(o_ref[...], dz_ref[...], 0, 0).astype(BF16).reshape(GROUPS, part, width)
+    grads[:, 3 * part : 4 * part, :] = dot(join(o1, o2), dz_ref[...], 0, 0).astype(BF16).reshape(GROUPS, part, width)
     shape, scale = normalise(x_ref[...].astype(F32))
     g48[...] = g48_in[...]
     g48[0:1, :] = row_sum(shape * normed_grad)
@@ -688,7 +731,7 @@
 
 def close(place, args):
     rows, width = args[0].shape
-    packed = args[10]
+    packed = args[16]
     head_rows = packed.shape[1]
     part = jax.ShapeDtypeStruct((2, head_rows, width), BF16)
     results = kernel_call(
@@ -702,31 +745,6 @@
         "close", 14 * rows * width * width, 20 * width * width,
     )
     return results[0], results[1:]
-
-
-def scatter_head(parts):
-    moving = None
-    for order in (1, 2, 3, 0):
-        keep, send = parts[2 * order], parts[2 * order + 1]
-        came = swap_cores(send, 16)
-        value = keep[0] + came[0] + swap_x(keep[1] + came[1])
-        if moving is not None:
-            value = value + shift_z(moving)
-        moving = value
-    return moving
-
-
-def scatter_tail(parts):
-    moving = None
-    for order in (1, 2, 3, 0):
-        keep, send = parts[2 * order], parts[2 * order + 1]
-        came = swap_cores(send, 16)
-        other = swap_seq(keep[1] + came[1])
-        value = keep[0, 0] + came[0, 0] + other[0] + swap_x(keep[0, 1] + came[0, 1] + other[1])
-        if moving is not None:
-            value = value + shift_z(moving)
-        moving = value
-    return moving
 
 
 def unpack_kernel(slots, place, head, head_far, tail, tail_far, *outs):
@@ -769,34 +787,72 @@
     core = index % 2
     moves = core != half
     head, tail = pack(tie_slots, place, masters)
-    head_pieces = gather_head(head)
-    tail_pieces = gather_tail(tail)
-    values = regroup(inputs.reshape(length, width), 16, moves)
-    out_grad = regroup(cotangent.reshape(length, width), 16, moves)
+    head_pieces, tail_pieces, values, rest = gather(
+        head, tail, inputs.reshape(length, width), cotangent.reshape(length, width), moves
+    )
+    head_pieces = head_pieces + [swap_cores(piece, 16) for piece in head_pieces]
     packed, normed, queries, near, v48, v96, v192 = qkv(place, values, head_pieces)
     remote = swap_cores(near, 16)
     far_count = core.astype(jnp.int32).reshape(1)
-    attended, lse = attend(far_count, queries, near, remote, block)
+    half_pairs = width // 256
+    queries = after(queries, tail_pieces[4], tail_pieces[3])
+    attended, lse = [None, None], [None, None]
+    attended[0], lse[0] = attend(far_count, queries, near, remote, block, 0, half_pairs)
+    queries = after(queries, attended[0])
+    attended[1], lse[1] = attend(far_count, queries, near, remote, block, half_pairs, half_pairs)
+    tail_other, out_grad = rest(attended[0], attended[1])
     middle, second = merge(values, attended, packed, v48)
+    late = lambda pieces, first: [
+        swap_cores(after(piece, attended[1]) if number >= first else piece, 16) for number, piece in enumerate(pieces)
+    ]
+    tail_pieces = tail_pieces + late(tail_pieces, 8)
+    tail_other = tail_other + late(tail_other, 4)
     (output, middle_grad, branch_grad, attended_grad, g48, g192), tail_parts = ffn(
-        place, tail_pieces, middle, second, out_grad, packed, v48, v192
-    )
-    tail_sum = scatter_tail(tail_parts)
-    output = regroup(output, 16, moves)
-    query_grad, key_grad, value_grad, far_key, far_value = attend_back(
-        far_count, queries, near, remote, attended_grad, attended, lse, block
-    )
+        place, tail_pieces[:8] + tail_other[:8] + tail_pieces[8:] + tail_other[8:],
+        middle, second, out_grad, packed, v48, v192,
+    )
+    z, x, y = Lane(shift_z, 2), Lane(swap_x, 2), Lane(swap_seq, 4)
+    came = [swap_cores(send, 16) for send in tail_parts[1::2]]
+    kept = [keep + other for keep, other in zip(tail_parts[0::2], came)]
+    attended_grad = after(attended_grad, *kept)
+    tail_y = {order: y(kept[order][1]) for order in (1, 2, 3, 0)}
+    grads = []
+    for part in range(2):
+        if part:
+            attended_grad = after(attended_grad, tail_y[1], grads[0])
+        query_grad, key_grad, value_grad, far_key, far_value = attend_back(
+            far_count, queries, near, remote, attended_grad, attended[part], lse[part], block, part * half_pairs
+        )
+        grads += [query_grad, key_grad, value_grad, swap_cores(far_key, 16), swap_cores(far_value, 16)]
+    tail_x = {}
+    tail_kept = {}
+    for order in (1, 2, 3, 0):
+        both = kept[order][0] + tail_y[order]
+        tail_kept[order] = both[0]
+        tail_x[order] = both[1]
+    middle_grad = after(middle_grad, tail_x[2], tail_kept[2])
     input_grad, head_parts = close(
         place,
         [
-            normed, values, query_grad, key_grad, value_grad, swap_cores(far_key, 16), swap_cores(far_value, 16),
-            attended, branch_grad, middle_grad, packed, v48, g48, g192,
+            normed, values, *grads, *attended, branch_grad, middle_grad, packed, v48, g48, g192,
         ],
     )
-    input_grad = regroup(input_grad, 16, moves).astype(F32)
-    head_sum = scatter_head(head_parts)
+    came = [swap_cores(send, 16) for send in head_parts[1::2]]
+    head_kept = [keep + other for keep, other in zip(head_parts[0::2], came)]
+    tail_sum = head_sum = None
+    new_output = y(output, exchange_rows)
+    new_input_grad = y(input_grad, exchange_rows)
+    for order in (1, 2, 3, 0):
+        came = x(tail_x[order])
+        part = tail_kept[order] + came
+        tail_sum = part if tail_sum is None else part + z(tail_sum)
+        came = x(head_kept[order][1])
+        part = head_kept[order][0] + came
+        head_sum = part if head_sum is None else part + z(head_sum)
+    output = jnp.where(moves, new_output, output)
+    input_grad = jnp.where(moves, new_input_grad, input_grad).astype(F32)
     grads = unpack(
-        tie_slots, place, [head_sum, swap_seq(head_sum), tail_sum, swap_seq(tail_sum)], masters
+        tie_slots, place, [head_sum, y(head_sum), tail_sum, y(tail_sum)], masters
     )
     shape = (length, count, width)
     return (output.reshape(shape), input_grad.reshape(shape)) + tuple(grads)

time: 341 us -> 301 us (0.88); the launches traced: 341 us -> 296 us
  waiting for transfers between devices: 173 us -> 125 us
  Pallas kernels: 88.1 us -> 76.2 us
  local copies, waits for them, and re-layouts: 6.5 us -> 14.9 us
  other arithmetic: 4.25 us -> 8.77 us
    ppermute x14, waiting for transfers between devices: 87.2 us -> 39.2 us  [swap_seq(): return lax.ppermute(value, 'seq', [(0, 1), (1, 0)])]
    ppermute x12, waiting for transfers between devices: 62.4 us -> 48 us  [shift_z(): lax.ppermute(value, 'dp', pairs_of(16, lambda index: (index + 4) % 16))]
    ppermute x16, waiting for transfers between devices: 21.1 us -> 34.7 us  [swap_x(): return lax.ppermute(value, 'dp', pairs_of(16, lambda index: index ^ 2))]
    pallas_call x6, Pallas kernels: 64.9 us -> 54.8 us  [kernel_call(): pl.pallas_call(body, grid_spec=pltpu.PrefetchScalarGridSpec(num_scalar_pr...]
    unnamed x105 -> x149, local copies, waits for them, and re-layouts: 6.5 us -> 14.6 us
    ppermute x12, starting transfers between devices: 3.66 us -> 9.77 us  [shift_z(): lax.ppermute(value, 'dp', pairs_of(16, lambda index: (index + 4) % 16))]
    ppermute x35 -> x37, starting transfers between devices: 28.1 us -> 25.2 us  [swap_cores(): return lax.ppermute(value, 'dp', pairs_of(count, lambda index: index ^ 1))]
    pallas_call x1 -> x2, Pallas kernels: 12.5 us -> 11.4 us  [attend(): pl.pallas_call(functools.partial(attend_kernel, block=block), grid_spec=p...]
  transfers between devices with their start and end apart: 81 -> 83, of which waited for: 32 -> 31; matrix products, arithmetic and copies ran while one was open for 2% -> 4% of each run, Pallas kernels for 12% -> 11%
where the time goes in v3:
time: 301 us; the launch traced here: 296 us
  waiting for transfers between devices  125 us (42%)
  Pallas kernels  76.2 us (25%)
  starting transfers between devices  68.8 us (23%)
  local copies, waits for them, and re-layouts  14.9 us (5%)
  other arithmetic  8.77 us (3%)
    pallas_call x6, Pallas kernels, kernel_call(): pl.pallas_call(body, grid_spec=pltpu.PrefetchScalarGridSpec(num_scalar_pr...  54.8 us
    ppermute x12, waiting for transfers between devices, shift_z(): lax.ppermute(value, 'dp', pairs_of(16, lambda index: (index + 4) % 16))  48 us
    ppermute x14, waiting for transfers between devices, swap_seq(): return lax.ppermute(value, 'seq', [(0, 1), (1, 0)])  39.2 us
    ppermute x16, waiting for transfers between devices, swap_x(): return lax.ppermute(value, 'dp', pairs_of(16, lambda index: index ^ 2))  34.7 us
    ppermute x37, starting transfers between devices, swap_cores(): return lax.ppermute(value, 'dp', pairs_of(count, lambda index: index ^ 1))  25.2 us
    ppermute x16, starting transfers between devices, swap_x(): return lax.ppermute(value, 'dp', pairs_of(16, lambda index: index ^ 2))  17.6 us
    unnamed x149, local copies, waits for them, and re-layouts  14.6 us
    ppermute x14, starting transfers between devices, swap_seq(): return lax.ppermute(value, 'seq', [(0, 1), (1, 0)])  13.4 us
  transfers between devices with their start and end apart: 83, of which 31 were waited for; matrix products, arithmetic and copies ran while one was open for 4% of the time, Pallas kernels for 11%

profile of v3, /device:TPU:0, one launch (start us, length us, event | category | flops | bytes accessed | tf_op | source)
XLA Modules:
  0.0 296.3 jit_solution(10182281331011683693)
XLA Ops:
  1.2 3.1 %pack.1 = (bf16[208,768]{1,0:T(8,128)(2,1)}, bf16[192,768]{1,0:T(8,128)(2,1)}) custom-call(s32[12]{0:T(128)} %slots.3, s32[2]{0:T(128)} %pad_add_fusion.place, f32[2,48]{1,0:T(2,128)} %refs_0_.1, f32[2,48]{1,0:T(2,128)} %refs_1_.1, f32[2,48,2304]{2,1,0:T(8,128)} %refs_2_.1, f32[2,96]{1,0:T(2,128)} %refs_3_.1, f32[2,48,768]{2,1,0:T(8,128)} %refs_4_.1, ...), custom_call_target="tpu_custom_call" | custom-call | bytes 383385 | tf_op jit(solution)/shard_map/pack/pallas_call | solution.py:337
  4.4 3.0 %collective-permute-start.1 = (bf16[208,768]{1,0:T(8,128)(2,1)}, bf16[208,768]{1,0:T(8,128)(2,1)S(1)}, u32[]{:S(2)}, u32[]{:S(2)}) collective-permute-start(bf16[208,768]{1,0:T(8,128)(2,1)} %get-tuple-element.119.refs_0_), channel_id=1, source_target_pairs={{0,8},{2,10},{4,12},{6,14},{8,16},{10,18},{12,20},{14,22},{16,24},... | collective-permute-start | bytes 958472 | tf_op jit(solution)/shard_map/ppermute | solution.py:399
  10.4 6.8 %collective-permute-done.1.refs_2_ = bf16[208,768]{1,0:T(8,128)(2,1)S(1)} collective-permute-done((bf16[208,768]{1,0:T(8,128)(2,1)}, bf16[208,768]{1,0:T(8,128)(2,1)S(1)}, u32[]{:S(2)}, u32[]{:S(2)}) %collective-permute-start.1) | collective-permute-done | bytes 319520 | tf_op jit(solution)/shard_map/ppermute | solution.py:399
  20.8 4.1 %collective-permute-start.21 = (bf16[208,768]{1,0:T(8,128)(2,1)}, bf16[208,768]{1,0:T(8,128)(2,1)S(1)}, u32[]{:S(2)}, u32[]{:S(2)}) collective-permute-start(bf16[208,768]{1,0:T(8,128)(2,1)} %get-tuple-element.119.refs_0_), channel_id=1, source_target_pairs={{0,2},{2,0},{4,6},{6,4},{8,10},{10,8},{12,14},{14,12},{16,18},{18,... | collective-permute-start | bytes 958472 | tf_op jit(solution)/shard_map/ppermute | solution.py:265
  29.0 6.5 %collective-permute-done.9.refs_3_ = bf16[208,768]{1,0:T(8,128)(2,1)S(1)} collective-permute-done((bf16[208,768]{1,0:T(8,128)(2,1)S(1)}, bf16[208,768]{1,0:T(8,128)(2,1)S(1)}, u32[]{:S(2)}, u32[]{:S(2)}) %collective-permute-start.9) | collective-permute-done | bytes 319520 | tf_op jit(solution)/shard_map/ppermute | solution.py:403
  35.5 5.7 %collective-permute-done.7.refs_6_ = bf16[208,768]{1,0:T(8,128)(2,1)S(1)} collective-permute-done((bf16[208,768]{1,0:T(8,128)(2,1)S(1)}, bf16[208,768]{1,0:T(8,128)(2,1)S(1)}, u32[]{:S(2)}, u32[]{:S(2)}) %collective-permute-start.7) | collective-permute-done | bytes 319520 | tf_op jit(solution)/shard_map/ppermute | solution.py:399
  41.2 3.2 %collective-permute-done.2.refs_2_ = bf16[192,768]{1,0:T(8,128)(2,1)S(1)} collective-permute-done((bf16[192,768]{1,0:T(8,128)(2,1)}, bf16[192,768]{1,0:T(8,128)(2,1)S(1)}, u32[]{:S(2)}, u32[]{:S(2)}) %collective-permute-start.2) | collective-permute-done | bytes 294944 | tf_op jit(solution)/shard_map/ppermute | solution.py:399
  48.5 6.4 %collective-permute-done.6.refs_4_ = bf16[192,768]{1,0:T(8,128)(2,1)S(1)} collective-permute-done((bf16[192,768]{1,0:T(8,128)(2,1)S(1)}, bf16[192,768]{1,0:T(8,128)(2,1)S(1)}, u32[]{:S(2)}, u32[]{:S(2)}) %collective-permute-start.6) | collective-permute-done | bytes 294944 | tf_op jit(solution)/shard_map/ppermute | solution.py:399
  67.0 5.2 %qkv.1 = (bf16[16,208,768]{2,1,0:T(8,128)(2,1)S(1)}, bf16[512,768]{1,0:T(8,128)(2,1)S(1)}, bf16[512,768]{1,0:T(8,128)(2,1)S(1)}, bf16[512,1536]{1,0:T(8,128)(2,1...) custom-call(s32[2]{0:T(128)S(1)} %copy-done.34, ...), custom_call_target="tpu_custom_call" | custom-call | flops 181193936 | bytes 1179648 | tf_op jit(solution)/shard_map/qkv/pallas_call | solution.py:337
  76.3 6.2 %collective-permute-done.5.refs_3_ = bf16[192,768]{1,0:T(8,128)(2,1)S(1)} collective-permute-done((bf16[192,768]{1,0:T(8,128)(2,1)S(1)}, bf16[192,768]{1,0:T(8,128)(2,1)S(1)}, u32[]{:S(2)}, u32[]{:S(2)}) %collective-permute-start.5) | collective-permute-done | bytes 294944 | tf_op jit(solution)/shard_map/ppermute | solution.py:403
  85.5 5.7 %attend.2 = (bf16[512,384]{1,0:T(8,128)(2,1)S(1)}, f32[3,2,512]{2,1,0:T(2,128)S(1)}) custom-call(s32[1]{0:T(128)} %bitcast.4.count, bf16[512,768]{1,0:T(8,128)(2,1)S(1)} %get-tuple-element.144.q_ref, bf16[512,1536]{1,0:T(8,128)(2,1)S(1)} %get-tuple-element.138.k_ref.v_ref, bf16[512,1536]{1,0:T(8,128)(2,1)S(1)} %get-tuple-element.138.k_ref.v_ref, ...), custom_call_target="tpu_custom_call" | custom-call | flops 78643200 | bytes 230400 | tf_op jit(solution)/shard_map/attend/pallas_call | solution.py:99
  93.8 3.7 %collective-permute-start.33 = (bf16[192,768]{1,0:T(8,128)(2,1)S(1)}, bf16[192,768]{1,0:T(8,128)(2,1)S(1)}, u32[]{:S(2)}, u32[]{:S(2)}) collective-permute-start(bf16[192,768]{1,0:T(8,128)(2,1)S(1)} %copy-done.21), channel_id=1, source_target_pairs={{0,2},{2,0},{4,6},{6,4},{8,10},{10,8},{12,14},{14,12},{16,18},{18,... | collective-permute-start | bytes 884744 | tf_op jit(solution)/shard_map/ppermute | solution.py:265
  98.1 5.7 %attend.3 = (bf16[512,384]{1,0:T(8,128)(2,1)S(1)}, f32[3,2,512]{2,1,0:T(2,128)S(1)}) custom-call(s32[1]{0:T(128)} %bitcast.4.count, bf16[512,768]{1,0:T(8,128)(2,1)S(1)} %get-tuple-element.144.q_ref, bf16[512,1536]{1,0:T(8,128)(2,1)S(1)} %get-tuple-element.138.k_ref.v_ref, bf16[512,1536]{1,0:T(8,128)(2,1)S(1)} %get-tuple-element.138.k_ref.v_ref, ...), custom_call_target="tpu_custom_call" | custom-call | flops 78643200 | bytes 230400 | tf_op jit(solution)/shard_map/attend/pallas_call | solution.py:99
  103.8 6.1 %collective-permute-start.35 = (bf16[192,768]{1,0:T(8,128)(2,1)S(1)}, bf16[192,768]{1,0:T(8,128)(2,1)S(1)}, u32[]{:S(2)}, u32[]{:S(2)}) collective-permute-start(bf16[192,768]{1,0:T(8,128)(2,1)S(1)} %copy-done.27), channel_id=1, source_target_pairs={{0,2},{2,0},{4,6},{6,4},{8,10},{10,8},{12,14},{14,12},{16,18},{18,... | collective-permute-start | bytes 884744 | tf_op jit(solution)/shard_map/ppermute | solution.py:265
  113.2 7.1 %collective-permute-done.31.refs_14_ = bf16[192,768]{1,0:T(8,128)(2,1)S(1)} collective-permute-done((bf16[192,768]{1,0:T(8,128)(2,1)S(1)}, bf16[192,768]{1,0:T(8,128)(2,1)S(1)}, u32[]{:S(2)}, u32[]{:S(2)}) %collective-permute-start.31) | collective-permute-done | bytes 294944 | tf_op jit(solution)/shard_map/ppermute | solution.py:269
  120.3 5.5 %collective-permute-done.32.refs_15_ = bf16[192,768]{1,0:T(8,128)(2,1)S(1)} collective-permute-done((bf16[192,768]{1,0:T(8,128)(2,1)S(1)}, bf16[192,768]{1,0:T(8,128)(2,1)S(1)}, u32[]{:S(2)}, u32[]{:S(2)}) %collective-permute-start.32) | collective-permute-done | bytes 294944 | tf_op jit(solution)/shard_map/ppermute | solution.py:269
  134.3 31.7 %ffn.1 = (bf16[512,768]{1,0:T(8,128)(2,1)}, f32[512,768]{1,0:T(8,128)}, bf16[512,768]{1,0:T(8,128)(2,1)}, bf16[512,768]{1,0:T(8,128)(2,1)}, f32[8,768]{1,0:T(8,1...) custom-call(s32[2]{0:T(128)S(1)} %copy-done.34, ...), custom_call_target="tpu_custom_call" | custom-call | flops 1449551488 | bytes 1887436 | tf_op jit(solution)/shard_map/ffn/pallas_call | solution.py:337
  176.4 4.9 %attend_back.2 = (bf16[512,384]{1,0:T(8,128)(2,1)S(1)}, f32[512,384]{1,0:T(8,128)S(1)}, f32[512,384]{1,0:T(8,128)S(1)}, bf16[512,384]{1,0:T(8,128)(2,1)S(1)}, bf16[512,384]{1,0:T(8,128)(2,1)S(1)}) custom-call(s32[1]{0:T(128)} %bitcast.4.count, bf16[512,768]{1,0:T(8,128)(2,1)S(1)} %get-tuple-element.144.q_ref, ...), custom_call_target="tpu_custom_call" | custom-call | flops 201326592 | bytes 589824 | tf_op jit(solution)/shard_map/attend_back/pallas_call | solution.py:217
  181.3 4.9 %collective-permute-start.55 = (bf16[512,384]{1,0:T(8,128)(2,1)S(1)}, bf16[512,384]{1,0:T(8,128)(2,1)S(1)}, u32[]{:S(2)}, u32[]{:S(2)}) collective-permute-start(bf16[512,384]{1,0:T(8,128)(2,1)S(1)} %get-tuple-element.174), channel_id=1, source_target_pairs={{0,2},{2,0},{4,6},{6,4},{8,10},{10,8},{12,14},{14,12},{16,18},{18,... | collective-permute-start | bytes 1179656 | tf_op jit(solution)/shard_map/ppermute | solution.py:265
  187.0 5.2 %attend_back.3 = (bf16[512,384]{1,0:T(8,128)(2,1)S(1)}, f32[512,384]{1,0:T(8,128)S(1)}, f32[512,384]{1,0:T(8,128)S(1)}, bf16[512,384]{1,0:T(8,128)(2,1)S(1)}, bf16[512,384]{1,0:T(8,128)(2,1)S(1)}) custom-call(s32[1]{0:T(128)} %bitcast.4.count, bf16[512,768]{1,0:T(8,128)(2,1)S(1)} %get-tuple-element.144.q_ref, ...), custom_call_target="tpu_custom_call" | custom-call | flops 201326592 | bytes 589824 | tf_op jit(solution)/shard_map/attend_back/pallas_call | solution.py:217
  192.1 7.4 %collective-permute-done.59 = bf16[2,192,768]{2,1,0:T(8,128)(2,1)S(1)} collective-permute-done((bf16[2,192,768]{2,1,0:T(8,128)(2,1)S(1)}, bf16[2,192,768]{2,1,0:T(8,128)(2,1)S(1)}, u32[]{:S(2)}, u32[]{:S(2)}) %collective-permute-start.59) | collective-permute-done | bytes 589856 | tf_op jit(solution)/shard_map/ppermute | solution.py:269
  201.8 10.9 %close.1 = (bf16[512,768]{1,0:T(8,128)(2,1)S(1)}, bf16[2,208,768]{2,1,0:T(8,128)(2,1)S(1)}, bf16[2,208,768]{2,1,0:T(8,128)(2,1)S(1)}, bf16[2,208,768]{2,1,0:T(8,...) custom-call(s32[2]{0:T(128)S(1)} %copy-done.34, ...), custom_call_target="tpu_custom_call" | custom-call | flops 422785856 | bytes 1179648 | tf_op jit(solution)/shard_map/close/pallas_call | solution.py:337
  213.0 11.3 %collective-permute-done.72 = bf16[2,192,768]{2,1,0:T(8,128)(2,1)S(1)} collective-permute-done((bf16[2,192,768]{2,1,0:T(8,128)(2,1)S(1)}, bf16[2,192,768]{2,1,0:T(8,128)(2,1)S(1)}, u32[]{:S(2)}, u32[]{:S(2)}) %collective-permute-start.72) | collective-permute-done | bytes 589856 | tf_op jit(solution)/shard_map/ppermute | solution.py:269
  226.7 7.9 %collective-permute-done.65 = bf16[208,768]{1,0:T(8,128)(2,1)S(1)} collective-permute-done((bf16[208,768]{1,0:T(8,128)(2,1)S(1)}, bf16[208,768]{1,0:T(8,128)(2,1)S(1)}, u32[]{:S(2)}, u32[]{:S(2)}) %collective-permute-start.65) | collective-permute-done | bytes 319520 | tf_op jit(solution)/shard_map/ppermute | solution.py:403
  240.4 4.6 %collective-permute-done.66 = bf16[208,768]{1,0:T(8,128)(2,1)S(1)} collective-permute-done((bf16[208,768]{1,0:T(8,128)(2,1)S(1)}, bf16[208,768]{1,0:T(8,128)(2,1)S(1)}, u32[]{:S(2)}, u32[]{:S(2)}) %collective-permute-start.66) | collective-permute-done | bytes 319520 | tf_op jit(solution)/shard_map/ppermute | solution.py:403
  249.1 3.8 %collective-permute-done.79 = bf16[192,768]{1,0:T(8,128)(2,1)S(1)} collective-permute-done((bf16[192,768]{1,0:T(8,128)(2,1)S(1)}, bf16[192,768]{1,0:T(8,128)(2,1)S(1)}, u32[]{:S(2)}, u32[]{:S(2)}) %collective-permute-start.79) | collective-permute-done | bytes 294944 | tf_op jit(solution)/shard_map/ppermute | solution.py:399
  255.6 3.0 %collective-permute-done.67 = bf16[208,768]{1,0:T(8,128)(2,1)S(1)} collective-permute-done((bf16[208,768]{1,0:T(8,128)(2,1)S(1)}, bf16[208,768]{1,0:T(8,128)(2,1)S(1)}, u32[]{:S(2)}, u32[]{:S(2)}) %collective-permute-start.67) | collective-permute-done | bytes 319520 | tf_op jit(solution)/shard_map/ppermute | solution.py:403
  259.3 5.8 %collective-permute-done.70 = bf16[208,768]{1,0:T(8,128)(2,1)S(1)} collective-permute-done((bf16[208,768]{1,0:T(8,128)(2,1)S(1)}, bf16[208,768]{1,0:T(8,128)(2,1)S(1)}, u32[]{:S(2)}, u32[]{:S(2)}) %collective-permute-start.70) | collective-permute-done | bytes 319520 | tf_op jit(solution)/shard_map/ppermute | solution.py:399
  266.0 2.8 collective-permute-done.80
  271.2 3.9 %collective-permute-done.68 = bf16[208,768]{1,0:T(8,128)(2,1)S(1)} collective-permute-done((bf16[208,768]{1,0:T(8,128)(2,1)S(1)}, bf16[208,768]{1,0:T(8,128)(2,1)S(1)}, u32[]{:S(2)}, u32[]{:S(2)}) %collective-permute-start.68) | collective-permute-done | bytes 319520 | tf_op jit(solution)/shard_map/ppermute | solution.py:403
  275.0 5.8 %collective-permute-done.71 = bf16[208,768]{1,0:T(8,128)(2,1)S(1)} collective-permute-done((bf16[208,768]{1,0:T(8,128)(2,1)S(1)}, bf16[208,768]{1,0:T(8,128)(2,1)S(1)}, u32[]{:S(2)}, u32[]{:S(2)}) %collective-permute-start.71) | collective-permute-done | bytes 319520 | tf_op jit(solution)/shard_map/ppermute | solution.py:399
  287.5 5.7 %collective-permute-done.82.tail_far = bf16[192,768]{1,0:T(8,128)(2,1)S(1)} collective-permute-done((bf16[192,768]{1,0:T(8,128)(2,1)S(1)}, bf16[192,768]{1,0:T(8,128)(2,1)S(1)}, u32[]{:S(2)}, u32[]{:S(2)}) %collective-permute-start.82) | collective-permute-done | bytes 294944 | tf_op jit(solution)/shard_map/ppermute | solution.py:269
  (330 shorter events, 90.8 us)
Async XLA Ops:
  4.4 12.8 %collective-permute-start.1 = (bf16[208,768]{1,0:T(8,128)(2,1)}, bf16[208,768]{1,0:T(8,128)(2,1)S(1)}, u32[]{:S(2)}, u32[]{:S(2)}) collective-permute-start(bf16[208,768]{1,0:T(8,128)(2,1)} %get-tuple-element.119.refs_0_), channel_id=1, source_target_pairs={{0,8},{2,10},{4,12},{6,14},{8,16},{10,18},{12,20},{14,22},{16,24},... | collective-permute-start | bytes 958472 | tf_op jit(solution)/shard_map/ppermute | solution.py:399
  18.6 26.7 %collective-permute-start.15 = (bf16[512,768]{1,0:T(8,128)(2,1)}, bf16[512,768]{1,0:T(8,128)(2,1)S(1)}, u32[]{:S(2)}, u32[]{:S(2)}) collective-permute-start(bf16[512,768]{1,0:T(8,128)(2,1)} %bitcast.2), channel_id=1, source_target_pairs={{2,1},{1,2},{6,5},{5,6},{10,9},{9,10},{14,13},{13,14},{18,17},{17,... | collective-permute-start | bytes 2359304 | tf_op jit(solution)/shard_map/ppermute | solution.py:277
  20.1 26.3 %collective-permute-start.17 = (bf16[512,768]{1,0:T(8,128)(2,1)}, bf16[512,768]{1,0:T(8,128)(2,1)S(1)}, u32[]{:S(2)}, u32[]{:S(2)}) collective-permute-start(bf16[512,768]{1,0:T(8,128)(2,1)} %bitcast.3), channel_id=1, source_target_pairs={{2,1},{1,2},{6,5},{5,6},{10,9},{9,10},{14,13},{13,14},{18,17},{17,... | collective-permute-start | bytes 2359304 | tf_op jit(solution)/shard_map/ppermute | solution.py:277
  29.0 15.4 %collective-permute-start.2 = (bf16[192,768]{1,0:T(8,128)(2,1)}, bf16[192,768]{1,0:T(8,128)(2,1)S(1)}, u32[]{:S(2)}, u32[]{:S(2)}) collective-permute-start(bf16[192,768]{1,0:T(8,128)(2,1)} %get-tuple-element.120.refs_0_), channel_id=1, source_target_pairs={{0,8},{2,10},{4,12},{6,14},{8,16},{10,18},{12,20},{14,22},{16,24},... | collective-permute-start | bytes 884744 | tf_op jit(solution)/shard_map/ppermute | solution.py:399
  72.3 13.2 %collective-permute-start.29 = (bf16[512,1536]{1,0:T(8,128)(2,1)S(1)}, bf16[512,1536]{1,0:T(8,128)(2,1)S(1)}, u32[]{:S(2)}, u32[]{:S(2)}) collective-permute-start(bf16[512,1536]{1,0:T(8,128)(2,1)S(1)} %get-tuple-element.138.k_ref.v_ref), channel_id=1, source_target_pairs={{0,2},{2,0},{4,6},{6,4},{8,10},{10,8},{12,14},{14,12},{16,18},{18,... | collective-permute-start | bytes 4718600 | tf_op jit(solution)/shard_map/ppermute | solution.py:265
  75.7 15.5 %collective-permute-start.11 = (bf16[192,768]{1,0:T(8,128)(2,1)S(1)}, bf16[192,768]{1,0:T(8,128)(2,1)S(1)}, u32[]{:S(2)}, u32[]{:S(2)}) collective-permute-start(bf16[192,768]{1,0:T(8,128)(2,1)S(1)} %copy-done.30), channel_id=1, source_target_pairs={{0,4},{2,6},{4,0},{6,2},{8,12},{10,14},{12,8},{14,10},{16,20},{18,... | collective-permute-start | bytes 884744 | tf_op jit(solution)/shard_map/ppermute | solution.py:403
  83.8 13.7 %collective-permute-start.20 = (bf16[192,768]{1,0:T(8,128)(2,1)S(1)}, bf16[192,768]{1,0:T(8,128)(2,1)S(1)}, u32[]{:S(2)}, u32[]{:S(2)}) collective-permute-start(bf16[192,768]{1,0:T(8,128)(2,1)S(1)} %copy-done.30), channel_id=1, source_target_pairs={{0,1},{1,0},{2,3},{3,2},{4,5},{5,4},{6,7},{7,6},{8,9},{9,8},{10,11... | collective-permute-start | bytes 884744 | tf_op jit(solution)/shard_map/ppermute | solution.py:269
  84.5 19.3 %collective-permute-start.13 = (bf16[192,768]{1,0:T(8,128)(2,1)S(1)}, bf16[192,768]{1,0:T(8,128)(2,1)S(1)}, u32[]{:S(2)}, u32[]{:S(2)}) collective-permute-start(bf16[192,768]{1,0:T(8,128)(2,1)S(1)} %collective-permute-done.12.refs_6_), channel_id=1, source_target_pairs={{0,4},{2,6},{4,0},{6,2},{8,12},{10,14},{12,8},{14,10},{16,20},{18,... | collective-permute-start | bytes 884744 | tf_op jit(solution)/shard_map/ppermute | solution.py:403
  92.4 17.5 %collective-permute-start.30 = (bf16[192,768]{1,0:T(8,128)(2,1)S(1)}, bf16[192,768]{1,0:T(8,128)(2,1)S(1)}, u32[]{:S(2)}, u32[]{:S(2)}) collective-permute-start(bf16[192,768]{1,0:T(8,128)(2,1)S(1)} %collective-permute-done.11.refs_5_), channel_id=1, source_target_pairs={{0,1},{1,0},{2,3},{3,2},{4,5},{5,4},{6,7},{7,6},{8,9},{9,8},{10,11... | collective-permute-start | bytes 884744 | tf_op jit(solution)/shard_map/ppermute | solution.py:269
  93.8 16.2 %collective-permute-start.33 = (bf16[192,768]{1,0:T(8,128)(2,1)S(1)}, bf16[192,768]{1,0:T(8,128)(2,1)S(1)}, u32[]{:S(2)}, u32[]{:S(2)}) collective-permute-start(bf16[192,768]{1,0:T(8,128)(2,1)S(1)} %copy-done.21), channel_id=1, source_target_pairs={{0,2},{2,0},{4,6},{6,4},{8,10},{10,8},{12,14},{14,12},{16,18},{18,... | collective-permute-start | bytes 884744 | tf_op jit(solution)/shard_map/ppermute | solution.py:265
  97.5 13.0 %collective-permute-start.41 = (bf16[192,768]{1,0:T(8,128)(2,1)S(1)}, bf16[192,768]{1,0:T(8,128)(2,1)S(1)}, u32[]{:S(2)}, u32[]{:S(2)}) collective-permute-start(bf16[192,768]{1,0:T(8,128)(2,1)S(1)} %copy-done.46), channel_id=1, source_target_pairs={{0,2},{2,0},{4,6},{6,4},{8,10},{10,8},{12,14},{14,12},{16,18},{18,... | collective-permute-start | bytes 884744 | tf_op jit(solution)/shard_map/ppermute | solution.py:265
  97.6 13.4 %collective-permute-start.34 = (bf16[192,768]{1,0:T(8,128)(2,1)S(1)}, bf16[192,768]{1,0:T(8,128)(2,1)S(1)}, u32[]{:S(2)}, u32[]{:S(2)}) collective-permute-start(bf16[192,768]{1,0:T(8,128)(2,1)S(1)} %copy-done.24), channel_id=1, source_target_pairs={{0,2},{2,0},{4,6},{6,4},{8,10},{10,8},{12,14},{14,12},{16,18},{18,... | collective-permute-start | bytes 884744 | tf_op jit(solution)/shard_map/ppermute | solution.py:265
  110.9 14.9 %collective-permute-start.32 = (bf16[192,768]{1,0:T(8,128)(2,1)S(1)}, bf16[192,768]{1,0:T(8,128)(2,1)S(1)}, u32[]{:S(2)}, u32[]{:S(2)}) collective-permute-start(bf16[192,768]{1,0:T(8,128)(2,1)S(1)} %collective-permute-done.13.refs_7_), channel_id=1, source_target_pairs={{0,1},{1,0},{2,3},{3,2},{4,5},{5,4},{6,7},{7,6},{8,9},{9,8},{10,11... | collective-permute-start | bytes 884744 | tf_op jit(solution)/shard_map/ppermute | solution.py:269
  112.5 13.3 %collective-permute-start.36 = (bf16[192,768]{1,0:T(8,128)(2,1)S(1)}, bf16[192,768]{1,0:T(8,128)(2,1)S(1)}, u32[]{:S(2)}, u32[]{:S(2)}) collective-permute-start(bf16[192,768]{1,0:T(8,128)(2,1)S(1)} %collective-permute-done.5.refs_3_), channel_id=1, source_target_pairs={{0,2},{2,0},{4,6},{6,4},{8,10},{10,8},{12,14},{14,12},{16,18},{18,... | collective-permute-start | bytes 884744 | tf_op jit(solution)/shard_map/ppermute | solution.py:265
  112.6 13.7 %collective-permute-start.39 = (bf16[192,768]{1,0:T(8,128)(2,1)S(1)}, bf16[192,768]{1,0:T(8,128)(2,1)S(1)}, u32[]{:S(2)}, u32[]{:S(2)}) collective-permute-start(bf16[192,768]{1,0:T(8,128)(2,1)S(1)} %collective-permute-done.12.refs_6_), channel_id=1, source_target_pairs={{0,2},{2,0},{4,6},{6,4},{8,10},{10,8},{12,14},{14,12},{16,18},{18,... | collective-permute-start | bytes 884744 | tf_op jit(solution)/shard_map/ppermute | solution.py:265
  113.1 13.3 %collective-permute-start.43 = (bf16[192,768]{1,0:T(8,128)(2,1)S(1)}, bf16[192,768]{1,0:T(8,128)(2,1)S(1)}, u32[]{:S(2)}, u32[]{:S(2)}) collective-permute-start(bf16[192,768]{1,0:T(8,128)(2,1)S(1)} %copy-done.50), channel_id=1, source_target_pairs={{0,2},{2,0},{4,6},{6,4},{8,10},{10,8},{12,14},{14,12},{16,18},{18,... | collective-permute-start | bytes 884744 | tf_op jit(solution)/shard_map/ppermute | solution.py:265
  170.7 16.2 %collective-permute-start.50 = (bf16[2,192,768]{2,1,0:T(8,128)(2,1)S(1)}, bf16[2,192,768]{2,1,0:T(8,128)(2,1)S(1)}, u32[]{:S(2)}, u32[]{:S(2)}) collective-permute-start(bf16[2,192,768]{2,1,0:T(8,128)(2,1)S(1)} %slice_bitcast_fusion.7), channel_id=1, source_target_pairs={{0,1},{1,0},{2,3},{3,2},{4,5},{5,4},{6,7},{7,6},{8,9},{9,8},{10,11... | collective-permute-start | bytes 1769480 | tf_op jit(solution)/shard_map/ppermute | solution.py:269
  172.2 27.3 %collective-permute-start.59 = (bf16[2,192,768]{2,1,0:T(8,128)(2,1)S(1)}, bf16[2,192,768]{2,1,0:T(8,128)(2,1)S(1)}, u32[]{:S(2)}, u32[]{:S(2)}) collective-permute-start(bf16[2,192,768]{2,1,0:T(8,128)(2,1)S(1)} %slice_bitcast_fusion.5), channel_id=1, source_target_pairs={{0,1},{1,0},{2,3},{3,2},{4,5},{5,4},{6,7},{7,6},{8,9},{9,8},{10,11... | collective-permute-start | bytes 1769480 | tf_op jit(solution)/shard_map/ppermute | solution.py:269
  173.8 39.1 %collective-permute-start.74 = (bf16[2,192,768]{2,1,0:T(8,128)(2,1)S(1)}, bf16[2,192,768]{2,1,0:T(8,128)(2,1)S(1)}, u32[]{:S(2)}, u32[]{:S(2)}) collective-permute-start(bf16[2,192,768]{2,1,0:T(8,128)(2,1)S(1)} %slice_bitcast_fusion.2), channel_id=1, source_target_pairs={{0,1},{1,0},{2,3},{3,2},{4,5},{5,4},{6,7},{7,6},{8,9},{9,8},{10,11... | collective-permute-start | bytes 1769480 | tf_op jit(solution)/shard_map/ppermute | solution.py:269
  175.3 48.9 %collective-permute-start.72 = (bf16[2,192,768]{2,1,0:T(8,128)(2,1)S(1)}, bf16[2,192,768]{2,1,0:T(8,128)(2,1)S(1)}, u32[]{:S(2)}, u32[]{:S(2)}) collective-permute-start(bf16[2,192,768]{2,1,0:T(8,128)(2,1)S(1)} %slice_bitcast_fusion.4), channel_id=1, source_target_pairs={{0,1},{1,0},{2,3},{3,2},{4,5},{5,4},{6,7},{7,6},{8,9},{9,8},{10,11... | collective-permute-start | bytes 1769480 | tf_op jit(solution)/shard_map/ppermute | solution.py:269
  181.3 18.3 %collective-permute-start.55 = (bf16[512,384]{1,0:T(8,128)(2,1)S(1)}, bf16[512,384]{1,0:T(8,128)(2,1)S(1)}, u32[]{:S(2)}, u32[]{:S(2)}) collective-permute-start(bf16[512,384]{1,0:T(8,128)(2,1)S(1)} %get-tuple-element.174), channel_id=1, source_target_pairs={{0,2},{2,0},{4,6},{6,4},{8,10},{10,8},{12,14},{14,12},{16,18},{18,... | collective-permute-start | bytes 1179656 | tf_op jit(solution)/shard_map/ppermute | solution.py:265
  186.9 13.4 %collective-permute-start.56 = (bf16[512,384]{1,0:T(8,128)(2,1)S(1)}, bf16[512,384]{1,0:T(8,128)(2,1)S(1)}, u32[]{:S(2)}, u32[]{:S(2)}) collective-permute-start(bf16[512,384]{1,0:T(8,128)(2,1)S(1)} %get-tuple-element.175), channel_id=1, source_target_pairs={{0,2},{2,0},{4,6},{6,4},{8,10},{10,8},{12,14},{14,12},{16,18},{18,... | collective-permute-start | bytes 1179656 | tf_op jit(solution)/shard_map/ppermute | solution.py:265
  200.2 36.4 %collective-permute-start.75 = (bf16[192,768]{1,0:T(8,128)(2,1)S(1)}, bf16[192,768]{1,0:T(8,128)(2,1)S(1)}, u32[]{:S(2)}, u32[]{:S(2)}) collective-permute-start(bf16[192,768]{1,0:T(8,128)(2,1)S(1)} %slice_bitcast_fusion.18), channel_id=1, source_target_pairs={{0,4},{2,6},{4,0},{6,2},{8,12},{10,14},{12,8},{14,10},{16,20},{18,... | collective-permute-start | bytes 884744 | tf_op jit(solution)/shard_map/ppermute | solution.py:403
  225.8 14.4 %collective-permute-start.62 = (bf16[2,208,768]{2,1,0:T(8,128)(2,1)S(1)}, bf16[2,208,768]{2,1,0:T(8,128)(2,1)S(1)}, u32[]{:S(2)}, u32[]{:S(2)}) collective-permute-start(bf16[2,208,768]{2,1,0:T(8,128)(2,1)S(1)} %get-tuple-element.193), channel_id=1, source_target_pairs={{0,2},{2,0},{4,6},{6,4},{8,10},{10,8},{12,14},{14,12},{16,18},{18,... | collective-permute-start | bytes 1916936 | tf_op jit(solution)/shard_map/ppermute | solution.py:265
  236.7 16.1 %collective-permute-start.79 = (bf16[192,768]{1,0:T(8,128)(2,1)S(1)}, bf16[192,768]{1,0:T(8,128)(2,1)S(1)}, u32[]{:S(2)}, u32[]{:S(2)}) collective-permute-start(bf16[192,768]{1,0:T(8,128)(2,1)S(1)} %fusion.11), channel_id=1, source_target_pairs={{0,8},{2,10},{4,12},{6,14},{8,16},{10,18},{12,20},{14,22},{16,24},... | collective-permute-start | bytes 884744 | tf_op jit(solution)/shard_map/ppermute | solution.py:399
  238.8 14.0 %collective-permute-start.76 = (bf16[192,768]{1,0:T(8,128)(2,1)S(1)}, bf16[192,768]{1,0:T(8,128)(2,1)S(1)}, u32[]{:S(2)}, u32[]{:S(2)}) collective-permute-start(bf16[192,768]{1,0:T(8,128)(2,1)S(1)} %slice_bitcast_fusion.23), channel_id=1, source_target_pairs={{0,4},{2,6},{4,0},{6,2},{8,12},{10,14},{12,8},{14,10},{16,20},{18,... | collective-permute-start | bytes 884744 | tf_op jit(solution)/shard_map/ppermute | solution.py:403
  240.2 13.8 %collective-permute-start.61 = (bf16[2,208,768]{2,1,0:T(8,128)(2,1)S(1)}, bf16[2,208,768]{2,1,0:T(8,128)(2,1)S(1)}, u32[]{:S(2)}, u32[]{:S(2)}) collective-permute-start(bf16[2,208,768]{2,1,0:T(8,128)(2,1)S(1)} %get-tuple-element.191), channel_id=1, source_target_pairs={{0,2},{2,0},{4,6},{6,4},{8,10},{10,8},{12,14},{14,12},{16,18},{18,... | collective-permute-start | bytes 1916936 | tf_op jit(solution)/shard_map/ppermute | solution.py:265
  245.1 24.9 %collective-permute-start.51 = (bf16[512,768]{1,0:T(8,128)(2,1)S(1)}, bf16[512,768]{1,0:T(8,128)(2,1)S(1)}, u32[]{:S(2)}, u32[]{:S(2)}) collective-permute-start(bf16[512,768]{1,0:T(8,128)(2,1)S(1)} %copy-done.41), channel_id=1, source_target_pairs={{2,1},{1,2},{6,5},{5,6},{10,9},{9,10},{14,13},{13,14},{18,17},{17,... | collective-permute-start | bytes 2359304 | tf_op jit(solution)/shard_map/ppermute | solution.py:277
  252.9 16.0 %collective-permute-start.80 = (bf16[192,768]{1,0:T(8,128)(2,1)S(1)}, bf16[192,768]{1,0:T(8,128)(2,1)S(1)}, u32[]{:S(2)}, u32[]{:S(2)}) collective-permute-start(bf16[192,768]{1,0:T(8,128)(2,1)S(1)} %add_add_fusion), channel_id=1, source_target_pairs={{0,8},{2,10},{4,12},{6,14},{8,16},{10,18},{12,20},{14,22},{16,24},... | collective-permute-start | bytes 884744 | tf_op jit(solution)/shard_map/ppermute | solution.py:399
  254.0 14.9 %collective-permute-start.77 = (bf16[192,768]{1,0:T(8,128)(2,1)S(1)}, bf16[192,768]{1,0:T(8,128)(2,1)S(1)}, u32[]{:S(2)}, u32[]{:S(2)}) collective-permute-start(bf16[192,768]{1,0:T(8,128)(2,1)S(1)} %slice_bitcast_fusion.19), channel_id=1, source_target_pairs={{0,4},{2,6},{4,0},{6,2},{8,12},{10,14},{12,8},{14,10},{16,20},{18,... | collective-permute-start | bytes 884744 | tf_op jit(solution)/shard_map/ppermute | solution.py:403
  258.6 26.0 %collective-permute-start.60 = (bf16[512,768]{1,0:T(8,128)(2,1)S(1)}, bf16[512,768]{1,0:T(8,128)(2,1)S(1)}, u32[]{:S(2)}, u32[]{:S(2)}) collective-permute-start(bf16[512,768]{1,0:T(8,128)(2,1)S(1)} %get-tuple-element.189), channel_id=1, source_target_pairs={{2,1},{1,2},{6,5},{5,6},{10,9},{9,10},{14,13},{13,14},{18,17},{17,... | collective-permute-start | bytes 2359304 | tf_op jit(solution)/shard_map/ppermute | solution.py:277
  269.9 14.1 %collective-permute-start.81 = (bf16[192,768]{1,0:T(8,128)(2,1)S(1)}, bf16[192,768]{1,0:T(8,128)(2,1)S(1)}, u32[]{:S(2)}, u32[]{:S(2)}) collective-permute-start(bf16[192,768]{1,0:T(8,128)(2,1)S(1)} %fusion.13), channel_id=1, source_target_pairs={{0,8},{2,10},{4,12},{6,14},{8,16},{10,18},{12,20},{14,22},{16,24},... | collective-permute-start | bytes 884744 | tf_op jit(solution)/shard_map/ppermute | solution.py:399
  (125 other events, 1268.8 us)

commit v4 on v3

--- a/solution.py
+++ b/solution.py
@@ -16,7 +16,7 @@
 F32 = jnp.float32
 BF16 = jnp.bfloat16
 MEGA = 1024 * 1024
-VMEM = {"pack": 60, "qkv": 28, "merge": 14, "ffn": 52, "close": 40, "unpack": 36}
+VMEM = {"pack": 60, "qkv": 28, "merge": 14, "ffn": 40, "close": 40, "unpack": 36}
 
 
 def layer_norm(values, gain, shift):
@@ -281,6 +281,32 @@
     return jnp.where(moves, exchange_rows(value, dp), value)
 
 
+def turn_rows(value, back):
+    pairs = []
+    for first in range(0, 32, 4):
+        steps = [(0, 2), (2, 3), (3, 1), (1, 0)]
+        pairs += [(first + b, first + a) if back else (first + a, first + b) for a, b in steps]
+    return lax.ppermute(value, ("dp", "seq"), pairs)
+
+
+def deal(value, turn, cross, core, moves):
+    size = value.shape[0] // 2
+    first, second = value[:size], value[size:]
+    base = jnp.where(moves, cross(first), first)
+    came = turn(second)
+    lead = core == 0
+    return jnp.concatenate([jnp.where(lead, base, came), jnp.where(lead, came, base)], axis=0)
+
+
+def undeal(value, turn, cross, core, moves):
+    size = value.shape[0] // 2
+    low, high = value[:size], value[size:]
+    lead = core == 0
+    base = jnp.where(lead, low, high)
+    came = turn(jnp.where(lead, high, low))
+    return jnp.concatenate([jnp.where(moves, cross(base), base), came], axis=0)
+
+
 def split_columns(value, width):
     return [value[:, at : at + width] for at in range(0, value.shape[1], width)]
 
@@ -345,7 +371,7 @@
         ),
         out_shape=out_shape,
         compiler_params=pltpu.CompilerParams(vmem_limit_bytes=VMEM[name] * MEGA),
-        cost_estimate=pl.CostEstimate(flops=flops // 10, bytes_accessed=moved // 10, transcendentals=0),
+        cost_estimate=pl.CostEstimate(flops=flops // 2, bytes_accessed=moved // 2, transcendentals=0),
         name=name,
     )(*scalars, *args)
 
@@ -426,8 +452,8 @@
     return slots
 
 
-def gather(head, tail, values, out_grad, moves):
-    z, x, y = Lane(shift_z, 2), Lane(swap_x, 2), Lane(swap_seq, 2)
+def gather(head, tail, values, out_grad, core, moves):
+    z, x, y = Lane(shift_z, 2), Lane(swap_x, 1), Lane(swap_seq, 2)
     head, tail = [head], [tail]
     head_x, tail_x, tail_y, tail_xy = [], [], [], []
     head.append(z(head[0]))
@@ -435,10 +461,12 @@
     tail_y.append(y(tail[0]))
     head.append(z(head[1]))
     tail_x.append(x(tail[0]))
-    new_values = y(values, exchange_rows)
+    turn = lambda value: y(value, functools.partial(turn_rows, back=False))
+    cross = lambda value: y(value, exchange_rows)
+    values = deal(values, turn, cross, core, moves)
     tail.append(z(tail[0]))
     head_x.append(x(head[1]))
-    new_grad = y(out_grad, exchange_rows)
+    out_grad = deal(out_grad, turn, cross, core, moves)
     head.append(z(head[2]))
     head_x.append(x(head[2]))
     tail_xy.append(y(tail_x[0]))
@@ -446,8 +474,7 @@
     head_x.append(x(head[3]))
     tail_y.append(y(tail[1]))
     tail_x.append(x(tail[1]))
-    values = after(jnp.where(moves, new_values, values), tail_y[1], tail_xy[0], tail[2])
-    out_grad = jnp.where(moves, new_grad, out_grad)
+    values = after(values, tail_xy[0], tail[2], tail_x[1])
     tail.append(z(tail[2]))
     tail_xy.append(y(tail_x[1]))
     tail_x.append(x(tail[2]))
@@ -480,6 +507,121 @@
     first = jnp.mean(inner, axis=-1, keepdims=True)
     second = jnp.mean(inner * shape, axis=-1, keepdims=True)
     return scale * (inner - first - shape * second)
+
+
+def balanced_kernel(extra, q_ref, k_ref, v_ref, rk_ref, rv_ref, o_ref, lse_ref, *, block):
+    masks = pair_masks()
+    index = extra[0]
+    first = (index == 0).astype(F32)
+    spot = pl.ds(pl.multiple_of(index * block, block), block)
+    keys = jnp.concatenate([k_ref[0:block, :], rk_ref[0:block, :], k_ref[block:, :]], axis=0)
+    values = jnp.concatenate([v_ref[0:block, :], rv_ref[0:block, :], v_ref[block:, :]], axis=0)
+    sums, totals = [[], []], [[], []]
+    for head in range(2):
+        mask = (masks[head] * 0.125).astype(BF16)
+        long = dot(keys, q_ref[block:, :] * mask, 1, 1)
+        last = causal(long[2 * block :], block)
+        long = long[: 2 * block]
+        short = causal(dot(keys[0:block], q_ref[0:block, :] * mask, 1, 1), block)
+        more = dot(rk_ref[spot, :], q_ref[spot, :] * mask, 1, 1)
+        peak = lambda value: jnp.max(value, axis=0, keepdims=True)
+        top_more = peak(more)
+        top_short = peak(short)
+        top_long = jnp.maximum(peak(long), peak(last))
+        joined_short = jnp.maximum(top_short, top_more)
+        joined_long = jnp.maximum(top_long, top_more)
+        at_first = index == 0
+        top_short = jnp.where(at_first, joined_short, top_short)
+        top_long = jnp.where(at_first, top_long, joined_long)
+        more = jnp.exp(more - jnp.where(at_first, top_short, top_long))
+        short = jnp.exp(short - top_short)
+        long = jnp.exp(long - top_long)
+        last = jnp.exp(last - top_long)
+        more_total = row_sum(more)
+        more_sum = dot(rv_ref[spot, :], more.astype(BF16), 0, 0)
+        short_total = row_sum(short) + first * more_total
+        long_total = row_sum(long) + row_sum(last) + (1.0 - first) * more_total
+        long_low = jnp.concatenate([long.astype(BF16), last.astype(BF16)], axis=0)
+        half = slice(64 * head, 64 * head + 64)
+        sums[0].append((dot(values[0:block], short.astype(BF16), 0, 0) + first * more_sum)[half] / short_total)
+        sums[1].append((dot(values, long_low, 0, 0) + (1.0 - first) * more_sum)[half] / long_total)
+        lse_ref[0, head : head + 1, 0:block] = top_short + jnp.log(short_total)
+        lse_ref[0, head : head + 1, block:] = top_long + jnp.log(long_total)
+    for part in range(2):
+        joined = jnp.concatenate(sums[part], axis=0)
+        o_ref[part * block : (part + 1) * block, :] = jnp.transpose(joined).astype(BF16)
+
+
+def balanced_back_kernel(
+    extra, q_ref, k_ref, v_ref, rk_ref, rv_ref, do_ref, o_ref, lse_ref,
+    dq_ref, dk_ref, dv_ref, rdk_ref, rdv_ref, *, block,
+):
+    masks = pair_masks()
+    index = extra[0]
+    first = (index == 0).astype(F32)
+    spot = pl.ds(pl.multiple_of(index * block, block), block)
+    keys = jnp.concatenate([k_ref[0:block, :], rk_ref[0:block, :], k_ref[block:, :]], axis=0)
+    values = jnp.concatenate([v_ref[0:block, :], rv_ref[0:block, :], v_ref[block:, :]], axis=0)
+    product = jnp.transpose(do_ref[...].astype(F32) * o_ref[...].astype(F32))
+    key_grads, value_grads, query_grads = [0.0] * 3, [0.0] * 3, [0.0] * 3
+    for head in range(2):
+        mask = masks[head].astype(BF16)
+        scaled = (masks[head] * 0.125).astype(BF16)
+        delta = row_sum(product[64 * head : 64 * head + 64])
+        lse = lse_ref[0, head : head + 1, :]
+        pick = lambda row: jnp.where(index == 0, row[:, :block], row[:, block:])
+        sets = (
+            (slice(block, None), keys, values, lse[:, block:], delta[:, block:], 3),
+            (slice(0, block), keys[0:block], values[0:block], lse[:, :block], delta[:, :block], 1),
+            (spot, rk_ref[spot, :], rv_ref[spot, :], pick(lse), pick(delta), 0),
+        )
+        for at, (rows, near_keys, near_values, norm, shift, blocks) in enumerate(sets):
+            query = q_ref[rows, :] * scaled
+            grad = do_ref[rows, :] * mask
+            scores = dot(near_keys, query, 1, 1)
+            if blocks:
+                last = causal(scores[(blocks - 1) * block :], block)
+                scores = jnp.concatenate([scores[: (blocks - 1) * block], last], axis=0) if blocks > 1 else last
+            probs = jnp.exp(scores - norm)
+            score_grad = (probs * (dot(near_values, grad, 1, 1) - shift)).astype(BF16)
+            value_grads[at] += dot(probs.astype(BF16), grad, 1, 0)
+            key_grads[at] += dot(score_grad, query, 1, 0)
+            query_grads[at] += dot(near_keys * scaled, score_grad, 0, 0)
+    turned = jnp.concatenate([query_grads[1] + first * query_grads[2], query_grads[0] + (1.0 - first) * query_grads[2]], axis=1)
+    dq_ref[...] = jnp.transpose(turned).astype(BF16)
+    for out, far, grads in ((dk_ref, rdk_ref, key_grads), (dv_ref, rdv_ref, value_grads)):
+        out[0:block, :] = (grads[0][0:block] + grads[1]).astype(BF16)
+        out[block:, :] = grads[0][2 * block :].astype(BF16)
+        far[0:block, :] = (grads[0][block : 2 * block] + first * grads[2]).astype(BF16)
+        far[block:, :] = ((1.0 - first) * grads[2]).astype(BF16)
+
+
+def balanced(extra, args, first, pairs, cost):
+    queries = args[0]
+    rows, width = queries.shape
+    total = width // 128
+    column = lambda offset: pl.BlockSpec((rows, 128), lambda h, c: (0, h + offset))
+    line = pl.BlockSpec((1, 2, rows), lambda h, c: (h, 0, 0))
+    half = jax.ShapeDtypeStruct((rows, pairs * 128), BF16)
+    in_specs = [column(first), column(first), column(first + total), column(first), column(first + total)]
+    operands = [queries, args[1], args[1], args[2], args[2]]
+    if len(args) == 3:
+        body, out_specs = balanced_kernel, [column(0), line]
+        out_shape = [half, jax.ShapeDtypeStruct((pairs, 2, rows), F32)]
+    else:
+        body, out_specs, out_shape = balanced_back_kernel, [column(0)] * 5, [half] * 5
+        in_specs += [column(first), column(0), line]
+        operands += list(args[3:])
+    return pl.pallas_call(
+        functools.partial(body, block=rows // 2),
+        grid_spec=pltpu.PrefetchScalarGridSpec(
+            num_scalar_prefetch=1, grid=(pairs,), in_specs=in_specs, out_specs=out_specs
+        ),
+        out_shape=out_shape,
+        compiler_params=pltpu.CompilerParams(vmem_limit_bytes=16 * MEGA),
+        cost_estimate=pl.CostEstimate(flops=cost, bytes_accessed=cost // 1000, transcendentals=0),
+        name="attend" if len(args) == 3 else "attend_back",
+    )(extra, *operands)
 
 
 def qkv_kernel(place, x_ref, *refs):
@@ -620,7 +762,7 @@
                     copies.append(
                         pltpu.make_async_copy(
                             grads.at[source, half if kind == 0 else 1 - half],
-                            out.at[kind, column],
+                            out.at[column, kind],
                             out_sems.at[len(copies)],
                         )
                     )
@@ -688,9 +830,9 @@
         if at == 0:
             dt[...] = join(q1, q2)
         elif at == 1:
-            dt[...] = (join(k1, k2) + join(far_k1, far_k2).astype(F32)).astype(BF16)
+            dt[...] = (join(k1, k2).astype(F32) + join(far_k1, far_k2).astype(F32)).astype(BF16)
         else:
-            dt[...] = (join(v1, v2) + join(far_v1, far_v2).astype(F32)).astype(BF16)
+            dt[...] = (join(v1, v2).astype(F32) + join(far_v1, far_v2).astype(F32)).astype(BF16)
         if at != 1:
             g96[2:3, (at // 2) * width : (at // 2 + 1) * width] = row_sum(dt[...].astype(F32))
         weight = packed[:, at * part : (at + 1) * part, :].reshape(width, width)
@@ -750,10 +892,10 @@
 def unpack_kernel(slots, place, head, head_far, tail, tail_far, *outs):
     part, width = outs[4].shape[1:]
     total = head[...].astype(F32) + head_far[...].astype(F32)
-    near, far = tail[...].astype(F32), tail_far[...].astype(F32)
-    first = place[1] == 0
-    shrink = jnp.where(first, near, far)
-    expand = jnp.where(first, far, near)
+    own = tail[0].astype(F32) + tail_far[1].astype(F32)
+    other = tail[1].astype(F32) + tail_far[0].astype(F32)
+    lead = place[1] == 0
+    shrink, expand = jnp.where(lead, own, other), jnp.where(lead, other, own)
     for row, number in enumerate(SMALL):
         out = outs[number]
         size = out.shape[1]
@@ -781,56 +923,62 @@
 
 def per_device_fast(inputs, cotangent, tie_slots, *masters):
     length, count, width = inputs.shape
-    block = math.gcd(length, 256)
     index, half = lax.axis_index("dp"), lax.axis_index("seq")
     place = jnp.stack([index, half]).astype(jnp.int32)
     core = index % 2
     moves = core != half
     head, tail = pack(tie_slots, place, masters)
     head_pieces, tail_pieces, values, rest = gather(
-        head, tail, inputs.reshape(length, width), cotangent.reshape(length, width), moves
+        head, tail, inputs.reshape(length, width), cotangent.reshape(length, width), core, moves
     )
     head_pieces = head_pieces + [swap_cores(piece, 16) for piece in head_pieces]
     packed, normed, queries, near, v48, v96, v192 = qkv(place, values, head_pieces)
     remote = swap_cores(near, 16)
-    far_count = core.astype(jnp.int32).reshape(1)
+    extra = (1 - core).astype(jnp.int32).reshape(1)
     half_pairs = width // 256
-    queries = after(queries, tail_pieces[4], tail_pieces[3])
+    queries = after(queries, tail_pieces[6], tail_pieces[3])
     attended, lse = [None, None], [None, None]
-    attended[0], lse[0] = attend(far_count, queries, near, remote, block, 0, half_pairs)
+    attended[0], lse[0] = balanced(extra, (queries, near, remote), 0, half_pairs, 1000000)
     queries = after(queries, attended[0])
-    attended[1], lse[1] = attend(far_count, queries, near, remote, block, half_pairs, half_pairs)
+    attended[1], lse[1] = balanced(extra, (queries, near, remote), half_pairs, half_pairs, 1000000)
     tail_other, out_grad = rest(attended[0], attended[1])
     middle, second = merge(values, attended, packed, v48)
     late = lambda pieces, first: [
         swap_cores(after(piece, attended[1]) if number >= first else piece, 16) for number, piece in enumerate(pieces)
     ]
-    tail_pieces = tail_pieces + late(tail_pieces, 8)
-    tail_other = tail_other + late(tail_other, 4)
+    tail_pieces = tail_pieces + late(tail_pieces, 4)
+    tail_other = tail_other + late(tail_other, 5)
     (output, middle_grad, branch_grad, attended_grad, g48, g192), tail_parts = ffn(
         place, tail_pieces[:8] + tail_other[:8] + tail_pieces[8:] + tail_other[8:],
         middle, second, out_grad, packed, v48, v192,
     )
-    z, x, y = Lane(shift_z, 2), Lane(swap_x, 2), Lane(swap_seq, 4)
+    z, x, y = Lane(shift_z, 2), Lane(swap_x, 3), Lane(swap_seq, 2)
+    turn = lambda value: y(value, functools.partial(turn_rows, back=True))
+    cross = lambda value: y(value, exchange_rows)
     came = [swap_cores(send, 16) for send in tail_parts[1::2]]
     kept = [keep + other for keep, other in zip(tail_parts[0::2], came)]
+    tail_half, tail_part, head_part = {}, {}, {}
     attended_grad = after(attended_grad, *kept)
-    tail_y = {order: y(kept[order][1]) for order in (1, 2, 3, 0)}
+    tail_half[1] = kept[1][1, 0] + y(kept[1][1, 1])
+    tail_half[2] = kept[2][1, 0] + y(kept[2][1, 1])
+    tail_half[3] = kept[3][1, 0] + y(kept[3][1, 1])
+    tail_half[0] = kept[0][1, 0] + y(kept[0][1, 1])
+    output = undeal(output, turn, cross, core, moves)
     grads = []
     for part in range(2):
         if part:
-            attended_grad = after(attended_grad, tail_y[1], grads[0])
-        query_grad, key_grad, value_grad, far_key, far_value = attend_back(
-            far_count, queries, near, remote, attended_grad, attended[part], lse[part], block, part * half_pairs
+            attended_grad = after(attended_grad, grads[0], tail_half[1])
+        query_grad, key_grad, value_grad, far_key, far_value = balanced(
+            extra, (queries, near, remote, attended_grad, attended[part], lse[part]), part * half_pairs, half_pairs, 1000000
         )
         grads += [query_grad, key_grad, value_grad, swap_cores(far_key, 16), swap_cores(far_value, 16)]
-    tail_x = {}
-    tail_kept = {}
-    for order in (1, 2, 3, 0):
-        both = kept[order][0] + tail_y[order]
-        tail_kept[order] = both[0]
-        tail_x[order] = both[1]
-    middle_grad = after(middle_grad, tail_x[2], tail_kept[2])
+    tail_part[1] = jnp.stack([kept[1][0, 0] + x(tail_half[1]), kept[1][0, 1]])
+    tail_run = z(tail_part[1])
+    tail_part[2] = jnp.stack([kept[2][0, 0] + x(tail_half[2]), kept[2][0, 1]])
+    tail_run = z(tail_part[2] + tail_run)
+    tail_part[3] = jnp.stack([kept[3][0, 0] + x(tail_half[3]), kept[3][0, 1]])
+    tail_run = z(tail_part[3] + tail_run)
+    middle_grad = after(middle_grad, tail_half[3])
     input_grad, head_parts = close(
         place,
         [
@@ -839,18 +987,18 @@
     )
     came = [swap_cores(send, 16) for send in head_parts[1::2]]
     head_kept = [keep + other for keep, other in zip(head_parts[0::2], came)]
-    tail_sum = head_sum = None
-    new_output = y(output, exchange_rows)
-    new_input_grad = y(input_grad, exchange_rows)
-    for order in (1, 2, 3, 0):
-        came = x(tail_x[order])
-        part = tail_kept[order] + came
-        tail_sum = part if tail_sum is None else part + z(tail_sum)
-        came = x(head_kept[order][1])
-        part = head_kept[order][0] + came
-        head_sum = part if head_sum is None else part + z(head_sum)
-    output = jnp.where(moves, new_output, output)
-    input_grad = jnp.where(moves, new_input_grad, input_grad).astype(F32)
+    input_grad = undeal(input_grad, turn, cross, core, moves)
+    head_part[1] = head_kept[1][0] + x(head_kept[1][1])
+    head_run = z(head_part[1])
+    tail_part[0] = jnp.stack([kept[0][0, 0] + x(tail_half[0]), kept[0][0, 1]])
+    tail_sum = tail_part[0] + tail_run
+    head_part[2] = head_kept[2][0] + x(head_kept[2][1])
+    head_run = z(head_part[2] + head_run)
+    head_part[3] = head_kept[3][0] + x(head_kept[3][1])
+    head_run = z(head_part[3] + head_run)
+    head_part[0] = head_kept[0][0] + x(head_kept[0][1])
+    head_sum = head_part[0] + head_run
+    input_grad = input_grad.astype(F32)
     grads = unpack(
         tie_slots, place, [head_sum, y(head_sum), tail_sum, y(tail_sum)], masters
     )

time: 301 us -> 287 us (0.953)
  starting transfers between devices: 68.8 us -> 57 us
    ppermute x37, starting transfers between devices: 25.2 us -> 10.7 us  [swap_cores(): return lax.ppermute(value, 'dp', pairs_of(count, lambda index: index ^ 1))]
    ppermute x16, waiting for transfers between devices: 34.7 us -> 39.7 us  [swap_x(): return lax.ppermute(value, 'dp', pairs_of(16, lambda index: index ^ 2))]
    ppermute x0 -> x4, starting transfers between devices: none -> 4.37 us  [turn_rows(): return lax.ppermute(value, ('dp', 'seq'), pairs)]
    ppermute x14, starting transfers between devices: 13.4 us -> 9.65 us  [swap_seq(): return lax.ppermute(value, 'seq', [(0, 1), (1, 0)])]
    unnamed x149 -> x85, local copies, waits for them, and re-layouts: 14.6 us -> 12.3 us
  transfers between devices with their start and end apart: 83 -> 87, of which waited for: 31 -> 33; matrix products, arithmetic and copies ran while one was open for 4% -> 4% of each run, Pallas kernels for 11% -> 12%
where the time goes in v4:
time: 287 us; the launch traced here: 282 us
  waiting for transfers between devices  127 us (44%)
  Pallas kernels  75.1 us (26%)
  starting transfers between devices  57 us (20%)
  local copies, waits for them, and re-layouts  13.4 us (5%)
  other arithmetic  7.62 us (3%)
    pallas_call x6, Pallas kernels, kernel_call(): pl.pallas_call(body, grid_spec=pltpu.PrefetchScalarGridSpec(num_scalar_pr...  52.2 us
    ppermute x12, waiting for transfers between devices, shift_z(): lax.ppermute(value, 'dp', pairs_of(16, lambda index: (index + 4) % 16))  46.4 us
    ppermute x16, waiting for transfers between devices, swap_x(): return lax.ppermute(value, 'dp', pairs_of(16, lambda index: index ^ 2))  39.7 us
    ppermute x14, waiting for transfers between devices, swap_seq(): return lax.ppermute(value, 'seq', [(0, 1), (1, 0)])  36.5 us
    pallas_call x4, Pallas kernels, balanced(): pl.pallas_call(functools.partial(body, block=rows // 2), grid_spec=pltpu....  22.9 us
    ppermute x16, starting transfers between devices, swap_x(): return lax.ppermute(value, 'dp', pairs_of(16, lambda index: index ^ 2))  17.9 us
    unnamed x85, local copies, waits for them, and re-layouts  12.3 us
    ppermute x12, starting transfers between devices, shift_z(): lax.ppermute(value, 'dp', pairs_of(16, lambda index: (index + 4) % 16))  10.8 us
  transfers between devices with their start and end apart: 87, of which 33 were waited for; matrix products, arithmetic and copies ran while one was open for 4% of the time, Pallas kernels for 12%

profile of v4, /device:TPU:0, one launch (start us, length us, event | category | flops | bytes accessed | tf_op | source)
XLA Modules:
  0.0 282.4 jit_solution(15389888800845477568)
XLA Ops:
  1.2 3.3 %pack.1 = (bf16[208,768]{1,0:T(8,128)(2,1)}, bf16[192,768]{1,0:T(8,128)(2,1)}) custom-call(s32[12]{0:T(128)} %slots.3, s32[2]{0:T(128)} %pad_add_fusion.place, f32[2,48]{1,0:T(2,128)} %refs_0_.1, f32[2,48]{1,0:T(2,128)} %refs_1_.1, f32[2,48,2304]{2,1,0:T(8,128)} %refs_2_.1, f32[2,96]{1,0:T(2,128)} %refs_3_.1, f32[2,48,768]{2,1,0:T(8,128)} %refs_4_.1, ...), custom_call_target="tpu_custom_call" | custom-call | bytes 1916928 | tf_op jit(solution)/shard_map/pack/pallas_call | solution.py:363
  4.5 2.9 %collective-permute-start = (bf16[208,768]{1,0:T(8,128)(2,1)}, bf16[208,768]{1,0:T(8,128)(2,1)S(1)}, u32[]{:S(2)}, u32[]{:S(2)}) collective-permute-start(bf16[208,768]{1,0:T(8,128)(2,1)} %get-tuple-element.127.refs_0_), channel_id=1, source_target_pairs={{0,4},{2,6},{4,0},{6,2},{8,12},{10,14},{12,8},{14,10},{16,20},{18,... | collective-permute-start | bytes 958472 | tf_op jit(solution)/shard_map/ppermute | solution.py:429
  9.0 6.2 %collective-permute-done.refs_1_ = bf16[208,768]{1,0:T(8,128)(2,1)S(1)} collective-permute-done((bf16[208,768]{1,0:T(8,128)(2,1)}, bf16[208,768]{1,0:T(8,128)(2,1)S(1)}, u32[]{:S(2)}, u32[]{:S(2)}) %collective-permute-start) | collective-permute-done | bytes 319520 | tf_op jit(solution)/shard_map/ppermute | solution.py:429
  20.0 3.7 %collective-permute-done.1.refs_1_ = bf16[192,768]{1,0:T(8,128)(2,1)} collective-permute-done((bf16[192,768]{1,0:T(8,128)(2,1)}, bf16[192,768]{1,0:T(8,128)(2,1)}, u32[]{:S(2)}, u32[]{:S(2)}) %collective-permute-start.1) | collective-permute-done | bytes 294944 | tf_op jit(solution)/shard_map/ppermute | solution.py:429
  35.7 4.6 %collective-permute-done.5.refs_6_ = bf16[208,768]{1,0:T(8,128)(2,1)S(1)} collective-permute-done((bf16[208,768]{1,0:T(8,128)(2,1)S(1)}, bf16[208,768]{1,0:T(8,128)(2,1)S(1)}, u32[]{:S(2)}, u32[]{:S(2)}) %collective-permute-start.5) | collective-permute-done | bytes 319520 | tf_op jit(solution)/shard_map/ppermute | solution.py:425
  41.4 3.0 %collective-permute-done.3.refs_2_ = bf16[192,768]{1,0:T(8,128)(2,1)} collective-permute-done((bf16[192,768]{1,0:T(8,128)(2,1)S(1)}, bf16[192,768]{1,0:T(8,128)(2,1)}, u32[]{:S(2)}, u32[]{:S(2)}) %collective-permute-start.3) | collective-permute-done | bytes 294944 | tf_op jit(solution)/shard_map/ppermute | solution.py:425
  46.6 2.4 collective-permute-done.8.refs_7_
  51.2 7.3 %collective-permute-done.10.refs_4_ = bf16[192,768]{1,0:T(8,128)(2,1)} collective-permute-done((bf16[192,768]{1,0:T(8,128)(2,1)}, bf16[192,768]{1,0:T(8,128)(2,1)}, u32[]{:S(2)}, u32[]{:S(2)}) %collective-permute-start.10) | collective-permute-done | bytes 294944 | tf_op jit(solution)/shard_map/ppermute | solution.py:425
  59.9 2.4 broadcast_select_fusion.5
  63.9 4.9 %qkv.1 = (bf16[16,208,768]{2,1,0:T(8,128)(2,1)S(1)}, bf16[512,768]{1,0:T(8,128)(2,1)S(1)}, bf16[512,768]{1,0:T(8,128)(2,1)S(1)}, bf16[512,1536]{1,0:T(8,128)(2,1...) custom-call(s32[2]{0:T(128)S(1)} %copy-done.17, ...), custom_call_target="tpu_custom_call" | custom-call | flops 905969664 | bytes 5898240 | tf_op jit(solution)/shard_map/qkv/pallas_call | solution.py:363
  77.5 6.8 %collective-permute-done.20.refs_10_ = bf16[192,768]{1,0:T(8,128)(2,1)S(1)} collective-permute-done((bf16[192,768]{1,0:T(8,128)(2,1)}, bf16[192,768]{1,0:T(8,128)(2,1)S(1)}, u32[]{:S(2)}, u32[]{:S(2)}) %collective-permute-start.20) | collective-permute-done | bytes 294944 | tf_op jit(solution)/shard_map/ppermute | solution.py:269
  87.6 4.9 %attend.2 = (bf16[512,384]{1,0:T(8,128)(2,1)S(1)}, f32[3,2,512]{2,1,0:T(2,128)S(1)}) custom-call(s32[1]{0:T(128)} %bitcast.6.extra, bf16[512,768]{1,0:T(8,128)(2,1)S(1)} %copy-done.2, bf16[512,1536]{1,0:T(8,128)(2,1)S(1)} %get-tuple-element.149.k_ref.v_ref, bf16[512,1536]{1,0:T(8,128)(2,1)S(1)} %get-tuple-element.149.k_ref.v_ref, ...), custom_call_target="tpu_custom_call" | custom-call | flops 1000000 | bytes 1000 | tf_op jit(solution)/shard_map/attend/pallas_call | solution.py:615
  94.3 2.7 collective-permute-done.22.refs_12_
  97.0 4.9 %attend.3 = (bf16[512,384]{1,0:T(8,128)(2,1)S(1)}, f32[3,2,512]{2,1,0:T(2,128)S(1)}) custom-call(s32[1]{0:T(128)} %bitcast.6.extra, bf16[512,768]{1,0:T(8,128)(2,1)S(1)} %copy-done.2, bf16[512,1536]{1,0:T(8,128)(2,1)S(1)} %get-tuple-element.149.k_ref.v_ref, bf16[512,1536]{1,0:T(8,128)(2,1)S(1)} %get-tuple-element.149.k_ref.v_ref, ...), custom_call_target="tpu_custom_call" | custom-call | flops 1000000 | bytes 1000 | tf_op jit(solution)/shard_map/attend/pallas_call | solution.py:615
  105.7 7.4 %collective-permute-done.33.refs_14_ = bf16[192,768]{1,0:T(8,128)(2,1)S(1)} collective-permute-done((bf16[192,768]{1,0:T(8,128)(2,1)}, bf16[192,768]{1,0:T(8,128)(2,1)S(1)}, u32[]{:S(2)}, u32[]{:S(2)}) %collective-permute-start.33) | collective-permute-done | bytes 294944 | tf_op jit(solution)/shard_map/ppermute | solution.py:269
  113.1 5.5 %collective-permute-done.34.refs_15_ = bf16[192,768]{1,0:T(8,128)(2,1)S(1)} collective-permute-done((bf16[192,768]{1,0:T(8,128)(2,1)S(1)}, bf16[192,768]{1,0:T(8,128)(2,1)S(1)}, u32[]{:S(2)}, u32[]{:S(2)}) %collective-permute-start.34) | collective-permute-done | bytes 294944 | tf_op jit(solution)/shard_map/ppermute | solution.py:269
  123.1 29.4 %ffn.1 = (bf16[512,768]{1,0:T(8,128)(2,1)S(1)}, f32[512,768]{1,0:T(8,128)}, bf16[512,768]{1,0:T(8,128)(2,1)S(1)}, bf16[512,768]{1,0:T(8,128)(2,1)S(1)}, f32[8,76...) custom-call(s32[2]{0:T(128)S(1)} %copy-done.17, ...), custom_call_target="tpu_custom_call" | custom-call | flops 7247757312 | bytes 9437184 | tf_op jit(solution)/shard_map/ffn/pallas_call | solution.py:363
  162.1 6.5 %attend_back.2 = (bf16[512,384]{1,0:T(8,128)(2,1)S(1)}, bf16[512,384]{1,0:T(8,128)(2,1)S(1)}, bf16[512,384]{1,0:T(8,128)(2,1)S(1)}, bf16[512,384]{1,0:T(8,128)(2,1)S(1)}, bf16[512,384]{1,0:T(8,128)(2,1)S(1)}) custom-call(s32[1]{0:T(128)} %bitcast.6.extra, bf16[512,768]{1,0:T(8,128)(2,1)S(1)} %copy-done.3, ...), custom_call_target="tpu_custom_call" | custom-call | flops 1000000 | bytes 1000 | tf_op jit(solution)/shard_map/attend_back/pallas_call | solution.py:615
  172.3 6.6 %attend_back.3 = (bf16[512,384]{1,0:T(8,128)(2,1)S(1)}, bf16[512,384]{1,0:T(8,128)(2,1)S(1)}, bf16[512,384]{1,0:T(8,128)(2,1)S(1)}, bf16[512,384]{1,0:T(8,128)(2,1)S(1)}, bf16[512,384]{1,0:T(8,128)(2,1)S(1)}) custom-call(s32[1]{0:T(128)} %bitcast.6.extra, bf16[512,768]{1,0:T(8,128)(2,1)S(1)} %copy-done.3, ...), custom_call_target="tpu_custom_call" | custom-call | flops 1000000 | bytes 1000 | tf_op jit(solution)/shard_map/attend_back/pallas_call | solution.py:615
  180.2 4.6 %collective-permute-done.59 = bf16[192,768]{1,0:T(8,128)(2,1)S(1)} collective-permute-done((bf16[192,768]{1,0:T(8,128)(2,1)S(1)}, bf16[192,768]{1,0:T(8,128)(2,1)S(1)}, u32[]{:S(2)}, u32[]{:S(2)}) %collective-permute-start.59) | collective-permute-done | bytes 294944 | tf_op jit(solution)/shard_map/ppermute | solution.py:269
  191.5 10.7 %close.1 = (bf16[512,768]{1,0:T(8,128)(2,1)S(1)}, bf16[2,208,768]{2,1,0:T(8,128)(2,1)S(1)}, bf16[2,208,768]{2,1,0:T(8,128)(2,1)S(1)}, bf16[2,208,768]{2,1,0:T(8,...) custom-call(s32[2]{0:T(128)S(1)} %copy-done.17, ...), custom_call_target="tpu_custom_call" | custom-call | flops 2113929216 | bytes 5898240 | tf_op jit(solution)/shard_map/close/pallas_call | solution.py:363
  210.2 7.8 %collective-permute-done.74 = bf16[208,768]{1,0:T(8,128)(2,1)S(1)} collective-permute-done((bf16[208,768]{1,0:T(8,128)(2,1)S(1)}, bf16[208,768]{1,0:T(8,128)(2,1)S(1)}, u32[]{:S(2)}, u32[]{:S(2)}) %collective-permute-start.74) | collective-permute-done | bytes 319520 | tf_op jit(solution)/shard_map/ppermute | solution.py:429
  218.0 7.3 %collective-permute-done.80 = bf16[2,192,768]{2,1,0:T(8,128)(2,1)S(1)} collective-permute-done((bf16[2,192,768]{2,1,0:T(8,128)(2,1)S(1)}, bf16[2,192,768]{2,1,0:T(8,128)(2,1)S(1)}, u32[]{:S(2)}, u32[]{:S(2)}) %collective-permute-start.80) | collective-permute-done | bytes 589856 | tf_op jit(solution)/shard_map/ppermute | solution.py:425
  228.0 5.9 %collective-permute-done.78 = bf16[208,768]{1,0:T(8,128)(2,1)S(1)} collective-permute-done((bf16[208,768]{1,0:T(8,128)(2,1)S(1)}, bf16[208,768]{1,0:T(8,128)(2,1)S(1)}, u32[]{:S(2)}, u32[]{:S(2)}) %collective-permute-start.78) | collective-permute-done | bytes 319520 | tf_op jit(solution)/shard_map/ppermute | solution.py:429
  233.9 15.7 %collective-permute-done.81 = bf16[208,768]{1,0:T(8,128)(2,1)S(1)} collective-permute-done((bf16[208,768]{1,0:T(8,128)(2,1)S(1)}, bf16[208,768]{1,0:T(8,128)(2,1)S(1)}, u32[]{:S(2)}, u32[]{:S(2)}) %collective-permute-start.81) | collective-permute-done | bytes 319520 | tf_op jit(solution)/shard_map/ppermute | solution.py:425
  252.1 8.0 %collective-permute-done.75 = bf16[208,768]{1,0:T(8,128)(2,1)S(1)} collective-permute-done((bf16[208,768]{1,0:T(8,128)(2,1)S(1)}, bf16[208,768]{1,0:T(8,128)(2,1)S(1)}, u32[]{:S(2)}, u32[]{:S(2)}) %collective-permute-start.75) | collective-permute-done | bytes 319520 | tf_op jit(solution)/shard_map/ppermute | solution.py:429
  261.3 2.5 collective-permute-done.70
  263.8 5.1 %collective-permute-done.84 = bf16[208,768]{1,0:T(8,128)(2,1)S(1)} collective-permute-done((bf16[208,768]{1,0:T(8,128)(2,1)S(1)}, bf16[208,768]{1,0:T(8,128)(2,1)S(1)}, u32[]{:S(2)}, u32[]{:S(2)}) %collective-permute-start.84) | collective-permute-done | bytes 319520 | tf_op jit(solution)/shard_map/ppermute | solution.py:425
  269.3 2.8 copy.29
  272.0 3.8 %collective-permute-done.86.tail_far = bf16[2,192,768]{2,1,0:T(8,128)(2,1)S(1)} collective-permute-done((bf16[2,192,768]{2,1,0:T(8,128)(2,1)S(1)}, bf16[2,192,768]{2,1,0:T(8,128)(2,1)S(1)}, u32[]{:S(2)}, u32[]{:S(2)}) %collective-permute-start.86) | collective-permute-done | bytes 589856 | tf_op jit(solution)/shard_map/ppermute | solution.py:269
  275.9 3.4 %collective-permute-done.85.head_far = bf16[208,768]{1,0:T(8,128)(2,1)S(1)} collective-permute-done((bf16[208,768]{1,0:T(8,128)(2,1)S(1)}, bf16[208,768]{1,0:T(8,128)(2,1)S(1)}, u32[]{:S(2)}, u32[]{:S(2)}) %collective-permute-start.85) | collective-permute-done | bytes 319520 | tf_op jit(solution)/shard_map/ppermute | solution.py:269
  279.3 2.7 unpack.1
  (282 shorter events, 84.8 us)
Async XLA Ops:
  26.7 14.1 %collective-permute-start.18 = (bf16[256,768]{1,0:T(8,128)(2,1)S(1)}, bf16[256,768]{1,0:T(8,128)(2,1)}, u32[]{:S(2)}, u32[]{:S(2)}) collective-permute-start(bf16[256,768]{1,0:T(8,128)(2,1)S(1)} %get-tuple-element.141), channel_id=1, source_target_pairs={{0,2},{2,3},{3,1},{1,0},{4,6},{6,7},{7,5},{5,4},{8,10},{10,11},{11... | collective-permute-start | bytes 1179656 | tf_op jit(solution)/shard_map/ppermute | solution.py:289
  28.9 11.4 %collective-permute-start.5 = (bf16[208,768]{1,0:T(8,128)(2,1)S(1)}, bf16[208,768]{1,0:T(8,128)(2,1)S(1)}, u32[]{:S(2)}, u32[]{:S(2)}) collective-permute-start(bf16[208,768]{1,0:T(8,128)(2,1)S(1)} %collective-permute-done.4.refs_4_), channel_id=1, source_target_pairs={{0,8},{2,10},{4,12},{6,14},{8,16},{10,18},{12,20},{14,22},{16,24},... | collective-permute-start | bytes 958472 | tf_op jit(solution)/shard_map/ppermute | solution.py:425
  33.4 13.1 %collective-permute-start.16 = (bf16[256,768]{1,0:T(8,128)(2,1)S(1)}, bf16[256,768]{1,0:T(8,128)(2,1)S(1)}, u32[]{:S(2)}, u32[]{:S(2)}) collective-permute-start(bf16[256,768]{1,0:T(8,128)(2,1)S(1)} %get-tuple-element.139), channel_id=1, source_target_pairs={{2,1},{1,2},{6,5},{5,6},{10,9},{9,10},{14,13},{13,14},{18,17},{17,... | collective-permute-start | bytes 1179656 | tf_op jit(solution)/shard_map/ppermute | solution.py:277
  44.4 15.0 %collective-permute-start.19 = (bf16[256,768]{1,0:T(8,128)(2,1)}, bf16[256,768]{1,0:T(8,128)(2,1)}, u32[]{:S(2)}, u32[]{:S(2)}) collective-permute-start(bf16[256,768]{1,0:T(8,128)(2,1)} %get-tuple-element.142), channel_id=1, source_target_pairs={{0,2},{2,3},{3,1},{1,0},{4,6},{6,7},{7,5},{5,4},{8,10},{10,11},{11... | collective-permute-start | bytes 1179656 | tf_op jit(solution)/shard_map/ppermute | solution.py:289
  51.2 11.3 %collective-permute-start.27 = (bf16[208,768]{1,0:T(8,128)(2,1)S(1)}, bf16[208,768]{1,0:T(8,128)(2,1)S(1)}, u32[]{:S(2)}, u32[]{:S(2)}) collective-permute-start(bf16[208,768]{1,0:T(8,128)(2,1)S(1)} %collective-permute-done.4.refs_4_), channel_id=1, source_target_pairs={{0,2},{2,0},{4,6},{6,4},{8,10},{10,8},{12,14},{14,12},{16,18},{18,... | collective-permute-start | bytes 958472 | tf_op jit(solution)/shard_map/ppermute | solution.py:265
  73.5 13.0 %collective-permute-start.31 = (bf16[512,1536]{1,0:T(8,128)(2,1)S(1)}, bf16[512,1536]{1,0:T(8,128)(2,1)S(1)}, u32[]{:S(2)}, u32[]{:S(2)}) collective-permute-start(bf16[512,1536]{1,0:T(8,128)(2,1)S(1)} %get-tuple-element.149.k_ref.v_ref), channel_id=1, source_target_pairs={{0,2},{2,0},{4,6},{6,4},{8,10},{10,8},{12,14},{14,12},{16,18},{18,... | collective-permute-start | bytes 4718600 | tf_op jit(solution)/shard_map/ppermute | solution.py:265
  74.7 11.2 %collective-permute-start.12 = (bf16[192,768]{1,0:T(8,128)(2,1)}, bf16[192,768]{1,0:T(8,128)(2,1)}, u32[]{:S(2)}, u32[]{:S(2)}) collective-permute-start(bf16[192,768]{1,0:T(8,128)(2,1)} %collective-permute-done.10.refs_4_), channel_id=1, source_target_pairs={{0,8},{2,10},{4,12},{6,14},{8,16},{10,18},{12,20},{14,22},{16,24},... | collective-permute-start | bytes 884744 | tf_op jit(solution)/shard_map/ppermute | solution.py:425
  76.6 16.0 %collective-permute-start.21 = (bf16[192,768]{1,0:T(8,128)(2,1)}, bf16[192,768]{1,0:T(8,128)(2,1)}, u32[]{:S(2)}, u32[]{:S(2)}) collective-permute-start(bf16[192,768]{1,0:T(8,128)(2,1)} %collective-permute-done.9.refs_3_), channel_id=1, source_target_pairs={{0,1},{1,0},{2,3},{3,2},{4,5},{5,4},{6,7},{7,6},{8,9},{9,8},{10,11... | collective-permute-start | bytes 884744 | tf_op jit(solution)/shard_map/ppermute | solution.py:269
  84.2 12.7 %collective-permute-start.22 = (bf16[192,768]{1,0:T(8,128)(2,1)}, bf16[192,768]{1,0:T(8,128)(2,1)}, u32[]{:S(2)}, u32[]{:S(2)}) collective-permute-start(bf16[192,768]{1,0:T(8,128)(2,1)} %collective-permute-done.10.refs_4_), channel_id=1, source_target_pairs={{0,1},{1,0},{2,3},{3,2},{4,5},{5,4},{6,7},{7,6},{8,9},{9,8},{10,11... | collective-permute-start | bytes 884744 | tf_op jit(solution)/shard_map/ppermute | solution.py:269
  86.0 16.0 %collective-permute-start.13 = (bf16[192,768]{1,0:T(8,128)(2,1)}, bf16[192,768]{1,0:T(8,128)(2,1)S(1)}, u32[]{:S(2)}, u32[]{:S(2)}) collective-permute-start(bf16[192,768]{1,0:T(8,128)(2,1)} %collective-permute-done.12.refs_6_), channel_id=1, source_target_pairs={{0,4},{2,6},{4,0},{6,2},{8,12},{10,14},{12,8},{14,10},{16,20},{18,... | collective-permute-start | bytes 884744 | tf_op jit(solution)/shard_map/ppermute | solution.py:429
  103.7 14.9 %collective-permute-start.34 = (bf16[192,768]{1,0:T(8,128)(2,1)S(1)}, bf16[192,768]{1,0:T(8,128)(2,1)S(1)}, u32[]{:S(2)}, u32[]{:S(2)}) collective-permute-start(bf16[192,768]{1,0:T(8,128)(2,1)S(1)} %collective-permute-done.13.refs_7_), channel_id=1, source_target_pairs={{0,1},{1,0},{2,3},{3,2},{4,5},{5,4},{6,7},{7,6},{8,9},{9,8},{10,11... | collective-permute-start | bytes 884744 | tf_op jit(solution)/shard_map/ppermute | solution.py:269
  105.1 13.5 %collective-permute-start.47 = (bf16[192,768]{1,0:T(8,128)(2,1)}, bf16[192,768]{1,0:T(8,128)(2,1)S(1)}, u32[]{:S(2)}, u32[]{:S(2)}) collective-permute-start(bf16[192,768]{1,0:T(8,128)(2,1)} %collective-permute-done.22.refs_12_), channel_id=1, source_target_pairs={{0,2},{2,0},{4,6},{6,4},{8,10},{10,8},{12,14},{14,12},{16,18},{18,... | collective-permute-start | bytes 884744 | tf_op jit(solution)/shard_map/ppermute | solution.py:265
  105.1 14.0 %collective-permute-start.38 = (bf16[192,768]{1,0:T(8,128)(2,1)}, bf16[192,768]{1,0:T(8,128)(2,1)S(1)}, u32[]{:S(2)}, u32[]{:S(2)}) collective-permute-start(bf16[192,768]{1,0:T(8,128)(2,1)} %collective-permute-done.9.refs_3_), channel_id=1, source_target_pairs={{0,2},{2,0},{4,6},{6,4},{8,10},{10,8},{12,14},{14,12},{16,18},{18,... | collective-permute-start | bytes 884744 | tf_op jit(solution)/shard_map/ppermute | solution.py:265
  105.6 13.6 %collective-permute-start.46 = (bf16[192,768]{1,0:T(8,128)(2,1)}, bf16[192,768]{1,0:T(8,128)(2,1)S(1)}, u32[]{:S(2)}, u32[]{:S(2)}) collective-permute-start(bf16[192,768]{1,0:T(8,128)(2,1)} %collective-permute-done.21.refs_11_), channel_id=1, source_target_pairs={{0,2},{2,0},{4,6},{6,4},{8,10},{10,8},{12,14},{14,12},{16,18},{18,... | collective-permute-start | bytes 884744 | tf_op jit(solution)/shard_map/ppermute | solution.py:265
  156.0 13.3 %collective-permute-start.53 = (bf16[192,768]{1,0:T(8,128)(2,1)S(1)}, bf16[192,768]{1,0:T(8,128)(2,1)S(1)}, u32[]{:S(2)}, u32[]{:S(2)}) collective-permute-start(bf16[192,768]{1,0:T(8,128)(2,1)S(1)} %get-tuple-element.261), channel_id=1, source_target_pairs={{0,1},{1,0},{2,3},{3,2},{4,5},{5,4},{6,7},{7,6},{8,9},{9,8},{10,11... | collective-permute-start | bytes 884744 | tf_op jit(solution)/shard_map/ppermute | solution.py:269
  159.4 12.3 %collective-permute-start.58 = (bf16[192,768]{1,0:T(8,128)(2,1)S(1)}, bf16[192,768]{1,0:T(8,128)(2,1)S(1)}, u32[]{:S(2)}, u32[]{:S(2)}) collective-permute-start(bf16[192,768]{1,0:T(8,128)(2,1)S(1)} %get-tuple-element.263), channel_id=1, source_target_pairs={{0,1},{1,0},{2,3},{3,2},{4,5},{5,4},{6,7},{7,6},{8,9},{9,8},{10,11... | collective-permute-start | bytes 884744 | tf_op jit(solution)/shard_map/ppermute | solution.py:269
  168.7 20.0 %collective-permute-start.61 = (bf16[512,384]{1,0:T(8,128)(2,1)S(1)}, bf16[512,384]{1,0:T(8,128)(2,1)S(1)}, u32[]{:S(2)}, u32[]{:S(2)}) collective-permute-start(bf16[512,384]{1,0:T(8,128)(2,1)S(1)} %get-tuple-element.190), channel_id=1, source_target_pairs={{0,2},{2,0},{4,6},{6,4},{8,10},{10,8},{12,14},{14,12},{16,18},{18,... | collective-permute-start | bytes 1179656 | tf_op jit(solution)/shard_map/ppermute | solution.py:265
  169.1 20.2 %collective-permute-start.62 = (bf16[512,384]{1,0:T(8,128)(2,1)S(1)}, bf16[512,384]{1,0:T(8,128)(2,1)S(1)}, u32[]{:S(2)}, u32[]{:S(2)}) collective-permute-start(bf16[512,384]{1,0:T(8,128)(2,1)S(1)} %get-tuple-element.191), channel_id=1, source_target_pairs={{0,2},{2,0},{4,6},{6,4},{8,10},{10,8},{12,14},{14,12},{16,18},{18,... | collective-permute-start | bytes 1179656 | tf_op jit(solution)/shard_map/ppermute | solution.py:265
  171.6 13.2 %collective-permute-start.59 = (bf16[192,768]{1,0:T(8,128)(2,1)S(1)}, bf16[192,768]{1,0:T(8,128)(2,1)S(1)}, u32[]{:S(2)}, u32[]{:S(2)}) collective-permute-start(bf16[192,768]{1,0:T(8,128)(2,1)S(1)} %get-tuple-element.181), channel_id=1, source_target_pairs={{0,1},{1,0},{2,3},{3,2},{4,5},{5,4},{6,7},{7,6},{8,9},{9,8},{10,11... | collective-permute-start | bytes 884744 | tf_op jit(solution)/shard_map/ppermute | solution.py:269
  187.1 21.4 %collective-permute-start.77 = (bf16[192,768]{1,0:T(8,128)(2,1)S(1)}, bf16[192,768]{1,0:T(8,128)(2,1)S(1)}, u32[]{:S(2)}, u32[]{:S(2)}) collective-permute-start(bf16[192,768]{1,0:T(8,128)(2,1)S(1)} %fusion.17), channel_id=1, source_target_pairs={{0,4},{2,6},{4,0},{6,2},{8,12},{10,14},{12,8},{14,10},{16,20},{18,... | collective-permute-start | bytes 884744 | tf_op jit(solution)/shard_map/ppermute | solution.py:429
  188.6 38.2 %collective-permute-start.69 = (bf16[192,768]{1,0:T(8,128)(2,1)S(1)}, bf16[192,768]{1,0:T(8,128)(2,1)S(1)}, u32[]{:S(2)}, u32[]{:S(2)}) collective-permute-start(bf16[192,768]{1,0:T(8,128)(2,1)S(1)} %fusion.16), channel_id=1, source_target_pairs={{0,4},{2,6},{4,0},{6,2},{8,12},{10,14},{12,8},{14,10},{16,20},{18,... | collective-permute-start | bytes 884744 | tf_op jit(solution)/shard_map/ppermute | solution.py:429
  189.3 37.7 %collective-permute-start.55 = (bf16[256,768]{1,0:T(8,128)(2,1)S(1)}, bf16[256,768]{1,0:T(8,128)(2,1)S(1)}, u32[]{:S(2)}, u32[]{:S(2)}) collective-permute-start(bf16[256,768]{1,0:T(8,128)(2,1)S(1)} %get-tuple-element.176), channel_id=1, source_target_pairs={{2,1},{1,2},{6,5},{5,6},{10,9},{9,10},{14,13},{13,14},{18,17},{17,... | collective-permute-start | bytes 1179656 | tf_op jit(solution)/shard_map/ppermute | solution.py:277
  190.0 16.4 %collective-permute-start.79 = (bf16[2,192,768]{2,1,0:T(8,128)(2,1)S(1)}, bf16[2,192,768]{2,1,0:T(8,128)(2,1)S(1)}, u32[]{:S(2)}, u32[]{:S(2)}) collective-permute-start(bf16[2,192,768]{2,1,0:T(8,128)(2,1)S(1)} %pad_maximum_fusion.2), channel_id=1, source_target_pairs={{0,8},{2,10},{4,12},{6,14},{8,16},{10,18},{12,20},{14,22},{16,24},... | collective-permute-start | bytes 1769480 | tf_op jit(solution)/shard_map/ppermute | solution.py:425
  208.2 17.1 %collective-permute-start.80 = (bf16[2,192,768]{2,1,0:T(8,128)(2,1)S(1)}, bf16[2,192,768]{2,1,0:T(8,128)(2,1)S(1)}, u32[]{:S(2)}, u32[]{:S(2)}) collective-permute-start(bf16[2,192,768]{2,1,0:T(8,128)(2,1)S(1)} %maximum_add_fusion), channel_id=1, source_target_pairs={{0,8},{2,10},{4,12},{6,14},{8,16},{10,18},{12,20},{14,22},{16,24},... | collective-permute-start | bytes 1769480 | tf_op jit(solution)/shard_map/ppermute | solution.py:425
  210.0 16.8 %collective-permute-start.60 = (bf16[256,768]{1,0:T(8,128)(2,1)S(1)}, bf16[256,768]{1,0:T(8,128)(2,1)S(1)}, u32[]{:S(2)}, u32[]{:S(2)}) collective-permute-start(bf16[256,768]{1,0:T(8,128)(2,1)S(1)} %copy-done.39), channel_id=1, source_target_pairs={{2,0},{3,2},{1,3},{0,1},{6,4},{7,6},{5,7},{4,5},{10,8},{11,10},{9,... | collective-permute-start | bytes 1179656 | tf_op jit(solution)/shard_map/ppermute | solution.py:289
  226.8 23.5 %collective-permute-start.82 = (bf16[2,192,768]{2,1,0:T(8,128)(2,1)S(1)}, bf16[2,192,768]{2,1,0:T(8,128)(2,1)S(1)}, u32[]{:S(2)}, u32[]{:S(2)}) collective-permute-start(bf16[2,192,768]{2,1,0:T(8,128)(2,1)S(1)} %maximum_add_fusion.1), channel_id=1, source_target_pairs={{0,8},{2,10},{4,12},{6,14},{8,16},{10,18},{12,20},{14,22},{16,24},... | collective-permute-start | bytes 1769480 | tf_op jit(solution)/shard_map/ppermute | solution.py:425
  226.9 22.7 %collective-permute-start.81 = (bf16[208,768]{1,0:T(8,128)(2,1)S(1)}, bf16[208,768]{1,0:T(8,128)(2,1)S(1)}, u32[]{:S(2)}, u32[]{:S(2)}) collective-permute-start(bf16[208,768]{1,0:T(8,128)(2,1)S(1)} %fusion), channel_id=1, source_target_pairs={{0,8},{2,10},{4,12},{6,14},{8,16},{10,18},{12,20},{14,22},{16,24},... | collective-permute-start | bytes 958472 | tf_op jit(solution)/shard_map/ppermute | solution.py:425
  227.0 23.4 %collective-permute-start.67 = (bf16[2,208,768]{2,1,0:T(8,128)(2,1)S(1)}, bf16[2,208,768]{2,1,0:T(8,128)(2,1)S(1)}, u32[]{:S(2)}, u32[]{:S(2)}) collective-permute-start(bf16[2,208,768]{2,1,0:T(8,128)(2,1)S(1)} %get-tuple-element.208), channel_id=1, source_target_pairs={{0,2},{2,0},{4,6},{6,4},{8,10},{10,8},{12,14},{14,12},{16,18},{18,... | collective-permute-start | bytes 1916936 | tf_op jit(solution)/shard_map/ppermute | solution.py:265
  227.1 34.1 %collective-permute-start.65 = (bf16[256,768]{1,0:T(8,128)(2,1)S(1)}, bf16[256,768]{1,0:T(8,128)(2,1)S(1)}, u32[]{:S(2)}, u32[]{:S(2)}) collective-permute-start(bf16[256,768]{1,0:T(8,128)(2,1)S(1)} %get-tuple-element.205), channel_id=1, source_target_pairs={{2,1},{1,2},{6,5},{5,6},{10,9},{9,10},{14,13},{13,14},{18,17},{17,... | collective-permute-start | bytes 1179656 | tf_op jit(solution)/shard_map/ppermute | solution.py:277
  233.9 35.1 %collective-permute-start.66 = (bf16[256,768]{1,0:T(8,128)(2,1)S(1)}, bf16[256,768]{1,0:T(8,128)(2,1)S(1)}, u32[]{:S(2)}, u32[]{:S(2)}) collective-permute-start(bf16[256,768]{1,0:T(8,128)(2,1)S(1)} %get-tuple-element.206), channel_id=1, source_target_pairs={{2,0},{3,2},{1,3},{0,1},{6,4},{7,6},{5,7},{4,5},{10,8},{11,10},{9,... | collective-permute-start | bytes 1179656 | tf_op jit(solution)/shard_map/ppermute | solution.py:289
  250.6 13.2 %collective-permute-start.70 = (bf16[208,768]{1,0:T(8,128)(2,1)S(1)}, bf16[208,768]{1,0:T(8,128)(2,1)S(1)}, u32[]{:S(2)}, u32[]{:S(2)}) collective-permute-start(bf16[208,768]{1,0:T(8,128)(2,1)S(1)} %slice_bitcast_fusion.10), channel_id=1, source_target_pairs={{0,4},{2,6},{4,0},{6,2},{8,12},{10,14},{12,8},{14,10},{16,20},{18,... | collective-permute-start | bytes 958472 | tf_op jit(solution)/shard_map/ppermute | solution.py:429
  261.2 14.6 %collective-permute-start.86 = (bf16[2,192,768]{2,1,0:T(8,128)(2,1)S(1)}, bf16[2,192,768]{2,1,0:T(8,128)(2,1)S(1)}, u32[]{:S(2)}, u32[]{:S(2)}) collective-permute-start(bf16[2,192,768]{2,1,0:T(8,128)(2,1)S(1)} %maximum_add_fusion.2.tail), channel_id=1, source_target_pairs={{0,1},{1,0},{2,3},{3,2},{4,5},{5,4},{6,7},{7,6},{8,9},{9,8},{10,11... | collective-permute-start | bytes 1769480 | tf_op jit(solution)/shard_map/ppermute | solution.py:269
  (97 other events, 784.4 us)

commit v5 on v4

--- a/solution.py
+++ b/solution.py
@@ -16,7 +16,7 @@
 F32 = jnp.float32
 BF16 = jnp.bfloat16
 MEGA = 1024 * 1024
-VMEM = {"pack": 60, "qkv": 28, "merge": 14, "ffn": 40, "close": 40, "unpack": 36}
+VMEM = {"pack": 60, "qkv": 28, "merge": 14, "ffn": 40, "close": 26, "unpack": 36}
 
 
 def layer_norm(values, gain, shift):
@@ -963,7 +963,6 @@
     tail_half[2] = kept[2][1, 0] + y(kept[2][1, 1])
     tail_half[3] = kept[3][1, 0] + y(kept[3][1, 1])
     tail_half[0] = kept[0][1, 0] + y(kept[0][1, 1])
-    output = undeal(output, turn, cross, core, moves)
     grads = []
     for part in range(2):
         if part:
@@ -973,12 +972,10 @@
         )
         grads += [query_grad, key_grad, value_grad, swap_cores(far_key, 16), swap_cores(far_value, 16)]
     tail_part[1] = jnp.stack([kept[1][0, 0] + x(tail_half[1]), kept[1][0, 1]])
-    tail_run = z(tail_part[1])
+    tail_run = tail_run1 = z(tail_part[1])
     tail_part[2] = jnp.stack([kept[2][0, 0] + x(tail_half[2]), kept[2][0, 1]])
-    tail_run = z(tail_part[2] + tail_run)
-    tail_part[3] = jnp.stack([kept[3][0, 0] + x(tail_half[3]), kept[3][0, 1]])
-    tail_run = z(tail_part[3] + tail_run)
-    middle_grad = after(middle_grad, tail_half[3])
+    tail_run = tail_run2 = z(tail_part[2] + tail_run)
+    middle_grad = after(middle_grad, tail_run1)
     input_grad, head_parts = close(
         place,
         [
@@ -987,15 +984,18 @@
     )
     came = [swap_cores(send, 16) for send in head_parts[1::2]]
     head_kept = [keep + other for keep, other in zip(head_parts[0::2], came)]
+    output = undeal(output, turn, cross, core, moves)
     input_grad = undeal(input_grad, turn, cross, core, moves)
     head_part[1] = head_kept[1][0] + x(head_kept[1][1])
-    head_run = z(head_part[1])
+    head_run = head_run1 = z(head_part[1])
+    tail_part[3] = jnp.stack([kept[3][0, 0] + x(tail_half[3]), kept[3][0, 1]])
+    tail_run = tail_run3 = z(tail_part[3] + tail_run)
+    head_part[2] = head_kept[2][0] + x(head_kept[2][1])
+    head_run = head_run2 = z(head_part[2] + head_run)
     tail_part[0] = jnp.stack([kept[0][0, 0] + x(tail_half[0]), kept[0][0, 1]])
     tail_sum = tail_part[0] + tail_run
-    head_part[2] = head_kept[2][0] + x(head_kept[2][1])
-    head_run = z(head_part[2] + head_run)
     head_part[3] = head_kept[3][0] + x(head_kept[3][1])
-    head_run = z(head_part[3] + head_run)
+    head_run = head_run3 = z(head_part[3] + head_run)
     head_part[0] = head_kept[0][0] + x(head_kept[0][1])
     head_sum = head_part[0] + head_run
     input_grad = input_grad.astype(F32)

time: 287 us -> 278 us (0.969)
  waiting for transfers between devices: 127 us -> 115 us
  starting transfers between devices: 57 us -> 62 us
  Pallas kernels: 75.1 us -> 72.2 us
    ppermute x16, waiting for transfers between devices: 39.7 us -> 26.4 us  [swap_x(): return lax.ppermute(value, 'dp', pairs_of(16, lambda index: index ^ 2))]
    ppermute x4, starting transfers between devices: 4.37 us -> 8.97 us  [turn_rows(): return lax.ppermute(value, ('dp', 'seq'), pairs)]
    ppermute x14, starting transfers between devices: 9.65 us -> 14.1 us  [swap_seq(): return lax.ppermute(value, 'seq', [(0, 1), (1, 0)])]
    ppermute x14, waiting for transfers between devices: 36.5 us -> 40.3 us  [swap_seq(): return lax.ppermute(value, 'seq', [(0, 1), (1, 0)])]
    ppermute x16, starting transfers between devices: 17.9 us -> 14.9 us  [swap_x(): return lax.ppermute(value, 'dp', pairs_of(16, lambda index: index ^ 2))]
    unnamed x85 -> x87, local copies, waits for them, and re-layouts: 12.3 us -> 12.7 us
  transfers between devices with their start and end apart: 87 -> 87, of which waited for: 33 -> 29; matrix products, arithmetic and copies ran while one was open for 4% -> 4% of each run, Pallas kernels for 12% -> 12%
where the time goes in v5:
time: 278 us; the launch traced here: 274 us
  waiting for transfers between devices  115 us (41%)
  Pallas kernels  72.2 us (26%)
  starting transfers between devices  62 us (22%)
  local copies, waits for them, and re-layouts  13.8 us (5%)
  other arithmetic  8.29 us (3%)
    pallas_call x6, Pallas kernels, kernel_call(): pl.pallas_call(body, grid_spec=pltpu.PrefetchScalarGridSpec(num_scalar_pr...  49.3 us
    ppermute x12, waiting for transfers between devices, shift_z(): lax.ppermute(value, 'dp', pairs_of(16, lambda index: (index + 4) % 16))  44.8 us
    ppermute x14, waiting for transfers between devices, swap_seq(): return lax.ppermute(value, 'seq', [(0, 1), (1, 0)])  40.3 us
    ppermute x16, waiting for transfers between devices, swap_x(): return lax.ppermute(value, 'dp', pairs_of(16, lambda index: index ^ 2))  26.4 us
    pallas_call x4, Pallas kernels, balanced(): pl.pallas_call(functools.partial(body, block=rows // 2), grid_spec=pltpu....  22.9 us
    ppermute x16, starting transfers between devices, swap_x(): return lax.ppermute(value, 'dp', pairs_of(16, lambda index: index ^ 2))  14.9 us
    ppermute x14, starting transfers between devices, swap_seq(): return lax.ppermute(value, 'seq', [(0, 1), (1, 0)])  14.1 us
    unnamed x87, local copies, waits for them, and re-layouts  12.7 us
  transfers between devices with their start and end apart: 87, of which 29 were waited for; matrix products, arithmetic and copies ran while one was open for 4% of the time, Pallas kernels for 12%

profile of v5, /device:TPU:0, one launch (start us, length us, event | category | flops | bytes accessed | tf_op | source)
XLA Modules:
  0.0 273.7 jit_solution(16512644932271760233)
XLA Ops:
  1.2 3.3 %pack.1 = (bf16[208,768]{1,0:T(8,128)(2,1)}, bf16[192,768]{1,0:T(8,128)(2,1)}) custom-call(s32[12]{0:T(128)} %slots.3, s32[2]{0:T(128)} %pad_add_fusion.place, f32[2,48]{1,0:T(2,128)} %refs_0_.1, f32[2,48]{1,0:T(2,128)} %refs_1_.1, f32[2,48,2304]{2,1,0:T(8,128)} %refs_2_.1, f32[2,96]{1,0:T(2,128)} %refs_3_.1, f32[2,48,768]{2,1,0:T(8,128)} %refs_4_.1, ...), custom_call_target="tpu_custom_call" | custom-call | bytes 1916928 | tf_op jit(solution)/shard_map/pack/pallas_call | solution.py:363
  4.5 2.9 %collective-permute-start = (bf16[208,768]{1,0:T(8,128)(2,1)}, bf16[208,768]{1,0:T(8,128)(2,1)S(1)}, u32[]{:S(2)}, u32[]{:S(2)}) collective-permute-start(bf16[208,768]{1,0:T(8,128)(2,1)} %get-tuple-element.127.refs_0_), channel_id=1, source_target_pairs={{0,4},{2,6},{4,0},{6,2},{8,12},{10,14},{12,8},{14,10},{16,20},{18,... | collective-permute-start | bytes 958472 | tf_op jit(solution)/shard_map/ppermute | solution.py:429
  9.0 6.2 %collective-permute-done.refs_1_ = bf16[208,768]{1,0:T(8,128)(2,1)S(1)} collective-permute-done((bf16[208,768]{1,0:T(8,128)(2,1)}, bf16[208,768]{1,0:T(8,128)(2,1)S(1)}, u32[]{:S(2)}, u32[]{:S(2)}) %collective-permute-start) | collective-permute-done | bytes 319520 | tf_op jit(solution)/shard_map/ppermute | solution.py:429
  20.0 3.7 %collective-permute-done.1.refs_1_ = bf16[192,768]{1,0:T(8,128)(2,1)} collective-permute-done((bf16[192,768]{1,0:T(8,128)(2,1)}, bf16[192,768]{1,0:T(8,128)(2,1)}, u32[]{:S(2)}, u32[]{:S(2)}) %collective-permute-start.1) | collective-permute-done | bytes 294944 | tf_op jit(solution)/shard_map/ppermute | solution.py:429
  35.7 4.6 %collective-permute-done.5.refs_6_ = bf16[208,768]{1,0:T(8,128)(2,1)S(1)} collective-permute-done((bf16[208,768]{1,0:T(8,128)(2,1)S(1)}, bf16[208,768]{1,0:T(8,128)(2,1)S(1)}, u32[]{:S(2)}, u32[]{:S(2)}) %collective-permute-start.5) | collective-permute-done | bytes 319520 | tf_op jit(solution)/shard_map/ppermute | solution.py:425
  41.4 3.0 %collective-permute-done.3.refs_2_ = bf16[192,768]{1,0:T(8,128)(2,1)} collective-permute-done((bf16[192,768]{1,0:T(8,128)(2,1)S(1)}, bf16[192,768]{1,0:T(8,128)(2,1)}, u32[]{:S(2)}, u32[]{:S(2)}) %collective-permute-start.3) | collective-permute-done | bytes 294944 | tf_op jit(solution)/shard_map/ppermute | solution.py:425
  46.6 2.4 collective-permute-done.8.refs_7_
  51.2 7.3 %collective-permute-done.10.refs_4_ = bf16[192,768]{1,0:T(8,128)(2,1)} collective-permute-done((bf16[192,768]{1,0:T(8,128)(2,1)}, bf16[192,768]{1,0:T(8,128)(2,1)}, u32[]{:S(2)}, u32[]{:S(2)}) %collective-permute-start.10) | collective-permute-done | bytes 294944 | tf_op jit(solution)/shard_map/ppermute | solution.py:425
  59.9 2.4 broadcast_select_fusion.5
  63.9 4.9 %qkv.1 = (bf16[16,208,768]{2,1,0:T(8,128)(2,1)S(1)}, bf16[512,768]{1,0:T(8,128)(2,1)S(1)}, bf16[512,768]{1,0:T(8,128)(2,1)S(1)}, bf16[512,1536]{1,0:T(8,128)(2,1...) custom-call(s32[2]{0:T(128)S(1)} %copy-done.18, ...), custom_call_target="tpu_custom_call" | custom-call | flops 905969664 | bytes 5898240 | tf_op jit(solution)/shard_map/qkv/pallas_call | solution.py:363
  68.8 2.3 copy-done
  77.5 6.8 %collective-permute-done.20.refs_10_ = bf16[192,768]{1,0:T(8,128)(2,1)S(1)} collective-permute-done((bf16[192,768]{1,0:T(8,128)(2,1)}, bf16[192,768]{1,0:T(8,128)(2,1)S(1)}, u32[]{:S(2)}, u32[]{:S(2)}) %collective-permute-start.20) | collective-permute-done | bytes 294944 | tf_op jit(solution)/shard_map/ppermute | solution.py:269
  87.7 4.9 %attend.2 = (bf16[512,384]{1,0:T(8,128)(2,1)S(1)}, f32[3,2,512]{2,1,0:T(2,128)S(1)}) custom-call(s32[1]{0:T(128)} %bitcast.6.extra, bf16[512,768]{1,0:T(8,128)(2,1)S(1)} %copy-done.2, bf16[512,1536]{1,0:T(8,128)(2,1)S(1)} %get-tuple-element.149.k_ref.v_ref, bf16[512,1536]{1,0:T(8,128)(2,1)S(1)} %get-tuple-element.149.k_ref.v_ref, ...), custom_call_target="tpu_custom_call" | custom-call | flops 1000000 | bytes 1000 | tf_op jit(solution)/shard_map/attend/pallas_call | solution.py:615
  94.4 2.7 collective-permute-done.22.refs_12_
  97.0 4.9 %attend.3 = (bf16[512,384]{1,0:T(8,128)(2,1)S(1)}, f32[3,2,512]{2,1,0:T(2,128)S(1)}) custom-call(s32[1]{0:T(128)} %bitcast.6.extra, bf16[512,768]{1,0:T(8,128)(2,1)S(1)} %copy-done.2, bf16[512,1536]{1,0:T(8,128)(2,1)S(1)} %get-tuple-element.149.k_ref.v_ref, bf16[512,1536]{1,0:T(8,128)(2,1)S(1)} %get-tuple-element.149.k_ref.v_ref, ...), custom_call_target="tpu_custom_call" | custom-call | flops 1000000 | bytes 1000 | tf_op jit(solution)/shard_map/attend/pallas_call | solution.py:615
  105.7 7.4 %collective-permute-done.33.refs_14_ = bf16[192,768]{1,0:T(8,128)(2,1)S(1)} collective-permute-done((bf16[192,768]{1,0:T(8,128)(2,1)}, bf16[192,768]{1,0:T(8,128)(2,1)S(1)}, u32[]{:S(2)}, u32[]{:S(2)}) %collective-permute-start.33) | collective-permute-done | bytes 294944 | tf_op jit(solution)/shard_map/ppermute | solution.py:269
  113.2 5.5 %collective-permute-done.34.refs_15_ = bf16[192,768]{1,0:T(8,128)(2,1)S(1)} collective-permute-done((bf16[192,768]{1,0:T(8,128)(2,1)S(1)}, bf16[192,768]{1,0:T(8,128)(2,1)S(1)}, u32[]{:S(2)}, u32[]{:S(2)}) %collective-permute-start.34) | collective-permute-done | bytes 294944 | tf_op jit(solution)/shard_map/ppermute | solution.py:269
  123.1 29.4 %ffn.1 = (bf16[512,768]{1,0:T(8,128)(2,1)S(1)}, f32[512,768]{1,0:T(8,128)}, bf16[512,768]{1,0:T(8,128)(2,1)S(1)}, bf16[512,768]{1,0:T(8,128)(2,1)S(1)}, f32[8,76...) custom-call(s32[2]{0:T(128)S(1)} %copy-done.18, ...), custom_call_target="tpu_custom_call" | custom-call | flops 7247757312 | bytes 9437184 | tf_op jit(solution)/shard_map/ffn/pallas_call | solution.py:363
  161.7 5.5 %collective-permute-done.58 = bf16[192,768]{1,0:T(8,128)(2,1)S(1)} collective-permute-done((bf16[192,768]{1,0:T(8,128)(2,1)S(1)}, bf16[192,768]{1,0:T(8,128)(2,1)S(1)}, u32[]{:S(2)}, u32[]{:S(2)}) %collective-permute-start.58) | collective-permute-done | bytes 294944 | tf_op jit(solution)/shard_map/ppermute | solution.py:269
  167.6 5.4 %collective-permute-done.53 = bf16[192,768]{1,0:T(8,128)(2,1)S(1)} collective-permute-done((bf16[192,768]{1,0:T(8,128)(2,1)S(1)}, bf16[192,768]{1,0:T(8,128)(2,1)S(1)}, u32[]{:S(2)}, u32[]{:S(2)}) %collective-permute-start.53) | collective-permute-done | bytes 294944 | tf_op jit(solution)/shard_map/ppermute | solution.py:269
  176.5 6.5 %attend_back.2 = (bf16[512,384]{1,0:T(8,128)(2,1)S(1)}, bf16[512,384]{1,0:T(8,128)(2,1)S(1)}, bf16[512,384]{1,0:T(8,128)(2,1)S(1)}, bf16[512,384]{1,0:T(8,128)(2,1)S(1)}, bf16[512,384]{1,0:T(8,128)(2,1)S(1)}) custom-call(s32[1]{0:T(128)} %bitcast.6.extra, bf16[512,768]{1,0:T(8,128)(2,1)S(1)} %copy-done.3, ...), custom_call_target="tpu_custom_call" | custom-call | flops 1000000 | bytes 1000 | tf_op jit(solution)/shard_map/attend_back/pallas_call | solution.py:615
  183.1 6.5 %attend_back.3 = (bf16[512,384]{1,0:T(8,128)(2,1)S(1)}, bf16[512,384]{1,0:T(8,128)(2,1)S(1)}, bf16[512,384]{1,0:T(8,128)(2,1)S(1)}, bf16[512,384]{1,0:T(8,128)(2,1)S(1)}, bf16[512,384]{1,0:T(8,128)(2,1)S(1)}) custom-call(s32[1]{0:T(128)} %bitcast.6.extra, bf16[512,768]{1,0:T(8,128)(2,1)S(1)} %copy-done.3, ...), custom_call_target="tpu_custom_call" | custom-call | flops 1000000 | bytes 1000 | tf_op jit(solution)/shard_map/attend_back/pallas_call | solution.py:615
  194.0 2.4 collective-permute-start.60
  196.5 7.9 %close.1 = (bf16[512,768]{1,0:T(8,128)(2,1)S(1)}, bf16[2,208,768]{2,1,0:T(8,128)(2,1)S(1)}, bf16[2,208,768]{2,1,0:T(8,128)(2,1)S(1)}, bf16[2,208,768]{2,1,0:T(8,...) custom-call(s32[2]{0:T(128)S(1)} %copy-done.18, ...), custom_call_target="tpu_custom_call" | custom-call | flops 2113929216 | bytes 5898240 | tf_op jit(solution)/shard_map/close/pallas_call | solution.py:363
  210.5 6.7 %collective-permute-done.78 = bf16[208,768]{1,0:T(8,128)(2,1)S(1)} collective-permute-done((bf16[208,768]{1,0:T(8,128)(2,1)S(1)}, bf16[208,768]{1,0:T(8,128)(2,1)S(1)}, u32[]{:S(2)}, u32[]{:S(2)}) %collective-permute-start.78) | collective-permute-done | bytes 319520 | tf_op jit(solution)/shard_map/ppermute | solution.py:429
  217.9 5.3 %collective-permute-done.81 = bf16[2,192,768]{2,1,0:T(8,128)(2,1)S(1)} collective-permute-done((bf16[2,192,768]{2,1,0:T(8,128)(2,1)S(1)}, bf16[2,192,768]{2,1,0:T(8,128)(2,1)S(1)}, u32[]{:S(2)}, u32[]{:S(2)}) %collective-permute-start.81) | collective-permute-done | bytes 589856 | tf_op jit(solution)/shard_map/ppermute | solution.py:425
  223.9 6.1 %collective-permute-done.79 = bf16[208,768]{1,0:T(8,128)(2,1)S(1)} collective-permute-done((bf16[208,768]{1,0:T(8,128)(2,1)S(1)}, bf16[208,768]{1,0:T(8,128)(2,1)S(1)}, u32[]{:S(2)}, u32[]{:S(2)}) %collective-permute-start.79) | collective-permute-done | bytes 319520 | tf_op jit(solution)/shard_map/ppermute | solution.py:425
  233.7 14.9 %collective-permute-done.80 = bf16[208,768]{1,0:T(8,128)(2,1)S(1)} collective-permute-done((bf16[208,768]{1,0:T(8,128)(2,1)S(1)}, bf16[208,768]{1,0:T(8,128)(2,1)S(1)}, u32[]{:S(2)}, u32[]{:S(2)}) %collective-permute-start.80) | collective-permute-done | bytes 319520 | tf_op jit(solution)/shard_map/ppermute | solution.py:425
  250.8 6.4 %collective-permute-done.73 = bf16[208,768]{1,0:T(8,128)(2,1)S(1)} collective-permute-done((bf16[208,768]{1,0:T(8,128)(2,1)S(1)}, bf16[208,768]{1,0:T(8,128)(2,1)S(1)}, u32[]{:S(2)}, u32[]{:S(2)}) %collective-permute-start.73) | collective-permute-done | bytes 319520 | tf_op jit(solution)/shard_map/ppermute | solution.py:429
  261.5 2.8 %copy.29 = f32[512,1,768]{2,1,0:T(1,128)} copy(f32[512,1,768]{2,0,1:T(8,128)S(1)} %maximum_convert_fusion) | data formatting | bytes 3145728
  265.5 5.0 %collective-permute-done.84.head_far = bf16[208,768]{1,0:T(8,128)(2,1)S(1)} collective-permute-done((bf16[208,768]{1,0:T(8,128)(2,1)S(1)}, bf16[208,768]{1,0:T(8,128)(2,1)S(1)}, u32[]{:S(2)}, u32[]{:S(2)}) %collective-permute-start.84) | collective-permute-done | bytes 319520 | tf_op jit(solution)/shard_map/ppermute | solution.py:269
  270.6 2.7 unpack.1
  (285 shorter events, 83.2 us)
Async XLA Ops:
  26.8 14.1 %collective-permute-start.18 = (bf16[256,768]{1,0:T(8,128)(2,1)S(1)}, bf16[256,768]{1,0:T(8,128)(2,1)}, u32[]{:S(2)}, u32[]{:S(2)}) collective-permute-start(bf16[256,768]{1,0:T(8,128)(2,1)S(1)} %get-tuple-element.141), channel_id=1, source_target_pairs={{0,2},{2,3},{3,1},{1,0},{4,6},{6,7},{7,5},{5,4},{8,10},{10,11},{11... | collective-permute-start | bytes 1179656 | tf_op jit(solution)/shard_map/ppermute | solution.py:289
  28.9 11.4 %collective-permute-start.5 = (bf16[208,768]{1,0:T(8,128)(2,1)S(1)}, bf16[208,768]{1,0:T(8,128)(2,1)S(1)}, u32[]{:S(2)}, u32[]{:S(2)}) collective-permute-start(bf16[208,768]{1,0:T(8,128)(2,1)S(1)} %collective-permute-done.4.refs_4_), channel_id=1, source_target_pairs={{0,8},{2,10},{4,12},{6,14},{8,16},{10,18},{12,20},{14,22},{16,24},... | collective-permute-start | bytes 958472 | tf_op jit(solution)/shard_map/ppermute | solution.py:425
  33.4 13.1 %collective-permute-start.16 = (bf16[256,768]{1,0:T(8,128)(2,1)S(1)}, bf16[256,768]{1,0:T(8,128)(2,1)S(1)}, u32[]{:S(2)}, u32[]{:S(2)}) collective-permute-start(bf16[256,768]{1,0:T(8,128)(2,1)S(1)} %get-tuple-element.139), channel_id=1, source_target_pairs={{2,1},{1,2},{6,5},{5,6},{10,9},{9,10},{14,13},{13,14},{18,17},{17,... | collective-permute-start | bytes 1179656 | tf_op jit(solution)/shard_map/ppermute | solution.py:277
  44.4 15.0 %collective-permute-start.19 = (bf16[256,768]{1,0:T(8,128)(2,1)}, bf16[256,768]{1,0:T(8,128)(2,1)}, u32[]{:S(2)}, u32[]{:S(2)}) collective-permute-start(bf16[256,768]{1,0:T(8,128)(2,1)} %get-tuple-element.142), channel_id=1, source_target_pairs={{0,2},{2,3},{3,1},{1,0},{4,6},{6,7},{7,5},{5,4},{8,10},{10,11},{11... | collective-permute-start | bytes 1179656 | tf_op jit(solution)/shard_map/ppermute | solution.py:289
  73.5 13.0 %collective-permute-start.31 = (bf16[512,1536]{1,0:T(8,128)(2,1)S(1)}, bf16[512,1536]{1,0:T(8,128)(2,1)S(1)}, u32[]{:S(2)}, u32[]{:S(2)}) collective-permute-start(bf16[512,1536]{1,0:T(8,128)(2,1)S(1)} %get-tuple-element.149.k_ref.v_ref), channel_id=1, source_target_pairs={{0,2},{2,0},{4,6},{6,4},{8,10},{10,8},{12,14},{14,12},{16,18},{18,... | collective-permute-start | bytes 4718600 | tf_op jit(solution)/shard_map/ppermute | solution.py:265
  76.7 16.0 %collective-permute-start.21 = (bf16[192,768]{1,0:T(8,128)(2,1)}, bf16[192,768]{1,0:T(8,128)(2,1)}, u32[]{:S(2)}, u32[]{:S(2)}) collective-permute-start(bf16[192,768]{1,0:T(8,128)(2,1)} %collective-permute-done.9.refs_3_), channel_id=1, source_target_pairs={{0,1},{1,0},{2,3},{3,2},{4,5},{5,4},{6,7},{7,6},{8,9},{9,8},{10,11... | collective-permute-start | bytes 884744 | tf_op jit(solution)/shard_map/ppermute | solution.py:269
  84.3 12.7 %collective-permute-start.22 = (bf16[192,768]{1,0:T(8,128)(2,1)}, bf16[192,768]{1,0:T(8,128)(2,1)}, u32[]{:S(2)}, u32[]{:S(2)}) collective-permute-start(bf16[192,768]{1,0:T(8,128)(2,1)} %collective-permute-done.10.refs_4_), channel_id=1, source_target_pairs={{0,1},{1,0},{2,3},{3,2},{4,5},{5,4},{6,7},{7,6},{8,9},{9,8},{10,11... | collective-permute-start | bytes 884744 | tf_op jit(solution)/shard_map/ppermute | solution.py:269
  86.0 16.0 %collective-permute-start.13 = (bf16[192,768]{1,0:T(8,128)(2,1)}, bf16[192,768]{1,0:T(8,128)(2,1)S(1)}, u32[]{:S(2)}, u32[]{:S(2)}) collective-permute-start(bf16[192,768]{1,0:T(8,128)(2,1)} %collective-permute-done.12.refs_6_), channel_id=1, source_target_pairs={{0,4},{2,6},{4,0},{6,2},{8,12},{10,14},{12,8},{14,10},{16,20},{18,... | collective-permute-start | bytes 884744 | tf_op jit(solution)/shard_map/ppermute | solution.py:429
  103.7 14.9 %collective-permute-start.34 = (bf16[192,768]{1,0:T(8,128)(2,1)S(1)}, bf16[192,768]{1,0:T(8,128)(2,1)S(1)}, u32[]{:S(2)}, u32[]{:S(2)}) collective-permute-start(bf16[192,768]{1,0:T(8,128)(2,1)S(1)} %collective-permute-done.13.refs_7_), channel_id=1, source_target_pairs={{0,1},{1,0},{2,3},{3,2},{4,5},{5,4},{6,7},{7,6},{8,9},{9,8},{10,11... | collective-permute-start | bytes 884744 | tf_op jit(solution)/shard_map/ppermute | solution.py:269
  105.1 13.5 %collective-permute-start.47 = (bf16[192,768]{1,0:T(8,128)(2,1)}, bf16[192,768]{1,0:T(8,128)(2,1)S(1)}, u32[]{:S(2)}, u32[]{:S(2)}) collective-permute-start(bf16[192,768]{1,0:T(8,128)(2,1)} %collective-permute-done.22.refs_12_), channel_id=1, source_target_pairs={{0,2},{2,0},{4,6},{6,4},{8,10},{10,8},{12,14},{14,12},{16,18},{18,... | collective-permute-start | bytes 884744 | tf_op jit(solution)/shard_map/ppermute | solution.py:265
  105.1 14.0 %collective-permute-start.38 = (bf16[192,768]{1,0:T(8,128)(2,1)}, bf16[192,768]{1,0:T(8,128)(2,1)S(1)}, u32[]{:S(2)}, u32[]{:S(2)}) collective-permute-start(bf16[192,768]{1,0:T(8,128)(2,1)} %collective-permute-done.9.refs_3_), channel_id=1, source_target_pairs={{0,2},{2,0},{4,6},{6,4},{8,10},{10,8},{12,14},{14,12},{16,18},{18,... | collective-permute-start | bytes 884744 | tf_op jit(solution)/shard_map/ppermute | solution.py:265
  105.6 13.6 %collective-permute-start.46 = (bf16[192,768]{1,0:T(8,128)(2,1)}, bf16[192,768]{1,0:T(8,128)(2,1)S(1)}, u32[]{:S(2)}, u32[]{:S(2)}) collective-permute-start(bf16[192,768]{1,0:T(8,128)(2,1)} %collective-permute-done.21.refs_11_), channel_id=1, source_target_pairs={{0,2},{2,0},{4,6},{6,4},{8,10},{10,8},{12,14},{14,12},{16,18},{18,... | collective-permute-start | bytes 884744 | tf_op jit(solution)/shard_map/ppermute | solution.py:265
  158.8 14.1 %collective-permute-start.53 = (bf16[192,768]{1,0:T(8,128)(2,1)S(1)}, bf16[192,768]{1,0:T(8,128)(2,1)S(1)}, u32[]{:S(2)}, u32[]{:S(2)}) collective-permute-start(bf16[192,768]{1,0:T(8,128)(2,1)S(1)} %get-tuple-element.261), channel_id=1, source_target_pairs={{0,1},{1,0},{2,3},{3,2},{4,5},{5,4},{6,7},{7,6},{8,9},{9,8},{10,11... | collective-permute-start | bytes 884744 | tf_op jit(solution)/shard_map/ppermute | solution.py:269
  173.0 17.3 %collective-permute-start.71 = (bf16[192,768]{1,0:T(8,128)(2,1)S(1)}, bf16[192,768]{1,0:T(8,128)(2,1)S(1)}, u32[]{:S(2)}, u32[]{:S(2)}) collective-permute-start(bf16[192,768]{1,0:T(8,128)(2,1)S(1)} %fusion.15), channel_id=1, source_target_pairs={{0,4},{2,6},{4,0},{6,2},{8,12},{10,14},{12,8},{14,10},{16,20},{18,... | collective-permute-start | bytes 884744 | tf_op jit(solution)/shard_map/ppermute | solution.py:429
  173.3 17.1 %collective-permute-start.54 = (bf16[192,768]{1,0:T(8,128)(2,1)S(1)}, bf16[192,768]{1,0:T(8,128)(2,1)S(1)}, u32[]{:S(2)}, u32[]{:S(2)}) collective-permute-start(bf16[192,768]{1,0:T(8,128)(2,1)S(1)} %get-tuple-element.175), channel_id=1, source_target_pairs={{0,1},{1,0},{2,3},{3,2},{4,5},{5,4},{6,7},{7,6},{8,9},{9,8},{10,11... | collective-permute-start | bytes 884744 | tf_op jit(solution)/shard_map/ppermute | solution.py:269
  174.2 15.5 %collective-permute-start.59 = (bf16[192,768]{1,0:T(8,128)(2,1)S(1)}, bf16[192,768]{1,0:T(8,128)(2,1)S(1)}, u32[]{:S(2)}, u32[]{:S(2)}) collective-permute-start(bf16[192,768]{1,0:T(8,128)(2,1)S(1)} %get-tuple-element.181), channel_id=1, source_target_pairs={{0,1},{1,0},{2,3},{3,2},{4,5},{5,4},{6,7},{7,6},{8,9},{9,8},{10,11... | collective-permute-start | bytes 884744 | tf_op jit(solution)/shard_map/ppermute | solution.py:269
  175.4 15.9 %collective-permute-start.66 = (bf16[2,192,768]{2,1,0:T(8,128)(2,1)S(1)}, bf16[2,192,768]{2,1,0:T(8,128)(2,1)S(1)}, u32[]{:S(2)}, u32[]{:S(2)}) collective-permute-start(bf16[2,192,768]{2,1,0:T(8,128)(2,1)S(1)} %pad_maximum_fusion.2), channel_id=1, source_target_pairs={{0,8},{2,10},{4,12},{6,14},{8,16},{10,18},{12,20},{14,22},{16,24},... | collective-permute-start | bytes 1769480 | tf_op jit(solution)/shard_map/ppermute | solution.py:425
  191.4 13.1 %collective-permute-start.75 = (bf16[192,768]{1,0:T(8,128)(2,1)S(1)}, bf16[192,768]{1,0:T(8,128)(2,1)S(1)}, u32[]{:S(2)}, u32[]{:S(2)}) collective-permute-start(bf16[192,768]{1,0:T(8,128)(2,1)S(1)} %fusion.14), channel_id=1, source_target_pairs={{0,4},{2,6},{4,0},{6,2},{8,12},{10,14},{12,8},{14,10},{16,20},{18,... | collective-permute-start | bytes 884744 | tf_op jit(solution)/shard_map/ppermute | solution.py:429
  193.1 12.0 %collective-permute-start.55 = (bf16[256,768]{1,0:T(8,128)(2,1)S(1)}, bf16[256,768]{1,0:T(8,128)(2,1)S(1)}, u32[]{:S(2)}, u32[]{:S(2)}) collective-permute-start(bf16[256,768]{1,0:T(8,128)(2,1)S(1)} %get-tuple-element.176), channel_id=1, source_target_pairs={{2,1},{1,2},{6,5},{5,6},{10,9},{9,10},{14,13},{13,14},{18,17},{17,... | collective-permute-start | bytes 1179656 | tf_op jit(solution)/shard_map/ppermute | solution.py:277
  194.0 13.0 %collective-permute-start.60 = (bf16[256,768]{1,0:T(8,128)(2,1)S(1)}, bf16[256,768]{1,0:T(8,128)(2,1)S(1)}, u32[]{:S(2)}, u32[]{:S(2)}) collective-permute-start(bf16[256,768]{1,0:T(8,128)(2,1)S(1)} %get-tuple-element.182), channel_id=1, source_target_pairs={{2,0},{3,2},{1,3},{0,1},{6,4},{7,6},{5,7},{4,5},{10,8},{11,10},{9,... | collective-permute-start | bytes 1179656 | tf_op jit(solution)/shard_map/ppermute | solution.py:289
  205.2 18.0 %collective-permute-start.81 = (bf16[2,192,768]{2,1,0:T(8,128)(2,1)S(1)}, bf16[2,192,768]{2,1,0:T(8,128)(2,1)S(1)}, u32[]{:S(2)}, u32[]{:S(2)}) collective-permute-start(bf16[2,192,768]{2,1,0:T(8,128)(2,1)S(1)} %maximum_add_fusion.1), channel_id=1, source_target_pairs={{0,8},{2,10},{4,12},{6,14},{8,16},{10,18},{12,20},{14,22},{16,24},... | collective-permute-start | bytes 1769480 | tf_op jit(solution)/shard_map/ppermute | solution.py:425
  208.0 23.0 %collective-permute-start.69 = (bf16[2,208,768]{2,1,0:T(8,128)(2,1)S(1)}, bf16[2,208,768]{2,1,0:T(8,128)(2,1)S(1)}, u32[]{:S(2)}, u32[]{:S(2)}) collective-permute-start(bf16[2,208,768]{2,1,0:T(8,128)(2,1)S(1)} %get-tuple-element.208), channel_id=1, source_target_pairs={{0,2},{2,0},{4,6},{6,4},{8,10},{10,8},{12,14},{14,12},{16,18},{18,... | collective-permute-start | bytes 1916936 | tf_op jit(solution)/shard_map/ppermute | solution.py:265
  208.0 15.4 %collective-permute-start.74 = (bf16[2,208,768]{2,1,0:T(8,128)(2,1)S(1)}, bf16[2,208,768]{2,1,0:T(8,128)(2,1)S(1)}, u32[]{:S(2)}, u32[]{:S(2)}) collective-permute-start(bf16[2,208,768]{2,1,0:T(8,128)(2,1)S(1)} %get-tuple-element.214), channel_id=1, source_target_pairs={{0,2},{2,0},{4,6},{6,4},{8,10},{10,8},{12,14},{14,12},{16,18},{18,... | collective-permute-start | bytes 1916936 | tf_op jit(solution)/shard_map/ppermute | solution.py:265
  208.7 15.3 %collective-permute-start.72 = (bf16[208,768]{1,0:T(8,128)(2,1)S(1)}, bf16[208,768]{1,0:T(8,128)(2,1)S(1)}, u32[]{:S(2)}, u32[]{:S(2)}) collective-permute-start(bf16[208,768]{1,0:T(8,128)(2,1)S(1)} %slice_bitcast_fusion.9), channel_id=1, source_target_pairs={{0,4},{2,6},{4,0},{6,2},{8,12},{10,14},{12,8},{14,10},{16,20},{18,... | collective-permute-start | bytes 958472 | tf_op jit(solution)/shard_map/ppermute | solution.py:429
  217.2 12.9 %collective-permute-start.79 = (bf16[208,768]{1,0:T(8,128)(2,1)S(1)}, bf16[208,768]{1,0:T(8,128)(2,1)S(1)}, u32[]{:S(2)}, u32[]{:S(2)}) collective-permute-start(bf16[208,768]{1,0:T(8,128)(2,1)S(1)} %fusion), channel_id=1, source_target_pairs={{0,8},{2,10},{4,12},{6,14},{8,16},{10,18},{12,20},{14,22},{16,24},... | collective-permute-start | bytes 958472 | tf_op jit(solution)/shard_map/ppermute | solution.py:425
  223.3 25.7 %collective-permute-start.82 = (bf16[2,192,768]{2,1,0:T(8,128)(2,1)S(1)}, bf16[2,192,768]{2,1,0:T(8,128)(2,1)S(1)}, u32[]{:S(2)}, u32[]{:S(2)}) collective-permute-start(bf16[2,192,768]{2,1,0:T(8,128)(2,1)S(1)} %maximum_add_fusion), channel_id=1, source_target_pairs={{0,8},{2,10},{4,12},{6,14},{8,16},{10,18},{12,20},{14,22},{16,24},... | collective-permute-start | bytes 1769480 | tf_op jit(solution)/shard_map/ppermute | solution.py:425
  230.1 18.5 %collective-permute-start.80 = (bf16[208,768]{1,0:T(8,128)(2,1)S(1)}, bf16[208,768]{1,0:T(8,128)(2,1)S(1)}, u32[]{:S(2)}, u32[]{:S(2)}) collective-permute-start(bf16[208,768]{1,0:T(8,128)(2,1)S(1)} %fusion.2), channel_id=1, source_target_pairs={{0,8},{2,10},{4,12},{6,14},{8,16},{10,18},{12,20},{14,22},{16,24},... | collective-permute-start | bytes 958472 | tf_op jit(solution)/shard_map/ppermute | solution.py:425
  230.3 19.0 %collective-permute-start.67 = (bf16[256,768]{1,0:T(8,128)(2,1)S(1)}, bf16[256,768]{1,0:T(8,128)(2,1)S(1)}, u32[]{:S(2)}, u32[]{:S(2)}) collective-permute-start(bf16[256,768]{1,0:T(8,128)(2,1)S(1)} %get-tuple-element.205), channel_id=1, source_target_pairs={{2,1},{1,2},{6,5},{5,6},{10,9},{9,10},{14,13},{13,14},{18,17},{17,... | collective-permute-start | bytes 1179656 | tf_op jit(solution)/shard_map/ppermute | solution.py:277
  231.1 17.9 %collective-permute-start.85 = (bf16[192,768]{1,0:T(8,128)(2,1)S(1)}, bf16[192,768]{1,0:T(8,128)(2,1)S(1)}, u32[]{:S(2)}, u32[]{:S(2)}) collective-permute-start(bf16[192,768]{1,0:T(8,128)(2,1)S(1)} %fusion.7), channel_id=1, source_target_pairs={{0,4},{2,6},{4,0},{6,2},{8,12},{10,14},{12,8},{14,10},{16,20},{18,... | collective-permute-start | bytes 884744 | tf_op jit(solution)/shard_map/ppermute | solution.py:429
  231.5 27.7 %collective-permute-start.68 = (bf16[256,768]{1,0:T(8,128)(2,1)S(1)}, bf16[256,768]{1,0:T(8,128)(2,1)S(1)}, u32[]{:S(2)}, u32[]{:S(2)}) collective-permute-start(bf16[256,768]{1,0:T(8,128)(2,1)S(1)} %get-tuple-element.206), channel_id=1, source_target_pairs={{2,0},{3,2},{1,3},{0,1},{6,4},{7,6},{5,7},{4,5},{10,8},{11,10},{9,... | collective-permute-start | bytes 1179656 | tf_op jit(solution)/shard_map/ppermute | solution.py:289
  249.2 16.3 %collective-permute-start.86 = (bf16[2,192,768]{2,1,0:T(8,128)(2,1)S(1)}, bf16[2,192,768]{2,1,0:T(8,128)(2,1)S(1)}, u32[]{:S(2)}, u32[]{:S(2)}) collective-permute-start(bf16[2,192,768]{2,1,0:T(8,128)(2,1)S(1)} %maximum_add_fusion.2.tail), channel_id=1, source_target_pairs={{0,1},{1,0},{2,3},{3,2},{4,5},{5,4},{6,7},{7,6},{8,9},{9,8},{10,11... | collective-permute-start | bytes 1769480 | tf_op jit(solution)/shard_map/ppermute | solution.py:269
  259.2 11.3 %collective-permute-start.84 = (bf16[208,768]{1,0:T(8,128)(2,1)S(1)}, bf16[208,768]{1,0:T(8,128)(2,1)S(1)}, u32[]{:S(2)}, u32[]{:S(2)}) collective-permute-start(bf16[208,768]{1,0:T(8,128)(2,1)S(1)} %fusion.6.head), channel_id=1, source_target_pairs={{0,1},{1,0},{2,3},{3,2},{4,5},{5,4},{6,7},{7,6},{8,9},{9,8},{10,11... | collective-permute-start | bytes 958472 | tf_op jit(solution)/shard_map/ppermute | solution.py:269
  (98 other events, 803.1 us)

commit v6 on v5

--- a/solution.py
+++ b/solution.py
@@ -16,7 +16,7 @@
 F32 = jnp.float32
 BF16 = jnp.bfloat16
 MEGA = 1024 * 1024
-VMEM = {"pack": 60, "qkv": 28, "merge": 14, "ffn": 40, "close": 26, "unpack": 36}
+VMEM = {"pack": 60, "qkv": 28, "merge": 14, "ffn": 36, "close": 26, "unpack": 36}
 
 
 def layer_norm(values, gain, shift):
@@ -708,8 +708,8 @@
 
 def ffn_kernel(place, *refs):
     pieces, refs = refs[:32], refs[32:]
-    m_ref, n2_ref, gy_ref, merge_weight, v48, v192, out_ref, dm_ref, dz_ref, do_ref, g48, g192 = refs[:12]
-    outs, (weights, grads, y, dn2, n2_t, u, df, in_sems, out_sems) = refs[12:20], refs[20:]
+    m_far, n2_ref, gy_ref, packed, v48, v192, out_ref, dm_ref, dz_ref, do_ref, g48, g192 = refs[:12]
+    outs, (weights, grads, y, dn2, n2_t, u, df, m_ref, merge_weight, in_sems, out_sems, late_sems) = refs[12:20], refs[20:]
     z, x, core, half = spot(place)
     slots = ring_slots(z, x)
     spots = [(slot + core, half) for slot in slots] + [(slot + core, 1 - half) for slot in slots]
@@ -722,6 +722,12 @@
         copy.start()
     width = m_ref.shape[1]
     part = width // GROUPS
+    late = [
+        pltpu.make_async_copy(m_far, m_ref, late_sems.at[0]),
+        pltpu.make_async_copy(packed.at[:, 3 * part : 4 * part, :], merge_weight, late_sems.at[1]),
+    ]
+    for copy in late:
+        copy.start()
     n2_t[...] = jnp.transpose(n2_ref[...])
     y[...] = jnp.zeros_like(y)
     dn2[...] = jnp.zeros_like(dn2)
@@ -768,6 +774,8 @@
                     )
     for copy in copies:
         copy.start()
+    for copy in late:
+        copy.wait()
     middle = m_ref[...]
     out_ref[...] = (middle + y[...] + v48[7:8, :]).astype(BF16)
     shape, scale = normalise(middle)
@@ -800,7 +808,7 @@
     results = kernel_call(
         ffn_kernel, (place,),
         [ANYWHERE] * 32
-        + [whole(middle.shape), whole(second.shape), whole(out_grad.shape), merge_spec(packed), whole(v48.shape), whole(v192.shape)],
+        + [ANYWHERE, whole(second.shape), whole(out_grad.shape), ANYWHERE, whole(v48.shape), whole(v192.shape)],
         pieces + [middle, second, out_grad, packed, v48, v192],
         [whole(shape) for shape, unused in shapes] + [ANYWHERE] * 8,
         [jax.ShapeDtypeStruct(shape, dtype) for shape, dtype in shapes] + [part] * 8,
@@ -808,7 +816,8 @@
             pltpu.VMEM(pack_shape, BF16), pltpu.VMEM(pack_shape, BF16),
             pltpu.VMEM((rows, width), F32), pltpu.VMEM((rows, width), F32), pltpu.VMEM((width, rows), BF16),
             pltpu.VMEM((rows, width), BF16), pltpu.VMEM((rows, width), BF16),
-            pltpu.SemaphoreType.DMA((32,)), pltpu.SemaphoreType.DMA((32,)),
+            pltpu.VMEM((rows, width), F32), pltpu.VMEM((GROUPS, width // GROUPS, width), BF16),
+            pltpu.SemaphoreType.DMA((32,)), pltpu.SemaphoreType.DMA((32,)), pltpu.SemaphoreType.DMA((2,)),
         ],
         "ffn", 12 * rows * width * ff, 8 * width * ff,
     )

time: 278 us -> 274 us (0.986)
  Pallas kernels: 72.2 us -> 69 us
    pallas_call x6, Pallas kernels: 49.3 us -> 46.1 us  [kernel_call(): pl.pallas_call(body, grid_spec=pltpu.PrefetchScalarGridSpec(num_scalar_pr...]
    unnamed x87 -> x81, local copies, waits for them, and re-layouts: 12.7 us -> 11.9 us
  transfers between devices with their start and end apart: 87 -> 87, of which waited for: 29 -> 30; matrix products, arithmetic and copies ran while one was open for 4% -> 4% of each run, Pallas kernels for 12% -> 12%
where the time goes in v6:
time: 274 us; the launch traced here: 269 us
  waiting for transfers between devices  116 us (42%)
  Pallas kernels  69 us (25%)
  starting transfers between devices  62 us (23%)
  local copies, waits for them, and re-layouts  13 us (5%)
  other arithmetic  6.89 us (3%)
    pallas_call x6, Pallas kernels, kernel_call(): pl.pallas_call(body, grid_spec=pltpu.PrefetchScalarGridSpec(num_scalar_pr...  46.1 us
    ppermute x12, waiting for transfers between devices, shift_z(): lax.ppermute(value, 'dp', pairs_of(16, lambda index: (index + 4) % 16))  44.7 us
    ppermute x14, waiting for transfers between devices, swap_seq(): return lax.ppermute(value, 'seq', [(0, 1), (1, 0)])  39.1 us
    ppermute x16, waiting for transfers between devices, swap_x(): return lax.ppermute(value, 'dp', pairs_of(16, lambda index: index ^ 2))  26.4 us
    pallas_call x4, Pallas kernels, balanced(): pl.pallas_call(functools.partial(body, block=rows // 2), grid_spec=pltpu....  22.9 us
    ppermute x16, starting transfers between devices, swap_x(): return lax.ppermute(value, 'dp', pairs_of(16, lambda index: index ^ 2))  15.1 us
    ppermute x14, starting transfers between devices, swap_seq(): return lax.ppermute(value, 'seq', [(0, 1), (1, 0)])  13.7 us
    unnamed x81, local copies, waits for them, and re-layouts  11.9 us
  transfers between devices with their start and end apart: 87, of which 30 were waited for; matrix products, arithmetic and copies ran while one was open for 4% of the time, Pallas kernels for 12%

profile of v6, /device:TPU:0, one launch (start us, length us, event | category | flops | bytes accessed | tf_op | source)
XLA Modules:
  0.0 269.1 jit_solution(733182918560238228)
XLA Ops:
  1.2 3.3 %pack.1 = (bf16[208,768]{1,0:T(8,128)(2,1)}, bf16[192,768]{1,0:T(8,128)(2,1)}) custom-call(s32[12]{0:T(128)} %slots.3, s32[2]{0:T(128)} %pad_add_fusion.place, f32[2,48]{1,0:T(2,128)} %refs_0_.1, f32[2,48]{1,0:T(2,128)} %refs_1_.1, f32[2,48,2304]{2,1,0:T(8,128)} %refs_2_.1, f32[2,96]{1,0:T(2,128)} %refs_3_.1, f32[2,48,768]{2,1,0:T(8,128)} %refs_4_.1, ...), custom_call_target="tpu_custom_call" | custom-call | bytes 1916928 | tf_op jit(solution)/shard_map/pack/pallas_call | solution.py:363
  4.5 2.9 %collective-permute-start = (bf16[208,768]{1,0:T(8,128)(2,1)}, bf16[208,768]{1,0:T(8,128)(2,1)S(1)}, u32[]{:S(2)}, u32[]{:S(2)}) collective-permute-start(bf16[208,768]{1,0:T(8,128)(2,1)} %get-tuple-element.127.refs_0_), channel_id=1, source_target_pairs={{0,4},{2,6},{4,0},{6,2},{8,12},{10,14},{12,8},{14,10},{16,20},{18,... | collective-permute-start | bytes 958472 | tf_op jit(solution)/shard_map/ppermute | solution.py:429
  9.0 6.2 %collective-permute-done.refs_1_ = bf16[208,768]{1,0:T(8,128)(2,1)S(1)} collective-permute-done((bf16[208,768]{1,0:T(8,128)(2,1)}, bf16[208,768]{1,0:T(8,128)(2,1)S(1)}, u32[]{:S(2)}, u32[]{:S(2)}) %collective-permute-start) | collective-permute-done | bytes 319520 | tf_op jit(solution)/shard_map/ppermute | solution.py:429
  20.0 3.7 %collective-permute-done.1.refs_1_ = bf16[192,768]{1,0:T(8,128)(2,1)} collective-permute-done((bf16[192,768]{1,0:T(8,128)(2,1)}, bf16[192,768]{1,0:T(8,128)(2,1)}, u32[]{:S(2)}, u32[]{:S(2)}) %collective-permute-start.1) | collective-permute-done | bytes 294944 | tf_op jit(solution)/shard_map/ppermute | solution.py:429
  35.7 4.6 %collective-permute-done.5.refs_6_ = bf16[208,768]{1,0:T(8,128)(2,1)S(1)} collective-permute-done((bf16[208,768]{1,0:T(8,128)(2,1)S(1)}, bf16[208,768]{1,0:T(8,128)(2,1)S(1)}, u32[]{:S(2)}, u32[]{:S(2)}) %collective-permute-start.5) | collective-permute-done | bytes 319520 | tf_op jit(solution)/shard_map/ppermute | solution.py:425
  41.4 3.0 %collective-permute-done.3.refs_2_ = bf16[192,768]{1,0:T(8,128)(2,1)} collective-permute-done((bf16[192,768]{1,0:T(8,128)(2,1)S(1)}, bf16[192,768]{1,0:T(8,128)(2,1)}, u32[]{:S(2)}, u32[]{:S(2)}) %collective-permute-start.3) | collective-permute-done | bytes 294944 | tf_op jit(solution)/shard_map/ppermute | solution.py:425
  46.6 2.4 collective-permute-done.8.refs_7_
  51.2 7.3 %collective-permute-done.10.refs_4_ = bf16[192,768]{1,0:T(8,128)(2,1)} collective-permute-done((bf16[192,768]{1,0:T(8,128)(2,1)}, bf16[192,768]{1,0:T(8,128)(2,1)}, u32[]{:S(2)}, u32[]{:S(2)}) %collective-permute-start.10) | collective-permute-done | bytes 294944 | tf_op jit(solution)/shard_map/ppermute | solution.py:425
  59.9 2.4 broadcast_select_fusion.5
  63.9 4.9 %qkv.1 = (bf16[16,208,768]{2,1,0:T(8,128)(2,1)S(1)}, bf16[512,768]{1,0:T(8,128)(2,1)S(1)}, bf16[512,768]{1,0:T(8,128)(2,1)S(1)}, bf16[512,1536]{1,0:T(8,128)(2,1...) custom-call(s32[2]{0:T(128)S(1)} %copy-done.18, ...), custom_call_target="tpu_custom_call" | custom-call | flops 905969664 | bytes 5898240 | tf_op jit(solution)/shard_map/qkv/pallas_call | solution.py:363
  77.5 6.8 %collective-permute-done.20.refs_10_ = bf16[192,768]{1,0:T(8,128)(2,1)S(1)} collective-permute-done((bf16[192,768]{1,0:T(8,128)(2,1)}, bf16[192,768]{1,0:T(8,128)(2,1)S(1)}, u32[]{:S(2)}, u32[]{:S(2)}) %collective-permute-start.20) | collective-permute-done | bytes 294944 | tf_op jit(solution)/shard_map/ppermute | solution.py:269
  87.6 4.9 %attend.2 = (bf16[512,384]{1,0:T(8,128)(2,1)S(1)}, f32[3,2,512]{2,1,0:T(2,128)S(1)}) custom-call(s32[1]{0:T(128)} %bitcast.6.extra, bf16[512,768]{1,0:T(8,128)(2,1)S(1)} %copy-done.2, bf16[512,1536]{1,0:T(8,128)(2,1)S(1)} %get-tuple-element.149.k_ref.v_ref, bf16[512,1536]{1,0:T(8,128)(2,1)S(1)} %get-tuple-element.149.k_ref.v_ref, ...), custom_call_target="tpu_custom_call" | custom-call | flops 1000000 | bytes 1000 | tf_op jit(solution)/shard_map/attend/pallas_call | solution.py:615
  94.3 2.7 collective-permute-done.22.refs_12_
  97.0 4.9 %attend.3 = (bf16[512,384]{1,0:T(8,128)(2,1)S(1)}, f32[3,2,512]{2,1,0:T(2,128)S(1)}) custom-call(s32[1]{0:T(128)} %bitcast.6.extra, bf16[512,768]{1,0:T(8,128)(2,1)S(1)} %copy-done.2, bf16[512,1536]{1,0:T(8,128)(2,1)S(1)} %get-tuple-element.149.k_ref.v_ref, bf16[512,1536]{1,0:T(8,128)(2,1)S(1)} %get-tuple-element.149.k_ref.v_ref, ...), custom_call_target="tpu_custom_call" | custom-call | flops 1000000 | bytes 1000 | tf_op jit(solution)/shard_map/attend/pallas_call | solution.py:615
  105.7 7.4 %collective-permute-done.33.refs_14_ = bf16[192,768]{1,0:T(8,128)(2,1)S(1)} collective-permute-done((bf16[192,768]{1,0:T(8,128)(2,1)}, bf16[192,768]{1,0:T(8,128)(2,1)S(1)}, u32[]{:S(2)}, u32[]{:S(2)}) %collective-permute-start.33) | collective-permute-done | bytes 294944 | tf_op jit(solution)/shard_map/ppermute | solution.py:269
  113.1 5.5 %collective-permute-done.34.refs_15_ = bf16[192,768]{1,0:T(8,128)(2,1)S(1)} collective-permute-done((bf16[192,768]{1,0:T(8,128)(2,1)S(1)}, bf16[192,768]{1,0:T(8,128)(2,1)S(1)}, u32[]{:S(2)}, u32[]{:S(2)}) %collective-permute-start.34) | collective-permute-done | bytes 294944 | tf_op jit(solution)/shard_map/ppermute | solution.py:269
  123.0 26.2 %ffn.1 = (bf16[512,768]{1,0:T(8,128)(2,1)S(1)}, f32[512,768]{1,0:T(8,128)}, bf16[512,768]{1,0:T(8,128)(2,1)S(1)}, bf16[512,768]{1,0:T(8,128)(2,1)S(1)}, f32[8,76...) custom-call(s32[2]{0:T(128)S(1)} %copy-done.18, ...), custom_call_target="tpu_custom_call" | custom-call | flops 7247757312 | bytes 9437184 | tf_op jit(solution)/shard_map/ffn/pallas_call | solution.py:363
  153.4 2.3 collective-permute-done.52
  158.4 4.3 %collective-permute-done.58 = bf16[192,768]{1,0:T(8,128)(2,1)S(1)} collective-permute-done((bf16[192,768]{1,0:T(8,128)(2,1)S(1)}, bf16[192,768]{1,0:T(8,128)(2,1)S(1)}, u32[]{:S(2)}, u32[]{:S(2)}) %collective-permute-start.58) | collective-permute-done | bytes 294944 | tf_op jit(solution)/shard_map/ppermute | solution.py:269
  163.2 5.3 %collective-permute-done.53 = bf16[192,768]{1,0:T(8,128)(2,1)S(1)} collective-permute-done((bf16[192,768]{1,0:T(8,128)(2,1)S(1)}, bf16[192,768]{1,0:T(8,128)(2,1)S(1)}, u32[]{:S(2)}, u32[]{:S(2)}) %collective-permute-start.53) | collective-permute-done | bytes 294944 | tf_op jit(solution)/shard_map/ppermute | solution.py:269
  172.1 6.5 %attend_back.2 = (bf16[512,384]{1,0:T(8,128)(2,1)S(1)}, bf16[512,384]{1,0:T(8,128)(2,1)S(1)}, bf16[512,384]{1,0:T(8,128)(2,1)S(1)}, bf16[512,384]{1,0:T(8,128)(2,1)S(1)}, bf16[512,384]{1,0:T(8,128)(2,1)S(1)}) custom-call(s32[1]{0:T(128)} %bitcast.6.extra, bf16[512,768]{1,0:T(8,128)(2,1)S(1)} %copy-done.3, ...), custom_call_target="tpu_custom_call" | custom-call | flops 1000000 | bytes 1000 | tf_op jit(solution)/shard_map/attend_back/pallas_call | solution.py:615
  178.7 6.6 %attend_back.3 = (bf16[512,384]{1,0:T(8,128)(2,1)S(1)}, bf16[512,384]{1,0:T(8,128)(2,1)S(1)}, bf16[512,384]{1,0:T(8,128)(2,1)S(1)}, bf16[512,384]{1,0:T(8,128)(2,1)S(1)}, bf16[512,384]{1,0:T(8,128)(2,1)S(1)}) custom-call(s32[1]{0:T(128)} %bitcast.6.extra, bf16[512,768]{1,0:T(8,128)(2,1)S(1)} %copy-done.3, ...), custom_call_target="tpu_custom_call" | custom-call | flops 1000000 | bytes 1000 | tf_op jit(solution)/shard_map/attend_back/pallas_call | solution.py:615
  189.5 2.4 collective-permute-start.60
  192.0 7.9 %close.1 = (bf16[512,768]{1,0:T(8,128)(2,1)S(1)}, bf16[2,208,768]{2,1,0:T(8,128)(2,1)S(1)}, bf16[2,208,768]{2,1,0:T(8,128)(2,1)S(1)}, bf16[2,208,768]{2,1,0:T(8,...) custom-call(s32[2]{0:T(128)S(1)} %copy-done.18, ...), custom_call_target="tpu_custom_call" | custom-call | flops 2113929216 | bytes 5898240 | tf_op jit(solution)/shard_map/close/pallas_call | solution.py:363
  206.0 6.7 %collective-permute-done.78 = bf16[208,768]{1,0:T(8,128)(2,1)S(1)} collective-permute-done((bf16[208,768]{1,0:T(8,128)(2,1)S(1)}, bf16[208,768]{1,0:T(8,128)(2,1)S(1)}, u32[]{:S(2)}, u32[]{:S(2)}) %collective-permute-start.78) | collective-permute-done | bytes 319520 | tf_op jit(solution)/shard_map/ppermute | solution.py:429
  213.5 5.2 %collective-permute-done.81 = bf16[2,192,768]{2,1,0:T(8,128)(2,1)S(1)} collective-permute-done((bf16[2,192,768]{2,1,0:T(8,128)(2,1)S(1)}, bf16[2,192,768]{2,1,0:T(8,128)(2,1)S(1)}, u32[]{:S(2)}, u32[]{:S(2)}) %collective-permute-start.81) | collective-permute-done | bytes 589856 | tf_op jit(solution)/shard_map/ppermute | solution.py:425
  219.4 6.1 %collective-permute-done.79 = bf16[208,768]{1,0:T(8,128)(2,1)S(1)} collective-permute-done((bf16[208,768]{1,0:T(8,128)(2,1)S(1)}, bf16[208,768]{1,0:T(8,128)(2,1)S(1)}, u32[]{:S(2)}, u32[]{:S(2)}) %collective-permute-start.79) | collective-permute-done | bytes 319520 | tf_op jit(solution)/shard_map/ppermute | solution.py:425
  229.2 14.9 %collective-permute-done.80 = bf16[208,768]{1,0:T(8,128)(2,1)S(1)} collective-permute-done((bf16[208,768]{1,0:T(8,128)(2,1)S(1)}, bf16[208,768]{1,0:T(8,128)(2,1)S(1)}, u32[]{:S(2)}, u32[]{:S(2)}) %collective-permute-start.80) | collective-permute-done | bytes 319520 | tf_op jit(solution)/shard_map/ppermute | solution.py:425
  246.3 6.5 %collective-permute-done.73 = bf16[208,768]{1,0:T(8,128)(2,1)S(1)} collective-permute-done((bf16[208,768]{1,0:T(8,128)(2,1)S(1)}, bf16[208,768]{1,0:T(8,128)(2,1)S(1)}, u32[]{:S(2)}, u32[]{:S(2)}) %collective-permute-start.73) | collective-permute-done | bytes 319520 | tf_op jit(solution)/shard_map/ppermute | solution.py:429
  257.0 2.8 %copy.29 = f32[512,1,768]{2,1,0:T(1,128)} copy(f32[512,1,768]{2,0,1:T(8,128)S(1)} %maximum_convert_fusion) | data formatting | bytes 3145728
  261.1 5.0 %collective-permute-done.84.head_far = bf16[208,768]{1,0:T(8,128)(2,1)S(1)} collective-permute-done((bf16[208,768]{1,0:T(8,128)(2,1)S(1)}, bf16[208,768]{1,0:T(8,128)(2,1)S(1)}, u32[]{:S(2)}, u32[]{:S(2)}) %collective-permute-start.84) | collective-permute-done | bytes 319520 | tf_op jit(solution)/shard_map/ppermute | solution.py:269
  266.0 2.7 unpack.1
  (279 shorter events, 83.2 us)
Async XLA Ops:
  26.7 14.1 %collective-permute-start.18 = (bf16[256,768]{1,0:T(8,128)(2,1)S(1)}, bf16[256,768]{1,0:T(8,128)(2,1)}, u32[]{:S(2)}, u32[]{:S(2)}) collective-permute-start(bf16[256,768]{1,0:T(8,128)(2,1)S(1)} %get-tuple-element.141), channel_id=1, source_target_pairs={{0,2},{2,3},{3,1},{1,0},{4,6},{6,7},{7,5},{5,4},{8,10},{10,11},{11... | collective-permute-start | bytes 1179656 | tf_op jit(solution)/shard_map/ppermute | solution.py:289
  28.9 11.4 %collective-permute-start.5 = (bf16[208,768]{1,0:T(8,128)(2,1)S(1)}, bf16[208,768]{1,0:T(8,128)(2,1)S(1)}, u32[]{:S(2)}, u32[]{:S(2)}) collective-permute-start(bf16[208,768]{1,0:T(8,128)(2,1)S(1)} %collective-permute-done.4.refs_4_), channel_id=1, source_target_pairs={{0,8},{2,10},{4,12},{6,14},{8,16},{10,18},{12,20},{14,22},{16,24},... | collective-permute-start | bytes 958472 | tf_op jit(solution)/shard_map/ppermute | solution.py:425
  33.4 13.1 %collective-permute-start.16 = (bf16[256,768]{1,0:T(8,128)(2,1)S(1)}, bf16[256,768]{1,0:T(8,128)(2,1)S(1)}, u32[]{:S(2)}, u32[]{:S(2)}) collective-permute-start(bf16[256,768]{1,0:T(8,128)(2,1)S(1)} %get-tuple-element.139), channel_id=1, source_target_pairs={{2,1},{1,2},{6,5},{5,6},{10,9},{9,10},{14,13},{13,14},{18,17},{17,... | collective-permute-start | bytes 1179656 | tf_op jit(solution)/shard_map/ppermute | solution.py:277
  44.4 15.0 %collective-permute-start.19 = (bf16[256,768]{1,0:T(8,128)(2,1)}, bf16[256,768]{1,0:T(8,128)(2,1)}, u32[]{:S(2)}, u32[]{:S(2)}) collective-permute-start(bf16[256,768]{1,0:T(8,128)(2,1)} %get-tuple-element.142), channel_id=1, source_target_pairs={{0,2},{2,3},{3,1},{1,0},{4,6},{6,7},{7,5},{5,4},{8,10},{10,11},{11... | collective-permute-start | bytes 1179656 | tf_op jit(solution)/shard_map/ppermute | solution.py:289
  73.5 13.0 %collective-permute-start.31 = (bf16[512,1536]{1,0:T(8,128)(2,1)S(1)}, bf16[512,1536]{1,0:T(8,128)(2,1)S(1)}, u32[]{:S(2)}, u32[]{:S(2)}) collective-permute-start(bf16[512,1536]{1,0:T(8,128)(2,1)S(1)} %get-tuple-element.149.k_ref.v_ref), channel_id=1, source_target_pairs={{0,2},{2,0},{4,6},{6,4},{8,10},{10,8},{12,14},{14,12},{16,18},{18,... | collective-permute-start | bytes 4718600 | tf_op jit(solution)/shard_map/ppermute | solution.py:265
  76.6 16.0 %collective-permute-start.21 = (bf16[192,768]{1,0:T(8,128)(2,1)}, bf16[192,768]{1,0:T(8,128)(2,1)}, u32[]{:S(2)}, u32[]{:S(2)}) collective-permute-start(bf16[192,768]{1,0:T(8,128)(2,1)} %collective-permute-done.9.refs_3_), channel_id=1, source_target_pairs={{0,1},{1,0},{2,3},{3,2},{4,5},{5,4},{6,7},{7,6},{8,9},{9,8},{10,11... | collective-permute-start | bytes 884744 | tf_op jit(solution)/shard_map/ppermute | solution.py:269
  84.2 12.7 %collective-permute-start.22 = (bf16[192,768]{1,0:T(8,128)(2,1)}, bf16[192,768]{1,0:T(8,128)(2,1)}, u32[]{:S(2)}, u32[]{:S(2)}) collective-permute-start(bf16[192,768]{1,0:T(8,128)(2,1)} %collective-permute-done.10.refs_4_), channel_id=1, source_target_pairs={{0,1},{1,0},{2,3},{3,2},{4,5},{5,4},{6,7},{7,6},{8,9},{9,8},{10,11... | collective-permute-start | bytes 884744 | tf_op jit(solution)/shard_map/ppermute | solution.py:269
  85.9 16.0 %collective-permute-start.13 = (bf16[192,768]{1,0:T(8,128)(2,1)}, bf16[192,768]{1,0:T(8,128)(2,1)S(1)}, u32[]{:S(2)}, u32[]{:S(2)}) collective-permute-start(bf16[192,768]{1,0:T(8,128)(2,1)} %collective-permute-done.12.refs_6_), channel_id=1, source_target_pairs={{0,4},{2,6},{4,0},{6,2},{8,12},{10,14},{12,8},{14,10},{16,20},{18,... | collective-permute-start | bytes 884744 | tf_op jit(solution)/shard_map/ppermute | solution.py:429
  103.7 14.9 %collective-permute-start.34 = (bf16[192,768]{1,0:T(8,128)(2,1)S(1)}, bf16[192,768]{1,0:T(8,128)(2,1)S(1)}, u32[]{:S(2)}, u32[]{:S(2)}) collective-permute-start(bf16[192,768]{1,0:T(8,128)(2,1)S(1)} %collective-permute-done.13.refs_7_), channel_id=1, source_target_pairs={{0,1},{1,0},{2,3},{3,2},{4,5},{5,4},{6,7},{7,6},{8,9},{9,8},{10,11... | collective-permute-start | bytes 884744 | tf_op jit(solution)/shard_map/ppermute | solution.py:269
  105.1 13.5 %collective-permute-start.47 = (bf16[192,768]{1,0:T(8,128)(2,1)}, bf16[192,768]{1,0:T(8,128)(2,1)S(1)}, u32[]{:S(2)}, u32[]{:S(2)}) collective-permute-start(bf16[192,768]{1,0:T(8,128)(2,1)} %collective-permute-done.22.refs_12_), channel_id=1, source_target_pairs={{0,2},{2,0},{4,6},{6,4},{8,10},{10,8},{12,14},{14,12},{16,18},{18,... | collective-permute-start | bytes 884744 | tf_op jit(solution)/shard_map/ppermute | solution.py:265
  105.1 14.0 %collective-permute-start.38 = (bf16[192,768]{1,0:T(8,128)(2,1)}, bf16[192,768]{1,0:T(8,128)(2,1)S(1)}, u32[]{:S(2)}, u32[]{:S(2)}) collective-permute-start(bf16[192,768]{1,0:T(8,128)(2,1)} %collective-permute-done.9.refs_3_), channel_id=1, source_target_pairs={{0,2},{2,0},{4,6},{6,4},{8,10},{10,8},{12,14},{14,12},{16,18},{18,... | collective-permute-start | bytes 884744 | tf_op jit(solution)/shard_map/ppermute | solution.py:265
  105.6 13.6 %collective-permute-start.46 = (bf16[192,768]{1,0:T(8,128)(2,1)}, bf16[192,768]{1,0:T(8,128)(2,1)S(1)}, u32[]{:S(2)}, u32[]{:S(2)}) collective-permute-start(bf16[192,768]{1,0:T(8,128)(2,1)} %collective-permute-done.21.refs_11_), channel_id=1, source_target_pairs={{0,2},{2,0},{4,6},{6,4},{8,10},{10,8},{12,14},{14,12},{16,18},{18,... | collective-permute-start | bytes 884744 | tf_op jit(solution)/shard_map/ppermute | solution.py:265
  156.1 12.3 %collective-permute-start.53 = (bf16[192,768]{1,0:T(8,128)(2,1)S(1)}, bf16[192,768]{1,0:T(8,128)(2,1)S(1)}, u32[]{:S(2)}, u32[]{:S(2)}) collective-permute-start(bf16[192,768]{1,0:T(8,128)(2,1)S(1)} %get-tuple-element.261), channel_id=1, source_target_pairs={{0,1},{1,0},{2,3},{3,2},{4,5},{5,4},{6,7},{7,6},{8,9},{9,8},{10,11... | collective-permute-start | bytes 884744 | tf_op jit(solution)/shard_map/ppermute | solution.py:269
  168.5 17.4 %collective-permute-start.71 = (bf16[192,768]{1,0:T(8,128)(2,1)S(1)}, bf16[192,768]{1,0:T(8,128)(2,1)S(1)}, u32[]{:S(2)}, u32[]{:S(2)}) collective-permute-start(bf16[192,768]{1,0:T(8,128)(2,1)S(1)} %fusion.15), channel_id=1, source_target_pairs={{0,4},{2,6},{4,0},{6,2},{8,12},{10,14},{12,8},{14,10},{16,20},{18,... | collective-permute-start | bytes 884744 | tf_op jit(solution)/shard_map/ppermute | solution.py:429
  168.9 17.1 %collective-permute-start.54 = (bf16[192,768]{1,0:T(8,128)(2,1)S(1)}, bf16[192,768]{1,0:T(8,128)(2,1)S(1)}, u32[]{:S(2)}, u32[]{:S(2)}) collective-permute-start(bf16[192,768]{1,0:T(8,128)(2,1)S(1)} %get-tuple-element.175), channel_id=1, source_target_pairs={{0,1},{1,0},{2,3},{3,2},{4,5},{5,4},{6,7},{7,6},{8,9},{9,8},{10,11... | collective-permute-start | bytes 884744 | tf_op jit(solution)/shard_map/ppermute | solution.py:269
  169.7 15.6 %collective-permute-start.59 = (bf16[192,768]{1,0:T(8,128)(2,1)S(1)}, bf16[192,768]{1,0:T(8,128)(2,1)S(1)}, u32[]{:S(2)}, u32[]{:S(2)}) collective-permute-start(bf16[192,768]{1,0:T(8,128)(2,1)S(1)} %get-tuple-element.181), channel_id=1, source_target_pairs={{0,1},{1,0},{2,3},{3,2},{4,5},{5,4},{6,7},{7,6},{8,9},{9,8},{10,11... | collective-permute-start | bytes 884744 | tf_op jit(solution)/shard_map/ppermute | solution.py:269
  171.0 15.8 %collective-permute-start.66 = (bf16[2,192,768]{2,1,0:T(8,128)(2,1)S(1)}, bf16[2,192,768]{2,1,0:T(8,128)(2,1)S(1)}, u32[]{:S(2)}, u32[]{:S(2)}) collective-permute-start(bf16[2,192,768]{2,1,0:T(8,128)(2,1)S(1)} %pad_maximum_fusion.2), channel_id=1, source_target_pairs={{0,8},{2,10},{4,12},{6,14},{8,16},{10,18},{12,20},{14,22},{16,24},... | collective-permute-start | bytes 1769480 | tf_op jit(solution)/shard_map/ppermute | solution.py:425
  186.9 13.1 %collective-permute-start.75 = (bf16[192,768]{1,0:T(8,128)(2,1)S(1)}, bf16[192,768]{1,0:T(8,128)(2,1)S(1)}, u32[]{:S(2)}, u32[]{:S(2)}) collective-permute-start(bf16[192,768]{1,0:T(8,128)(2,1)S(1)} %fusion.14), channel_id=1, source_target_pairs={{0,4},{2,6},{4,0},{6,2},{8,12},{10,14},{12,8},{14,10},{16,20},{18,... | collective-permute-start | bytes 884744 | tf_op jit(solution)/shard_map/ppermute | solution.py:429
  188.6 12.0 %collective-permute-start.55 = (bf16[256,768]{1,0:T(8,128)(2,1)S(1)}, bf16[256,768]{1,0:T(8,128)(2,1)S(1)}, u32[]{:S(2)}, u32[]{:S(2)}) collective-permute-start(bf16[256,768]{1,0:T(8,128)(2,1)S(1)} %get-tuple-element.176), channel_id=1, source_target_pairs={{2,1},{1,2},{6,5},{5,6},{10,9},{9,10},{14,13},{13,14},{18,17},{17,... | collective-permute-start | bytes 1179656 | tf_op jit(solution)/shard_map/ppermute | solution.py:277
  189.5 13.0 %collective-permute-start.60 = (bf16[256,768]{1,0:T(8,128)(2,1)S(1)}, bf16[256,768]{1,0:T(8,128)(2,1)S(1)}, u32[]{:S(2)}, u32[]{:S(2)}) collective-permute-start(bf16[256,768]{1,0:T(8,128)(2,1)S(1)} %get-tuple-element.182), channel_id=1, source_target_pairs={{2,0},{3,2},{1,3},{0,1},{6,4},{7,6},{5,7},{4,5},{10,8},{11,10},{9,... | collective-permute-start | bytes 1179656 | tf_op jit(solution)/shard_map/ppermute | solution.py:289
  200.7 18.0 %collective-permute-start.81 = (bf16[2,192,768]{2,1,0:T(8,128)(2,1)S(1)}, bf16[2,192,768]{2,1,0:T(8,128)(2,1)S(1)}, u32[]{:S(2)}, u32[]{:S(2)}) collective-permute-start(bf16[2,192,768]{2,1,0:T(8,128)(2,1)S(1)} %maximum_add_fusion.1), channel_id=1, source_target_pairs={{0,8},{2,10},{4,12},{6,14},{8,16},{10,18},{12,20},{14,22},{16,24},... | collective-permute-start | bytes 1769480 | tf_op jit(solution)/shard_map/ppermute | solution.py:425
  203.5 23.0 %collective-permute-start.69 = (bf16[2,208,768]{2,1,0:T(8,128)(2,1)S(1)}, bf16[2,208,768]{2,1,0:T(8,128)(2,1)S(1)}, u32[]{:S(2)}, u32[]{:S(2)}) collective-permute-start(bf16[2,208,768]{2,1,0:T(8,128)(2,1)S(1)} %get-tuple-element.208), channel_id=1, source_target_pairs={{0,2},{2,0},{4,6},{6,4},{8,10},{10,8},{12,14},{14,12},{16,18},{18,... | collective-permute-start | bytes 1916936 | tf_op jit(solution)/shard_map/ppermute | solution.py:265
  203.5 15.4 %collective-permute-start.74 = (bf16[2,208,768]{2,1,0:T(8,128)(2,1)S(1)}, bf16[2,208,768]{2,1,0:T(8,128)(2,1)S(1)}, u32[]{:S(2)}, u32[]{:S(2)}) collective-permute-start(bf16[2,208,768]{2,1,0:T(8,128)(2,1)S(1)} %get-tuple-element.214), channel_id=1, source_target_pairs={{0,2},{2,0},{4,6},{6,4},{8,10},{10,8},{12,14},{14,12},{16,18},{18,... | collective-permute-start | bytes 1916936 | tf_op jit(solution)/shard_map/ppermute | solution.py:265
  204.2 15.2 %collective-permute-start.72 = (bf16[208,768]{1,0:T(8,128)(2,1)S(1)}, bf16[208,768]{1,0:T(8,128)(2,1)S(1)}, u32[]{:S(2)}, u32[]{:S(2)}) collective-permute-start(bf16[208,768]{1,0:T(8,128)(2,1)S(1)} %slice_bitcast_fusion.9), channel_id=1, source_target_pairs={{0,4},{2,6},{4,0},{6,2},{8,12},{10,14},{12,8},{14,10},{16,20},{18,... | collective-permute-start | bytes 958472 | tf_op jit(solution)/shard_map/ppermute | solution.py:429
  212.7 12.9 %collective-permute-start.79 = (bf16[208,768]{1,0:T(8,128)(2,1)S(1)}, bf16[208,768]{1,0:T(8,128)(2,1)S(1)}, u32[]{:S(2)}, u32[]{:S(2)}) collective-permute-start(bf16[208,768]{1,0:T(8,128)(2,1)S(1)} %fusion), channel_id=1, source_target_pairs={{0,8},{2,10},{4,12},{6,14},{8,16},{10,18},{12,20},{14,22},{16,24},... | collective-permute-start | bytes 958472 | tf_op jit(solution)/shard_map/ppermute | solution.py:425
  218.8 25.7 %collective-permute-start.82 = (bf16[2,192,768]{2,1,0:T(8,128)(2,1)S(1)}, bf16[2,192,768]{2,1,0:T(8,128)(2,1)S(1)}, u32[]{:S(2)}, u32[]{:S(2)}) collective-permute-start(bf16[2,192,768]{2,1,0:T(8,128)(2,1)S(1)} %maximum_add_fusion), channel_id=1, source_target_pairs={{0,8},{2,10},{4,12},{6,14},{8,16},{10,18},{12,20},{14,22},{16,24},... | collective-permute-start | bytes 1769480 | tf_op jit(solution)/shard_map/ppermute | solution.py:425
  225.6 18.5 %collective-permute-start.80 = (bf16[208,768]{1,0:T(8,128)(2,1)S(1)}, bf16[208,768]{1,0:T(8,128)(2,1)S(1)}, u32[]{:S(2)}, u32[]{:S(2)}) collective-permute-start(bf16[208,768]{1,0:T(8,128)(2,1)S(1)} %fusion.2), channel_id=1, source_target_pairs={{0,8},{2,10},{4,12},{6,14},{8,16},{10,18},{12,20},{14,22},{16,24},... | collective-permute-start | bytes 958472 | tf_op jit(solution)/shard_map/ppermute | solution.py:425
  225.8 19.0 %collective-permute-start.67 = (bf16[256,768]{1,0:T(8,128)(2,1)S(1)}, bf16[256,768]{1,0:T(8,128)(2,1)S(1)}, u32[]{:S(2)}, u32[]{:S(2)}) collective-permute-start(bf16[256,768]{1,0:T(8,128)(2,1)S(1)} %get-tuple-element.205), channel_id=1, source_target_pairs={{2,1},{1,2},{6,5},{5,6},{10,9},{9,10},{14,13},{13,14},{18,17},{17,... | collective-permute-start | bytes 1179656 | tf_op jit(solution)/shard_map/ppermute | solution.py:277
  226.6 17.9 %collective-permute-start.85 = (bf16[192,768]{1,0:T(8,128)(2,1)S(1)}, bf16[192,768]{1,0:T(8,128)(2,1)S(1)}, u32[]{:S(2)}, u32[]{:S(2)}) collective-permute-start(bf16[192,768]{1,0:T(8,128)(2,1)S(1)} %fusion.7), channel_id=1, source_target_pairs={{0,4},{2,6},{4,0},{6,2},{8,12},{10,14},{12,8},{14,10},{16,20},{18,... | collective-permute-start | bytes 884744 | tf_op jit(solution)/shard_map/ppermute | solution.py:429
  227.0 27.7 %collective-permute-start.68 = (bf16[256,768]{1,0:T(8,128)(2,1)S(1)}, bf16[256,768]{1,0:T(8,128)(2,1)S(1)}, u32[]{:S(2)}, u32[]{:S(2)}) collective-permute-start(bf16[256,768]{1,0:T(8,128)(2,1)S(1)} %get-tuple-element.206), channel_id=1, source_target_pairs={{2,0},{3,2},{1,3},{0,1},{6,4},{7,6},{5,7},{4,5},{10,8},{11,10},{9,... | collective-permute-start | bytes 1179656 | tf_op jit(solution)/shard_map/ppermute | solution.py:289
  244.7 16.3 %collective-permute-start.86 = (bf16[2,192,768]{2,1,0:T(8,128)(2,1)S(1)}, bf16[2,192,768]{2,1,0:T(8,128)(2,1)S(1)}, u32[]{:S(2)}, u32[]{:S(2)}) collective-permute-start(bf16[2,192,768]{2,1,0:T(8,128)(2,1)S(1)} %maximum_add_fusion.2.tail), channel_id=1, source_target_pairs={{0,1},{1,0},{2,3},{3,2},{4,5},{5,4},{6,7},{7,6},{8,9},{9,8},{10,11... | collective-permute-start | bytes 1769480 | tf_op jit(solution)/shard_map/ppermute | solution.py:269
  254.7 11.3 %collective-permute-start.84 = (bf16[208,768]{1,0:T(8,128)(2,1)S(1)}, bf16[208,768]{1,0:T(8,128)(2,1)S(1)}, u32[]{:S(2)}, u32[]{:S(2)}) collective-permute-start(bf16[208,768]{1,0:T(8,128)(2,1)S(1)} %fusion.6.head), channel_id=1, source_target_pairs={{0,1},{1,0},{2,3},{3,2},{4,5},{5,4},{6,7},{7,6},{8,9},{9,8},{10,11... | collective-permute-start | bytes 958472 | tf_op jit(solution)/shard_map/ppermute | solution.py:269
  (95 other events, 792.1 us)

commit v7 on v6

--- a/solution.py
+++ b/solution.py
@@ -708,8 +708,8 @@
 
 def ffn_kernel(place, *refs):
     pieces, refs = refs[:32], refs[32:]
-    m_far, n2_ref, gy_ref, packed, v48, v192, out_ref, dm_ref, dz_ref, do_ref, g48, g192 = refs[:12]
-    outs, (weights, grads, y, dn2, n2_t, u, df, m_ref, merge_weight, in_sems, out_sems, late_sems) = refs[12:20], refs[20:]
+    m_far, n2_ref, gy_ref, packed, v48, v192, out_ref, dm_ref, do_ref, g48, g192 = refs[:11]
+    outs, (weights, grads, y, dn2, n2_t, u, df, m_ref, merge_weight, in_sems, out_sems, late_sems) = refs[11:19], refs[19:]
     z, x, core, half = spot(place)
     slots = ring_slots(z, x)
     spots = [(slot + core, half) for slot in slots] + [(slot + core, 1 - half) for slot in slots]
@@ -784,7 +784,6 @@
     middle_grad = out_grad + norm_back(second_grad, v48[4:5, :], shape, scale)
     dm_ref[...] = middle_grad
     low = middle_grad.astype(BF16)
-    dz_ref[...] = low
     g48[...] = jnp.zeros_like(g48)
     g48[3:4, :] = row_sum(low.astype(F32))
     g48[4:5, :] = row_sum(shape * second_grad)
@@ -800,7 +799,7 @@
     ff = 4 * width
     tail_rows = pieces[0].shape[0]
     shapes = [
-        ((rows, width), BF16), ((rows, width), F32), ((rows, width), BF16), ((rows, width), BF16),
+        ((rows, width), BF16), ((rows, width), F32), ((rows, width), BF16),
         ((8, width), F32), ((8, ff), F32),
     ]
     part = jax.ShapeDtypeStruct((2, 2, tail_rows, width), BF16)
@@ -821,12 +820,12 @@
         ],
         "ffn", 12 * rows * width * ff, 8 * width * ff,
     )
-    return results[:6], results[6:]
+    return results[:5], results[5:]
 
 
 def close_kernel(
     place, n1_ref, x_ref, q1, k1, v1, far_k1, far_v1, q2, k2, v2, far_k2, far_v2, o1, o2,
-    dz_ref, dm_ref, packed, v48, g48_in, g192, *refs,
+    dm_ref, packed, v48, g48_in, g192, *refs,
 ):
     join = lambda first, second: jnp.concatenate([first[...], second[...]], axis=1)
     grad_ref, outs, (grads, g48, g96, dt, sems) = refs[0], refs[1:9], refs[9:]
@@ -848,7 +847,7 @@
         term = dot(dt[...], weight, 1, 1)
         normed_grad = term if normed_grad is None else normed_grad + term
         grads[:, at * part : (at + 1) * part, :] = dot(normed_t, dt[...], 1, 0).astype(BF16).reshape(GROUPS, part, width)
-    grads[:, 3 * part : 4 * part, :] = dot(join(o1, o2), dz_ref[...], 0, 0).astype(BF16).reshape(GROUPS, part, width)
+    grads[:, 3 * part : 4 * part, :] = dot(join(o1, o2), dm_ref[...].astype(BF16), 0, 0).astype(BF16).reshape(GROUPS, part, width)
     shape, scale = normalise(x_ref[...].astype(F32))
     g48[...] = g48_in[...]
     g48[0:1, :] = row_sum(shape * normed_grad)
@@ -882,7 +881,7 @@
 
 def close(place, args):
     rows, width = args[0].shape
-    packed = args[16]
+    packed = args[15]
     head_rows = packed.shape[1]
     part = jax.ShapeDtypeStruct((2, head_rows, width), BF16)
     results = kernel_call(
@@ -957,7 +956,7 @@
     ]
     tail_pieces = tail_pieces + late(tail_pieces, 4)
     tail_other = tail_other + late(tail_other, 5)
-    (output, middle_grad, branch_grad, attended_grad, g48, g192), tail_parts = ffn(
+    (output, middle_grad, attended_grad, g48, g192), tail_parts = ffn(
         place, tail_pieces[:8] + tail_other[:8] + tail_pieces[8:] + tail_other[8:],
         middle, second, out_grad, packed, v48, v192,
     )
@@ -988,7 +987,7 @@
     input_grad, head_parts = close(
         place,
         [
-            normed, values, *grads, *attended, branch_grad, middle_grad, packed, v48, g48, g192,
+            normed, values, *grads, *attended, middle_grad, packed, v48, g48, g192,
         ],
     )
     came = [swap_cores(send, 16) for send in head_parts[1::2]]

time: 274 us -> 275 us (level)
    unnamed x81 -> x91, local copies, waits for them, and re-layouts: 11.9 us -> 12.6 us
where the time goes in v7:
time: 275 us; the launch traced here: 270 us
  waiting for transfers between devices  117 us (43%)
  Pallas kernels  69.1 us (25%)
  starting transfers between devices  61.2 us (22%)
  local copies, waits for them, and re-layouts  13.7 us (5%)
  other arithmetic  6.84 us (2%)
    pallas_call x6, Pallas kernels, kernel_call(): pl.pallas_call(body, grid_spec=pltpu.PrefetchScalarGridSpec(num_scalar_pr...  46.2 us
    ppermute x12, waiting for transfers between devices, shift_z(): lax.ppermute(value, 'dp', pairs_of(16, lambda index: (index + 4) % 16))  44.9 us
    ppermute x14, waiting for transfers between devices, swap_seq(): return lax.ppermute(value, 'seq', [(0, 1), (1, 0)])  39.2 us
    ppermute x16, waiting for transfers between devices, swap_x(): return lax.ppermute(value, 'dp', pairs_of(16, lambda index: index ^ 2))  26.6 us
    pallas_call x4, Pallas kernels, balanced(): pl.pallas_call(functools.partial(body, block=rows // 2), grid_spec=pltpu....  22.9 us
    ppermute x16, starting transfers between devices, swap_x(): return lax.ppermute(value, 'dp', pairs_of(16, lambda index: index ^ 2))  14.8 us
    ppermute x14, starting transfers between devices, swap_seq(): return lax.ppermute(value, 'seq', [(0, 1), (1, 0)])  13.5 us
    unnamed x91, local copies, waits for them, and re-layouts  12.6 us
  transfers between devices with their start and end apart: 87, of which 30 were waited for; matrix products, arithmetic and copies ran while one was open for 4% of the time, Pallas kernels for 12%

profile of v7, /device:TPU:0, one launch (start us, length us, event | category | flops | bytes accessed | tf_op | source)
XLA Modules:
  0.0 270.0 jit_solution(13264714723133002375)
XLA Ops:
  1.2 3.3 %pack.1 = (bf16[208,768]{1,0:T(8,128)(2,1)}, bf16[192,768]{1,0:T(8,128)(2,1)}) custom-call(s32[12]{0:T(128)} %slots.3, s32[2]{0:T(128)} %pad_add_fusion.place, f32[2,48]{1,0:T(2,128)} %refs_0_.1, f32[2,48]{1,0:T(2,128)} %refs_1_.1, f32[2,48,2304]{2,1,0:T(8,128)} %refs_2_.1, f32[2,96]{1,0:T(2,128)} %refs_3_.1, f32[2,48,768]{2,1,0:T(8,128)} %refs_4_.1, ...), custom_call_target="tpu_custom_call" | custom-call | bytes 1916928 | tf_op jit(solution)/shard_map/pack/pallas_call | solution.py:363
  4.5 2.9 %collective-permute-start = (bf16[208,768]{1,0:T(8,128)(2,1)}, bf16[208,768]{1,0:T(8,128)(2,1)S(1)}, u32[]{:S(2)}, u32[]{:S(2)}) collective-permute-start(bf16[208,768]{1,0:T(8,128)(2,1)} %get-tuple-element.126.refs_0_), channel_id=1, source_target_pairs={{0,4},{2,6},{4,0},{6,2},{8,12},{10,14},{12,8},{14,10},{16,20},{18,... | collective-permute-start | bytes 958472 | tf_op jit(solution)/shard_map/ppermute | solution.py:429
  9.0 6.2 %collective-permute-done.refs_1_ = bf16[208,768]{1,0:T(8,128)(2,1)S(1)} collective-permute-done((bf16[208,768]{1,0:T(8,128)(2,1)}, bf16[208,768]{1,0:T(8,128)(2,1)S(1)}, u32[]{:S(2)}, u32[]{:S(2)}) %collective-permute-start) | collective-permute-done | bytes 319520 | tf_op jit(solution)/shard_map/ppermute | solution.py:429
  20.0 3.7 %collective-permute-done.1.refs_1_ = bf16[192,768]{1,0:T(8,128)(2,1)} collective-permute-done((bf16[192,768]{1,0:T(8,128)(2,1)}, bf16[192,768]{1,0:T(8,128)(2,1)}, u32[]{:S(2)}, u32[]{:S(2)}) %collective-permute-start.1) | collective-permute-done | bytes 294944 | tf_op jit(solution)/shard_map/ppermute | solution.py:429
  35.7 4.6 %collective-permute-done.5.refs_6_ = bf16[208,768]{1,0:T(8,128)(2,1)S(1)} collective-permute-done((bf16[208,768]{1,0:T(8,128)(2,1)S(1)}, bf16[208,768]{1,0:T(8,128)(2,1)S(1)}, u32[]{:S(2)}, u32[]{:S(2)}) %collective-permute-start.5) | collective-permute-done | bytes 319520 | tf_op jit(solution)/shard_map/ppermute | solution.py:425
  41.4 3.0 %collective-permute-done.3.refs_2_ = bf16[192,768]{1,0:T(8,128)(2,1)} collective-permute-done((bf16[192,768]{1,0:T(8,128)(2,1)S(1)}, bf16[192,768]{1,0:T(8,128)(2,1)}, u32[]{:S(2)}, u32[]{:S(2)}) %collective-permute-start.3) | collective-permute-done | bytes 294944 | tf_op jit(solution)/shard_map/ppermute | solution.py:425
  46.6 2.4 collective-permute-done.8.refs_7_
  51.2 7.3 %collective-permute-done.10.refs_4_ = bf16[192,768]{1,0:T(8,128)(2,1)} collective-permute-done((bf16[192,768]{1,0:T(8,128)(2,1)}, bf16[192,768]{1,0:T(8,128)(2,1)}, u32[]{:S(2)}, u32[]{:S(2)}) %collective-permute-start.10) | collective-permute-done | bytes 294944 | tf_op jit(solution)/shard_map/ppermute | solution.py:425
  59.9 2.4 broadcast_select_fusion.5
  63.9 4.9 %qkv.1 = (bf16[16,208,768]{2,1,0:T(8,128)(2,1)S(1)}, bf16[512,768]{1,0:T(8,128)(2,1)S(1)}, bf16[512,768]{1,0:T(8,128)(2,1)S(1)}, bf16[512,1536]{1,0:T(8,128)(2,1...) custom-call(s32[2]{0:T(128)S(1)} %copy-done.22, ...), custom_call_target="tpu_custom_call" | custom-call | flops 905969664 | bytes 5898240 | tf_op jit(solution)/shard_map/qkv/pallas_call | solution.py:363
  68.8 2.3 copy-done
  78.1 6.8 %collective-permute-done.20.refs_10_ = bf16[192,768]{1,0:T(8,128)(2,1)S(1)} collective-permute-done((bf16[192,768]{1,0:T(8,128)(2,1)}, bf16[192,768]{1,0:T(8,128)(2,1)S(1)}, u32[]{:S(2)}, u32[]{:S(2)}) %collective-permute-start.20) | collective-permute-done | bytes 294944 | tf_op jit(solution)/shard_map/ppermute | solution.py:269
  88.3 4.9 %attend.2 = (bf16[512,384]{1,0:T(8,128)(2,1)S(1)}, f32[3,2,512]{2,1,0:T(2,128)S(1)}) custom-call(s32[1]{0:T(128)} %bitcast.6.extra, bf16[512,768]{1,0:T(8,128)(2,1)S(1)} %copy-done.4, bf16[512,1536]{1,0:T(8,128)(2,1)S(1)} %get-tuple-element.148.k_ref.v_ref, bf16[512,1536]{1,0:T(8,128)(2,1)S(1)} %get-tuple-element.148.k_ref.v_ref, ...), custom_call_target="tpu_custom_call" | custom-call | flops 1000000 | bytes 1000 | tf_op jit(solution)/shard_map/attend/pallas_call | solution.py:615
  95.0 2.7 collective-permute-done.22.refs_12_
  97.6 4.9 %attend.3 = (bf16[512,384]{1,0:T(8,128)(2,1)S(1)}, f32[3,2,512]{2,1,0:T(2,128)S(1)}) custom-call(s32[1]{0:T(128)} %bitcast.6.extra, bf16[512,768]{1,0:T(8,128)(2,1)S(1)} %copy-done.4, bf16[512,1536]{1,0:T(8,128)(2,1)S(1)} %get-tuple-element.148.k_ref.v_ref, bf16[512,1536]{1,0:T(8,128)(2,1)S(1)} %get-tuple-element.148.k_ref.v_ref, ...), custom_call_target="tpu_custom_call" | custom-call | flops 1000000 | bytes 1000 | tf_op jit(solution)/shard_map/attend/pallas_call | solution.py:615
  106.3 7.4 %collective-permute-done.33.refs_14_ = bf16[192,768]{1,0:T(8,128)(2,1)S(1)} collective-permute-done((bf16[192,768]{1,0:T(8,128)(2,1)}, bf16[192,768]{1,0:T(8,128)(2,1)S(1)}, u32[]{:S(2)}, u32[]{:S(2)}) %collective-permute-start.33) | collective-permute-done | bytes 294944 | tf_op jit(solution)/shard_map/ppermute | solution.py:269
  113.8 5.5 %collective-permute-done.34.refs_15_ = bf16[192,768]{1,0:T(8,128)(2,1)S(1)} collective-permute-done((bf16[192,768]{1,0:T(8,128)(2,1)S(1)}, bf16[192,768]{1,0:T(8,128)(2,1)S(1)}, u32[]{:S(2)}, u32[]{:S(2)}) %collective-permute-start.34) | collective-permute-done | bytes 294944 | tf_op jit(solution)/shard_map/ppermute | solution.py:269
  123.8 26.4 %ffn.1 = (bf16[512,768]{1,0:T(8,128)(2,1)S(1)}, f32[512,768]{1,0:T(8,128)}, bf16[512,768]{1,0:T(8,128)(2,1)S(1)}, f32[8,768]{1,0:T(8,128)S(1)}, f32[8,3072]{1,0:...) custom-call(s32[2]{0:T(128)S(1)} %copy-done.22, ...), custom_call_target="tpu_custom_call" | custom-call | flops 7247757312 | bytes 9437184 | tf_op jit(solution)/shard_map/ffn/pallas_call | solution.py:363
  159.2 4.4 %collective-permute-done.58 = bf16[192,768]{1,0:T(8,128)(2,1)S(1)} collective-permute-done((bf16[192,768]{1,0:T(8,128)(2,1)S(1)}, bf16[192,768]{1,0:T(8,128)(2,1)S(1)}, u32[]{:S(2)}, u32[]{:S(2)}) %collective-permute-start.58) | collective-permute-done | bytes 294944 | tf_op jit(solution)/shard_map/ppermute | solution.py:269
  164.0 5.4 %collective-permute-done.53 = bf16[192,768]{1,0:T(8,128)(2,1)S(1)} collective-permute-done((bf16[192,768]{1,0:T(8,128)(2,1)S(1)}, bf16[192,768]{1,0:T(8,128)(2,1)S(1)}, u32[]{:S(2)}, u32[]{:S(2)}) %collective-permute-start.53) | collective-permute-done | bytes 294944 | tf_op jit(solution)/shard_map/ppermute | solution.py:269
  172.9 6.5 %attend_back.2 = (bf16[512,384]{1,0:T(8,128)(2,1)S(1)}, bf16[512,384]{1,0:T(8,128)(2,1)S(1)}, bf16[512,384]{1,0:T(8,128)(2,1)S(1)}, bf16[512,384]{1,0:T(8,128)(2,1)S(1)}, bf16[512,384]{1,0:T(8,128)(2,1)S(1)}) custom-call(s32[1]{0:T(128)} %bitcast.6.extra, bf16[512,768]{1,0:T(8,128)(2,1)S(1)} %copy-done.5, ...), custom_call_target="tpu_custom_call" | custom-call | flops 1000000 | bytes 1000 | tf_op jit(solution)/shard_map/attend_back/pallas_call | solution.py:615
  179.6 6.5 %attend_back.3 = (bf16[512,384]{1,0:T(8,128)(2,1)S(1)}, bf16[512,384]{1,0:T(8,128)(2,1)S(1)}, bf16[512,384]{1,0:T(8,128)(2,1)S(1)}, bf16[512,384]{1,0:T(8,128)(2,1)S(1)}, bf16[512,384]{1,0:T(8,128)(2,1)S(1)}) custom-call(s32[1]{0:T(128)} %bitcast.6.extra, bf16[512,768]{1,0:T(8,128)(2,1)S(1)} %copy-done.5, ...), custom_call_target="tpu_custom_call" | custom-call | flops 1000000 | bytes 1000 | tf_op jit(solution)/shard_map/attend_back/pallas_call | solution.py:615
  190.5 2.4 collective-permute-start.60
  192.9 7.8 %close.1 = (bf16[512,768]{1,0:T(8,128)(2,1)S(1)}, bf16[2,208,768]{2,1,0:T(8,128)(2,1)S(1)}, bf16[2,208,768]{2,1,0:T(8,128)(2,1)S(1)}, bf16[2,208,768]{2,1,0:T(8,...) custom-call(s32[2]{0:T(128)S(1)} %copy-done.22, ...), custom_call_target="tpu_custom_call" | custom-call | flops 2113929216 | bytes 5898240 | tf_op jit(solution)/shard_map/close/pallas_call | solution.py:363
  206.8 6.7 %collective-permute-done.78 = bf16[208,768]{1,0:T(8,128)(2,1)S(1)} collective-permute-done((bf16[208,768]{1,0:T(8,128)(2,1)S(1)}, bf16[208,768]{1,0:T(8,128)(2,1)S(1)}, u32[]{:S(2)}, u32[]{:S(2)}) %collective-permute-start.78) | collective-permute-done | bytes 319520 | tf_op jit(solution)/shard_map/ppermute | solution.py:429
  214.2 5.3 %collective-permute-done.81 = bf16[2,192,768]{2,1,0:T(8,128)(2,1)S(1)} collective-permute-done((bf16[2,192,768]{2,1,0:T(8,128)(2,1)S(1)}, bf16[2,192,768]{2,1,0:T(8,128)(2,1)S(1)}, u32[]{:S(2)}, u32[]{:S(2)}) %collective-permute-start.81) | collective-permute-done | bytes 589856 | tf_op jit(solution)/shard_map/ppermute | solution.py:425
  220.3 6.1 %collective-permute-done.79 = bf16[208,768]{1,0:T(8,128)(2,1)S(1)} collective-permute-done((bf16[208,768]{1,0:T(8,128)(2,1)S(1)}, bf16[208,768]{1,0:T(8,128)(2,1)S(1)}, u32[]{:S(2)}, u32[]{:S(2)}) %collective-permute-start.79) | collective-permute-done | bytes 319520 | tf_op jit(solution)/shard_map/ppermute | solution.py:425
  230.1 15.0 %collective-permute-done.80 = bf16[208,768]{1,0:T(8,128)(2,1)S(1)} collective-permute-done((bf16[208,768]{1,0:T(8,128)(2,1)S(1)}, bf16[208,768]{1,0:T(8,128)(2,1)S(1)}, u32[]{:S(2)}, u32[]{:S(2)}) %collective-permute-start.80) | collective-permute-done | bytes 319520 | tf_op jit(solution)/shard_map/ppermute | solution.py:425
  247.1 6.7 %collective-permute-done.73 = bf16[208,768]{1,0:T(8,128)(2,1)S(1)} collective-permute-done((bf16[208,768]{1,0:T(8,128)(2,1)S(1)}, bf16[208,768]{1,0:T(8,128)(2,1)S(1)}, u32[]{:S(2)}, u32[]{:S(2)}) %collective-permute-start.73) | collective-permute-done | bytes 319520 | tf_op jit(solution)/shard_map/ppermute | solution.py:429
  257.8 2.8 %copy.29 = f32[512,1,768]{2,1,0:T(1,128)} copy(f32[512,1,768]{2,0,1:T(8,128)S(1)} %maximum_convert_fusion) | data formatting | bytes 3145728
  261.9 5.0 %collective-permute-done.84.head_far = bf16[208,768]{1,0:T(8,128)(2,1)S(1)} collective-permute-done((bf16[208,768]{1,0:T(8,128)(2,1)S(1)}, bf16[208,768]{1,0:T(8,128)(2,1)S(1)}, u32[]{:S(2)}, u32[]{:S(2)}) %collective-permute-start.84) | collective-permute-done | bytes 319520 | tf_op jit(solution)/shard_map/ppermute | solution.py:269
  266.9 2.7 unpack.1
  (289 shorter events, 83.3 us)
Async XLA Ops:
  26.7 14.1 %collective-permute-start.18 = (bf16[256,768]{1,0:T(8,128)(2,1)S(1)}, bf16[256,768]{1,0:T(8,128)(2,1)}, u32[]{:S(2)}, u32[]{:S(2)}) collective-permute-start(bf16[256,768]{1,0:T(8,128)(2,1)S(1)} %get-tuple-element.140), channel_id=1, source_target_pairs={{0,2},{2,3},{3,1},{1,0},{4,6},{6,7},{7,5},{5,4},{8,10},{10,11},{11... | collective-permute-start | bytes 1179656 | tf_op jit(solution)/shard_map/ppermute | solution.py:289
  28.9 11.4 %collective-permute-start.5 = (bf16[208,768]{1,0:T(8,128)(2,1)S(1)}, bf16[208,768]{1,0:T(8,128)(2,1)S(1)}, u32[]{:S(2)}, u32[]{:S(2)}) collective-permute-start(bf16[208,768]{1,0:T(8,128)(2,1)S(1)} %collective-permute-done.4.refs_4_), channel_id=1, source_target_pairs={{0,8},{2,10},{4,12},{6,14},{8,16},{10,18},{12,20},{14,22},{16,24},... | collective-permute-start | bytes 958472 | tf_op jit(solution)/shard_map/ppermute | solution.py:425
  33.4 13.1 %collective-permute-start.16 = (bf16[256,768]{1,0:T(8,128)(2,1)S(1)}, bf16[256,768]{1,0:T(8,128)(2,1)S(1)}, u32[]{:S(2)}, u32[]{:S(2)}) collective-permute-start(bf16[256,768]{1,0:T(8,128)(2,1)S(1)} %get-tuple-element.138), channel_id=1, source_target_pairs={{2,1},{1,2},{6,5},{5,6},{10,9},{9,10},{14,13},{13,14},{18,17},{17,... | collective-permute-start | bytes 1179656 | tf_op jit(solution)/shard_map/ppermute | solution.py:277
  44.4 15.0 %collective-permute-start.19 = (bf16[256,768]{1,0:T(8,128)(2,1)}, bf16[256,768]{1,0:T(8,128)(2,1)}, u32[]{:S(2)}, u32[]{:S(2)}) collective-permute-start(bf16[256,768]{1,0:T(8,128)(2,1)} %get-tuple-element.141), channel_id=1, source_target_pairs={{0,2},{2,3},{3,1},{1,0},{4,6},{6,7},{7,5},{5,4},{8,10},{10,11},{11... | collective-permute-start | bytes 1179656 | tf_op jit(solution)/shard_map/ppermute | solution.py:289
  51.2 11.3 %collective-permute-start.27 = (bf16[208,768]{1,0:T(8,128)(2,1)S(1)}, bf16[208,768]{1,0:T(8,128)(2,1)S(1)}, u32[]{:S(2)}, u32[]{:S(2)}) collective-permute-start(bf16[208,768]{1,0:T(8,128)(2,1)S(1)} %collective-permute-done.4.refs_4_), channel_id=1, source_target_pairs={{0,2},{2,0},{4,6},{6,4},{8,10},{10,8},{12,14},{14,12},{16,18},{18,... | collective-permute-start | bytes 958472 | tf_op jit(solution)/shard_map/ppermute | solution.py:265
  74.1 13.0 %collective-permute-start.31 = (bf16[512,1536]{1,0:T(8,128)(2,1)S(1)}, bf16[512,1536]{1,0:T(8,128)(2,1)S(1)}, u32[]{:S(2)}, u32[]{:S(2)}) collective-permute-start(bf16[512,1536]{1,0:T(8,128)(2,1)S(1)} %get-tuple-element.148.k_ref.v_ref), channel_id=1, source_target_pairs={{0,2},{2,0},{4,6},{6,4},{8,10},{10,8},{12,14},{14,12},{16,18},{18,... | collective-permute-start | bytes 4718600 | tf_op jit(solution)/shard_map/ppermute | solution.py:265
  77.3 16.0 %collective-permute-start.21 = (bf16[192,768]{1,0:T(8,128)(2,1)}, bf16[192,768]{1,0:T(8,128)(2,1)}, u32[]{:S(2)}, u32[]{:S(2)}) collective-permute-start(bf16[192,768]{1,0:T(8,128)(2,1)} %collective-permute-done.9.refs_3_), channel_id=1, source_target_pairs={{0,1},{1,0},{2,3},{3,2},{4,5},{5,4},{6,7},{7,6},{8,9},{9,8},{10,11... | collective-permute-start | bytes 884744 | tf_op jit(solution)/shard_map/ppermute | solution.py:269
  84.9 12.7 %collective-permute-start.22 = (bf16[192,768]{1,0:T(8,128)(2,1)}, bf16[192,768]{1,0:T(8,128)(2,1)}, u32[]{:S(2)}, u32[]{:S(2)}) collective-permute-start(bf16[192,768]{1,0:T(8,128)(2,1)} %collective-permute-done.10.refs_4_), channel_id=1, source_target_pairs={{0,1},{1,0},{2,3},{3,2},{4,5},{5,4},{6,7},{7,6},{8,9},{9,8},{10,11... | collective-permute-start | bytes 884744 | tf_op jit(solution)/shard_map/ppermute | solution.py:269
  86.6 16.0 %collective-permute-start.13 = (bf16[192,768]{1,0:T(8,128)(2,1)}, bf16[192,768]{1,0:T(8,128)(2,1)S(1)}, u32[]{:S(2)}, u32[]{:S(2)}) collective-permute-start(bf16[192,768]{1,0:T(8,128)(2,1)} %collective-permute-done.12.refs_6_), channel_id=1, source_target_pairs={{0,4},{2,6},{4,0},{6,2},{8,12},{10,14},{12,8},{14,10},{16,20},{18,... | collective-permute-start | bytes 884744 | tf_op jit(solution)/shard_map/ppermute | solution.py:429
  104.3 14.9 %collective-permute-start.34 = (bf16[192,768]{1,0:T(8,128)(2,1)S(1)}, bf16[192,768]{1,0:T(8,128)(2,1)S(1)}, u32[]{:S(2)}, u32[]{:S(2)}) collective-permute-start(bf16[192,768]{1,0:T(8,128)(2,1)S(1)} %collective-permute-done.13.refs_7_), channel_id=1, source_target_pairs={{0,1},{1,0},{2,3},{3,2},{4,5},{5,4},{6,7},{7,6},{8,9},{9,8},{10,11... | collective-permute-start | bytes 884744 | tf_op jit(solution)/shard_map/ppermute | solution.py:269
  105.7 13.5 %collective-permute-start.47 = (bf16[192,768]{1,0:T(8,128)(2,1)}, bf16[192,768]{1,0:T(8,128)(2,1)S(1)}, u32[]{:S(2)}, u32[]{:S(2)}) collective-permute-start(bf16[192,768]{1,0:T(8,128)(2,1)} %collective-permute-done.22.refs_12_), channel_id=1, source_target_pairs={{0,2},{2,0},{4,6},{6,4},{8,10},{10,8},{12,14},{14,12},{16,18},{18,... | collective-permute-start | bytes 884744 | tf_op jit(solution)/shard_map/ppermute | solution.py:265
  105.8 14.0 %collective-permute-start.38 = (bf16[192,768]{1,0:T(8,128)(2,1)}, bf16[192,768]{1,0:T(8,128)(2,1)S(1)}, u32[]{:S(2)}, u32[]{:S(2)}) collective-permute-start(bf16[192,768]{1,0:T(8,128)(2,1)} %collective-permute-done.9.refs_3_), channel_id=1, source_target_pairs={{0,2},{2,0},{4,6},{6,4},{8,10},{10,8},{12,14},{14,12},{16,18},{18,... | collective-permute-start | bytes 884744 | tf_op jit(solution)/shard_map/ppermute | solution.py:265
  106.3 13.6 %collective-permute-start.46 = (bf16[192,768]{1,0:T(8,128)(2,1)}, bf16[192,768]{1,0:T(8,128)(2,1)S(1)}, u32[]{:S(2)}, u32[]{:S(2)}) collective-permute-start(bf16[192,768]{1,0:T(8,128)(2,1)} %collective-permute-done.21.refs_11_), channel_id=1, source_target_pairs={{0,2},{2,0},{4,6},{6,4},{8,10},{10,8},{12,14},{14,12},{16,18},{18,... | collective-permute-start | bytes 884744 | tf_op jit(solution)/shard_map/ppermute | solution.py:265
  157.0 12.4 %collective-permute-start.53 = (bf16[192,768]{1,0:T(8,128)(2,1)S(1)}, bf16[192,768]{1,0:T(8,128)(2,1)S(1)}, u32[]{:S(2)}, u32[]{:S(2)}) collective-permute-start(bf16[192,768]{1,0:T(8,128)(2,1)S(1)} %get-tuple-element.259), channel_id=1, source_target_pairs={{0,1},{1,0},{2,3},{3,2},{4,5},{5,4},{6,7},{7,6},{8,9},{9,8},{10,11... | collective-permute-start | bytes 884744 | tf_op jit(solution)/shard_map/ppermute | solution.py:269
  169.4 17.3 %collective-permute-start.71 = (bf16[192,768]{1,0:T(8,128)(2,1)S(1)}, bf16[192,768]{1,0:T(8,128)(2,1)S(1)}, u32[]{:S(2)}, u32[]{:S(2)}) collective-permute-start(bf16[192,768]{1,0:T(8,128)(2,1)S(1)} %fusion.15), channel_id=1, source_target_pairs={{0,4},{2,6},{4,0},{6,2},{8,12},{10,14},{12,8},{14,10},{16,20},{18,... | collective-permute-start | bytes 884744 | tf_op jit(solution)/shard_map/ppermute | solution.py:429
  169.7 17.1 %collective-permute-start.54 = (bf16[192,768]{1,0:T(8,128)(2,1)S(1)}, bf16[192,768]{1,0:T(8,128)(2,1)S(1)}, u32[]{:S(2)}, u32[]{:S(2)}) collective-permute-start(bf16[192,768]{1,0:T(8,128)(2,1)S(1)} %get-tuple-element.174), channel_id=1, source_target_pairs={{0,1},{1,0},{2,3},{3,2},{4,5},{5,4},{6,7},{7,6},{8,9},{9,8},{10,11... | collective-permute-start | bytes 884744 | tf_op jit(solution)/shard_map/ppermute | solution.py:269
  170.6 15.5 %collective-permute-start.59 = (bf16[192,768]{1,0:T(8,128)(2,1)S(1)}, bf16[192,768]{1,0:T(8,128)(2,1)S(1)}, u32[]{:S(2)}, u32[]{:S(2)}) collective-permute-start(bf16[192,768]{1,0:T(8,128)(2,1)S(1)} %get-tuple-element.180), channel_id=1, source_target_pairs={{0,1},{1,0},{2,3},{3,2},{4,5},{5,4},{6,7},{7,6},{8,9},{9,8},{10,11... | collective-permute-start | bytes 884744 | tf_op jit(solution)/shard_map/ppermute | solution.py:269
  171.9 15.9 %collective-permute-start.66 = (bf16[2,192,768]{2,1,0:T(8,128)(2,1)S(1)}, bf16[2,192,768]{2,1,0:T(8,128)(2,1)S(1)}, u32[]{:S(2)}, u32[]{:S(2)}) collective-permute-start(bf16[2,192,768]{2,1,0:T(8,128)(2,1)S(1)} %pad_maximum_fusion.2), channel_id=1, source_target_pairs={{0,8},{2,10},{4,12},{6,14},{8,16},{10,18},{12,20},{14,22},{16,24},... | collective-permute-start | bytes 1769480 | tf_op jit(solution)/shard_map/ppermute | solution.py:425
  187.8 13.0 %collective-permute-start.75 = (bf16[192,768]{1,0:T(8,128)(2,1)S(1)}, bf16[192,768]{1,0:T(8,128)(2,1)S(1)}, u32[]{:S(2)}, u32[]{:S(2)}) collective-permute-start(bf16[192,768]{1,0:T(8,128)(2,1)S(1)} %fusion.14), channel_id=1, source_target_pairs={{0,4},{2,6},{4,0},{6,2},{8,12},{10,14},{12,8},{14,10},{16,20},{18,... | collective-permute-start | bytes 884744 | tf_op jit(solution)/shard_map/ppermute | solution.py:429
  189.5 11.9 %collective-permute-start.55 = (bf16[256,768]{1,0:T(8,128)(2,1)S(1)}, bf16[256,768]{1,0:T(8,128)(2,1)S(1)}, u32[]{:S(2)}, u32[]{:S(2)}) collective-permute-start(bf16[256,768]{1,0:T(8,128)(2,1)S(1)} %get-tuple-element.175), channel_id=1, source_target_pairs={{2,1},{1,2},{6,5},{5,6},{10,9},{9,10},{14,13},{13,14},{18,17},{17,... | collective-permute-start | bytes 1179656 | tf_op jit(solution)/shard_map/ppermute | solution.py:277
  190.5 12.9 %collective-permute-start.60 = (bf16[256,768]{1,0:T(8,128)(2,1)S(1)}, bf16[256,768]{1,0:T(8,128)(2,1)S(1)}, u32[]{:S(2)}, u32[]{:S(2)}) collective-permute-start(bf16[256,768]{1,0:T(8,128)(2,1)S(1)} %get-tuple-element.181), channel_id=1, source_target_pairs={{2,0},{3,2},{1,3},{0,1},{6,4},{7,6},{5,7},{4,5},{10,8},{11,10},{9,... | collective-permute-start | bytes 1179656 | tf_op jit(solution)/shard_map/ppermute | solution.py:289
  201.5 18.0 %collective-permute-start.81 = (bf16[2,192,768]{2,1,0:T(8,128)(2,1)S(1)}, bf16[2,192,768]{2,1,0:T(8,128)(2,1)S(1)}, u32[]{:S(2)}, u32[]{:S(2)}) collective-permute-start(bf16[2,192,768]{2,1,0:T(8,128)(2,1)S(1)} %maximum_add_fusion.1), channel_id=1, source_target_pairs={{0,8},{2,10},{4,12},{6,14},{8,16},{10,18},{12,20},{14,22},{16,24},... | collective-permute-start | bytes 1769480 | tf_op jit(solution)/shard_map/ppermute | solution.py:425
  204.3 22.9 %collective-permute-start.69 = (bf16[2,208,768]{2,1,0:T(8,128)(2,1)S(1)}, bf16[2,208,768]{2,1,0:T(8,128)(2,1)S(1)}, u32[]{:S(2)}, u32[]{:S(2)}) collective-permute-start(bf16[2,208,768]{2,1,0:T(8,128)(2,1)S(1)} %get-tuple-element.206), channel_id=1, source_target_pairs={{0,2},{2,0},{4,6},{6,4},{8,10},{10,8},{12,14},{14,12},{16,18},{18,... | collective-permute-start | bytes 1916936 | tf_op jit(solution)/shard_map/ppermute | solution.py:265
  204.3 15.4 %collective-permute-start.74 = (bf16[2,208,768]{2,1,0:T(8,128)(2,1)S(1)}, bf16[2,208,768]{2,1,0:T(8,128)(2,1)S(1)}, u32[]{:S(2)}, u32[]{:S(2)}) collective-permute-start(bf16[2,208,768]{2,1,0:T(8,128)(2,1)S(1)} %get-tuple-element.212), channel_id=1, source_target_pairs={{0,2},{2,0},{4,6},{6,4},{8,10},{10,8},{12,14},{14,12},{16,18},{18,... | collective-permute-start | bytes 1916936 | tf_op jit(solution)/shard_map/ppermute | solution.py:265
  205.0 15.2 %collective-permute-start.72 = (bf16[208,768]{1,0:T(8,128)(2,1)S(1)}, bf16[208,768]{1,0:T(8,128)(2,1)S(1)}, u32[]{:S(2)}, u32[]{:S(2)}) collective-permute-start(bf16[208,768]{1,0:T(8,128)(2,1)S(1)} %slice_bitcast_fusion.9), channel_id=1, source_target_pairs={{0,4},{2,6},{4,0},{6,2},{8,12},{10,14},{12,8},{14,10},{16,20},{18,... | collective-permute-start | bytes 958472 | tf_op jit(solution)/shard_map/ppermute | solution.py:429
  213.5 12.9 %collective-permute-start.79 = (bf16[208,768]{1,0:T(8,128)(2,1)S(1)}, bf16[208,768]{1,0:T(8,128)(2,1)S(1)}, u32[]{:S(2)}, u32[]{:S(2)}) collective-permute-start(bf16[208,768]{1,0:T(8,128)(2,1)S(1)} %fusion), channel_id=1, source_target_pairs={{0,8},{2,10},{4,12},{6,14},{8,16},{10,18},{12,20},{14,22},{16,24},... | collective-permute-start | bytes 958472 | tf_op jit(solution)/shard_map/ppermute | solution.py:425
  219.6 25.7 %collective-permute-start.82 = (bf16[2,192,768]{2,1,0:T(8,128)(2,1)S(1)}, bf16[2,192,768]{2,1,0:T(8,128)(2,1)S(1)}, u32[]{:S(2)}, u32[]{:S(2)}) collective-permute-start(bf16[2,192,768]{2,1,0:T(8,128)(2,1)S(1)} %maximum_add_fusion), channel_id=1, source_target_pairs={{0,8},{2,10},{4,12},{6,14},{8,16},{10,18},{12,20},{14,22},{16,24},... | collective-permute-start | bytes 1769480 | tf_op jit(solution)/shard_map/ppermute | solution.py:425
  226.4 18.6 %collective-permute-start.80 = (bf16[208,768]{1,0:T(8,128)(2,1)S(1)}, bf16[208,768]{1,0:T(8,128)(2,1)S(1)}, u32[]{:S(2)}, u32[]{:S(2)}) collective-permute-start(bf16[208,768]{1,0:T(8,128)(2,1)S(1)} %fusion.2), channel_id=1, source_target_pairs={{0,8},{2,10},{4,12},{6,14},{8,16},{10,18},{12,20},{14,22},{16,24},... | collective-permute-start | bytes 958472 | tf_op jit(solution)/shard_map/ppermute | solution.py:425
  226.6 19.0 %collective-permute-start.67 = (bf16[256,768]{1,0:T(8,128)(2,1)S(1)}, bf16[256,768]{1,0:T(8,128)(2,1)S(1)}, u32[]{:S(2)}, u32[]{:S(2)}) collective-permute-start(bf16[256,768]{1,0:T(8,128)(2,1)S(1)} %get-tuple-element.203), channel_id=1, source_target_pairs={{2,1},{1,2},{6,5},{5,6},{10,9},{9,10},{14,13},{13,14},{18,17},{17,... | collective-permute-start | bytes 1179656 | tf_op jit(solution)/shard_map/ppermute | solution.py:277
  227.5 17.9 %collective-permute-start.85 = (bf16[192,768]{1,0:T(8,128)(2,1)S(1)}, bf16[192,768]{1,0:T(8,128)(2,1)S(1)}, u32[]{:S(2)}, u32[]{:S(2)}) collective-permute-start(bf16[192,768]{1,0:T(8,128)(2,1)S(1)} %fusion.7), channel_id=1, source_target_pairs={{0,4},{2,6},{4,0},{6,2},{8,12},{10,14},{12,8},{14,10},{16,20},{18,... | collective-permute-start | bytes 884744 | tf_op jit(solution)/shard_map/ppermute | solution.py:429
  227.9 27.9 %collective-permute-start.68 = (bf16[256,768]{1,0:T(8,128)(2,1)S(1)}, bf16[256,768]{1,0:T(8,128)(2,1)S(1)}, u32[]{:S(2)}, u32[]{:S(2)}) collective-permute-start(bf16[256,768]{1,0:T(8,128)(2,1)S(1)} %get-tuple-element.204), channel_id=1, source_target_pairs={{2,0},{3,2},{1,3},{0,1},{6,4},{7,6},{5,7},{4,5},{10,8},{11,10},{9,... | collective-permute-start | bytes 1179656 | tf_op jit(solution)/shard_map/ppermute | solution.py:289
  245.5 16.3 %collective-permute-start.86 = (bf16[2,192,768]{2,1,0:T(8,128)(2,1)S(1)}, bf16[2,192,768]{2,1,0:T(8,128)(2,1)S(1)}, u32[]{:S(2)}, u32[]{:S(2)}) collective-permute-start(bf16[2,192,768]{2,1,0:T(8,128)(2,1)S(1)} %maximum_add_fusion.2.tail), channel_id=1, source_target_pairs={{0,1},{1,0},{2,3},{3,2},{4,5},{5,4},{6,7},{7,6},{8,9},{9,8},{10,11... | collective-permute-start | bytes 1769480 | tf_op jit(solution)/shard_map/ppermute | solution.py:269
  (100 other events, 848.3 us)
